TPU v7x, 128 devices: a whole 4x4x4 slice. The times are simulated.
128 devices in a mesh: seq: 16 (over x, z), head: 8 (over y, core).
Axes of the slice: x: 4, y: 4, z: 4, core: 2. Of those that a mesh axis runs over, the one named last changes fastest.
Arguments:
- x_in: bfloat16 [16384, 8192], P('seq', 'head'), may hold values from -6 to 6
- z_gate: bfloat16 [16384, 8192], P('seq', 'head'), may hold values from -6 to 6
- b_proj: bfloat16 [16384, 1024], P(('seq', 'head')), may hold values from -0.015625 to 0.015625
- c_proj: bfloat16 [16384, 1024], P(('seq', 'head')), may hold values from -6 to 6
- dt_raw: float32 [128, 16384], P('head', 'seq'), may hold values from -1.25 to 5.25
- dt_bias: float32 [128], P('head'), may hold values from -1 to 1
- a_log: float32 [128], P('head'), may hold values from -10 to -3.5
- skip: float32 [128], P('head'), may hold values from 0.5 to 1.5
- norm_weight: float32 [8192], P('head'), may hold values from 0.25 to 1.75
- doc_starts: int32 [16384], P('seq'), may hold values 0 or 1
- grad_out: bfloat16 [16384, 8192], P('seq', 'head'), may hold values from -16 to 16
Outputs:
- grad_x: bfloat16 [16384, 8192], P('seq', 'head')
- grad_z: bfloat16 [16384, 8192], P('seq', 'head')
- grad_b: bfloat16 [16384, 1024], P(('seq', 'head'))
- grad_c: bfloat16 [16384, 1024], P(('seq', 'head'))
- grad_dt: float32 [128, 16384], P('head', 'seq')
- grad_alog: float32 [128], P('head')
- grad_bias: float32 [128], P('head')
- grad_skip: float32 [128], P('head')
- grad_gain: float32 [8192], P('head')
All inputs are finite; a program needn't handle non-finite values. No bound on the sum of `doc_starts` on one device may be relied on, other than what follows from the above.
Results may differ from a plain program's by a relative error of at most 0.00165.
Values may be sent and summed in bfloat16 or wider, within the bound.
No kernel may reach another device: no remote copies, remote signals or barrier semaphores. Data moves between devices by JAX's collectives and lax.ppermute only.
A program may use at most 128 MiB of HBM per device.

v0:
```python
import jax
import jax.numpy as jnp
from jax import lax
from jax.sharding import PartitionSpec as P

HEADS = 128
HEAD_DIM = 64
STATE = 128
PROJECTION_SETS = 8


EPSILON = 1e-05
PRECISE = lax.Precision.HIGHEST


def prefix_2(x, axis, combine, identity, reverse):
    length, place = (lax.axis_size(axis), lax.axis_index(axis))
    everything = jax.tree.map(lambda part: lax.all_gather(part, axis), x)
    start = jax.tree.map(
        lambda part, zero: jnp.broadcast_to(jnp.asarray(zero, part.dtype), part.shape), x, identity
    )

    def lap(k, before):
        at = length - 1 - k if reverse else k
        reached = at > place if reverse else at < place
        new = combine(before, jax.tree.map(lambda part: part[at], everything))
        return jax.tree.map(lambda a, b: jnp.where(reached, a, b), new, before)

    return lax.fori_loop(0, length, lap, start)


def compose(earlier, later):
    return (earlier[0] * later[0], later[0][..., None, None] * earlier[1] + later[1])


def carry_weights(rate_block, start_block):
    cumulative = jnp.cumsum(rate_block, axis=2)
    segment = jnp.cumsum(start_block, dtype=jnp.int32)
    weight = jnp.where(segment == 0, jnp.exp(cumulative), 0.0)
    through = jnp.where(segment[-1] == 0, jnp.exp(cumulative[..., -1]), 0.0)
    return (cumulative, segment, weight, through)


def block_geometry(rate_block, start_block):
    cumulative, segment, weight, through = carry_weights(rate_block, start_block)
    length = start_block.shape[0]
    causal = lax.broadcasted_iota(jnp.int32, (length, length), 0) >= lax.broadcasted_iota(
        jnp.int32, (length, length), 1
    )
    masked = causal & (segment[:, None] == segment[None, :])
    spread = jnp.where(masked, cumulative[..., :, None] - cumulative[..., None, :], 0.0)
    decays = jnp.where(masked, jnp.exp(spread), 0.0)
    return (decays, weight, through)


def forward_block(pieces):
    x_block, b_block, c_block, dt_block, rate_block, start_block = pieces
    x_float = x_block.astype(jnp.float32)
    b_float = b_block.astype(jnp.float32)
    decays, weight, through = block_geometry(rate_block, start_block)
    intersection = jnp.einsum("tgn,sgn->gts", c_block, b_block, preferred_element_type=jnp.float32)
    score_values = decays * intersection[:, None] * dt_block[:, :, None, :]
    within = jnp.einsum("gkts,sgkp->tgkp", score_values, x_float, precision=PRECISE)
    to_end = decays[:, :, -1, :] * dt_block
    final_states = jnp.einsum("gks,sgkp,sgn->gkpn", to_end, x_float, b_float, precision=PRECISE)
    return (within, final_states, through)


def backward_block(pieces):
    x_block, b_block, c_block, dt_block, rate_block, start_block, state_in, state_out, grad_y = (
        pieces
    )
    x_float = x_block.astype(jnp.float32)
    b_float = b_block.astype(jnp.float32)
    c_float = c_block.astype(jnp.float32)
    decays, weight, through = block_geometry(rate_block, start_block)
    intersection = jnp.einsum("tgn,sgn->gts", c_block, b_block, preferred_element_type=jnp.float32)
    score_values = decays * intersection[:, None]
    cross = jnp.einsum("tgkp,sgkp->gkts", grad_y, x_float, precision=PRECISE)
    weighted_cross = decays * cross * dt_block[:, :, None, :]
    summed = jnp.sum(weighted_cross, axis=1)
    pulled = jnp.einsum("sgn,gkpn->sgkp", b_float, state_out, precision=PRECISE)
    to_end = decays[:, :, -1, :]
    dt_tokens = dt_block.transpose(2, 0, 1)[..., None]
    grad_pre = (
        jnp.einsum("gkts,tgkp->sgkp", score_values, grad_y, precision=PRECISE)
        + to_end.transpose(2, 0, 1)[..., None] * pulled
    )
    grad_x_state = grad_pre * dt_tokens
    dt_direct = jnp.sum(grad_pre * x_float, axis=3).transpose(1, 2, 0)
    grad_b_block = jnp.einsum("gts,tgn->sgn", summed, c_float, precision=PRECISE)
    grad_b_block = grad_b_block + jnp.einsum(
        "gks,sgkp,gkpn->sgn", to_end * dt_block, x_float, state_out, precision=PRECISE
    )
    carried = jnp.einsum("tgn,gkpn->tgkp", c_float, state_in, precision=PRECISE)
    grad_c_block = jnp.einsum("gts,sgn->tgn", summed, b_float, precision=PRECISE)
    grad_c_block = grad_c_block + jnp.einsum(
        "gkt,tgkp,gkpn->tgn", weight, grad_y, state_in, precision=PRECISE
    )
    weighted = weighted_cross * intersection[:, None]
    grad_cum = jnp.sum(weighted, axis=3) - jnp.sum(weighted, axis=2)
    grad_cum = grad_cum + jnp.sum(grad_y * carried, axis=3).transpose(1, 2, 0) * weight
    end_term = to_end * dt_block * jnp.sum(x_float * pulled, axis=3).transpose(1, 2, 0)
    grad_cum = grad_cum - end_term
    at_end = jnp.sum(end_term, axis=2) + jnp.sum(state_out * state_in, axis=(2, 3)) * through
    grad_cum = grad_cum.at[..., -1].add(at_end)
    grad_rate = jnp.flip(jnp.cumsum(jnp.flip(grad_cum, 2), axis=2), 2)
    return (grad_x_state, grad_b_block, grad_c_block, dt_direct, grad_rate)


def shards(
    x_in, z_gate, b_proj, c_proj, dt_raw, dt_bias, a_log, skip, norm_weight, doc_starts, grad_out
):
    tokens = x_in.shape[0]
    heads = dt_raw.shape[0]
    per_group = HEADS // PROJECTION_SETS
    groups = heads // per_group
    length = min(256, tokens)
    blocks = tokens // length
    b_rows, c_rows = (
        lax.all_to_all(b_proj, "head", split_axis=1, concat_axis=0, tiled=True),
        lax.all_to_all(c_proj, "head", split_axis=1, concat_axis=0, tiled=True),
    )
    b_blocks = b_rows.reshape(blocks, length, groups, STATE)
    c_blocks = c_rows.reshape(blocks, length, groups, STATE)
    x_blocks = x_in.reshape(blocks, length, groups, per_group, HEAD_DIM)
    z_blocks = z_gate.reshape(blocks, length, groups, per_group, HEAD_DIM)
    out_blocks = grad_out.reshape(blocks, length, groups, per_group, HEAD_DIM)
    pre_act = dt_raw + dt_bias[:, None]
    dt_full = jax.nn.softplus(pre_act)
    decay_rate = -jnp.exp(a_log)
    rate_full = dt_full * decay_rate[:, None]
    dt_blocks = dt_full.reshape(groups, per_group, blocks, length).transpose(2, 0, 1, 3)
    rate_blocks = rate_full.reshape(groups, per_group, blocks, length).transpose(2, 0, 1, 3)
    start_blocks = doc_starts.reshape(blocks, length)
    skip_heads = skip.reshape(groups, per_group)
    gain_heads = norm_weight.reshape(groups, per_group, HEAD_DIM)
    within, final_states, throughs = lax.map(
        forward_block, (x_blocks, b_blocks, c_blocks, dt_blocks, rate_blocks, start_blocks)
    )
    zero_state = jnp.zeros((groups, per_group, HEAD_DIM, STATE), jnp.float32)
    unit = jnp.ones((groups, per_group), jnp.float32)
    resident_input = []
    before = []
    running = zero_state
    passed = unit
    for block_id in range(blocks):
        resident_input.append(running)
        before.append(passed)
        running = throughs[block_id][..., None, None] * running + final_states[block_id]
        passed = passed * throughs[block_id]
    prefix = prefix_2((passed, running), "seq", compose, (unit, zero_state), False)
    incoming = prefix[1]
    folded_in = []
    running_in = incoming
    for block_id in range(blocks):
        folded_in.append(running_in)
        running_in = throughs[block_id][..., None, None] * running_in + final_states[block_id]
    states_in = jnp.stack(folded_in)

    def norm_block(pieces):
        within_block, x_block, z_block, out_block, c_block, rate_block, start_block, state_in = (
            pieces
        )
        x_float = x_block.astype(jnp.float32)
        z_float = z_block.astype(jnp.float32)
        out_float = out_block.astype(jnp.float32)
        c_float = c_block.astype(jnp.float32)
        _, _, weight, _ = carry_weights(rate_block, start_block)
        carried = jnp.einsum("tgn,gkpn->tgkp", c_float, state_in, precision=PRECISE)
        y_full = (
            within_block
            + carried * weight.transpose(2, 0, 1)[..., None]
            + skip_heads[None, :, :, None] * x_float
        )
        logistic = jax.nn.sigmoid(z_float)
        silu_z = z_float * logistic
        gated = y_full * silu_z
        inv_rms = lax.rsqrt(jnp.mean(gated * gated, axis=(2, 3), keepdims=True) + EPSILON)
        normed = gated * inv_rms
        grad_normed = out_float * gain_heads[None]
        grad_gated = inv_rms * (
            grad_normed - normed * jnp.mean(grad_normed * normed, axis=(2, 3), keepdims=True)
        )
        grad_y = grad_gated * silu_z
        grad_z_block = grad_gated * y_full * logistic * (1.0 + z_float * (1.0 - logistic))
        gain_part = jnp.sum(out_float * normed, axis=0)
        skip_part = jnp.sum(grad_y * x_float, axis=(0, 3))
        back_local = jnp.einsum("gkt,tgkp,tgn->gkpn", weight, grad_y, c_float, precision=PRECISE)
        return (grad_y, grad_z_block.astype(jnp.bfloat16), gain_part, skip_part, back_local)

    grad_ys, grad_z_blocks, gain_parts, skip_parts, back_locals = lax.map(
        norm_block,
        (within, x_blocks, z_blocks, out_blocks, c_blocks, rate_blocks, start_blocks, states_in),
    )
    after_local = [None] * blocks
    later_factor = [None] * blocks
    flowing = zero_state
    onward = unit
    for block_id in reversed(range(blocks)):
        after_local[block_id] = flowing
        later_factor[block_id] = onward
        flowing = back_locals[block_id] + throughs[block_id][..., None, None] * flowing
        onward = onward * throughs[block_id]
    suffix = prefix_2((onward, flowing), "seq", compose, (unit, zero_state), True)
    outgoing = suffix[1]
    folded_out = [None] * blocks
    running_out = outgoing
    for block_id in reversed(range(blocks)):
        folded_out[block_id] = running_out
        running_out = back_locals[block_id] + throughs[block_id][..., None, None] * running_out
    states_out = jnp.stack(folded_out)
    grad_x_states, grad_b_blocks, grad_c_blocks, dt_directs, grad_rates = lax.map(
        backward_block,
        (
            x_blocks,
            b_blocks,
            c_blocks,
            dt_blocks,
            rate_blocks,
            start_blocks,
            states_in,
            states_out,
            grad_ys,
        ),
    )
    grad_x = (grad_x_states + skip_heads[None, None, :, :, None] * grad_ys).astype(jnp.bfloat16)
    grad_x = grad_x.reshape(tokens, heads * HEAD_DIM)
    grad_z = grad_z_blocks.reshape(tokens, heads * HEAD_DIM)
    rate_heads = decay_rate.reshape(groups, per_group)
    grad_dt_blocks = dt_directs + grad_rates * rate_heads[None, :, :, None]
    grad_dt_full = grad_dt_blocks.transpose(1, 2, 0, 3).reshape(heads, tokens)
    grad_dt = grad_dt_full * jax.nn.sigmoid(pre_act)
    alog_part = (jnp.sum(grad_rates * dt_blocks, axis=(0, 3)) * rate_heads).reshape(heads)
    bias_part = jnp.sum(grad_dt, axis=1)
    skip_part = jnp.sum(skip_parts, axis=0).reshape(heads)
    gain_part = jnp.sum(gain_parts, axis=0).reshape(heads * HEAD_DIM)
    grad_b_rows = grad_b_blocks.reshape(tokens, groups * STATE).astype(jnp.bfloat16)
    grad_c_rows = grad_c_blocks.reshape(tokens, groups * STATE).astype(jnp.bfloat16)
    grad_b, grad_c = (
        lax.all_to_all(grad_b_rows, "head", split_axis=0, concat_axis=1, tiled=True),
        lax.all_to_all(grad_c_rows, "head", split_axis=0, concat_axis=1, tiled=True),
    )
    grad_alog, grad_bias, grad_skip, grad_gain = lax.psum(
        (alog_part, bias_part, skip_part, gain_part), "seq"
    )
    return (grad_x, grad_z, grad_b, grad_c, grad_dt, grad_alog, grad_bias, grad_skip, grad_gain)


def solution(mesh):
    in_specs = (
        P("seq", "head"),
        P("seq", "head"),
        P(("seq", "head"), None),
        P(("seq", "head"), None),
        P("head", "seq"),
        P("head"),
        P("head"),
        P("head"),
        P("head"),
        P("seq"),
        P("seq", "head"),
    )
    out_specs = (
        P("seq", "head"),
        P("seq", "head"),
        P(("seq", "head"), None),
        P(("seq", "head"), None),
        P("head", "seq"),
        P("head"),
        P("head"),
        P("head"),
        P("head"),
    )
    return jax.shard_map(shards, mesh=mesh, in_specs=in_specs, out_specs=out_specs, check_vma=False)
```

profile of v0, /device:TPU:8, one launch (start us, length us, event | category | flops | bytes accessed | tf_op | source)
XLA Modules:
  0.0 594.4 jit_solution(13490303458731816262)
XLA Ops:
  8.9 4.9 all-to-all-start
  19.9 4.8 all-to-all-start.1
  25.5 6.4 %reshape.1234 = bf16[4,256,1,16,64]{4,3,1,0,2:T(8,128)(2,1)} reshape(bf16[1024,1024]{1,0:T(8,128)(2,1)} %param.23) | data formatting | bytes 4194304 | tf_op jit(solution)/shard_map/reshape | solution.py:126
  31.9 4.9 copy.249
  40.8 42.2 %while.83 = (s32[]{:T(128)}, f32[4,256,1,16,64]{1,4,3,2,0:T(8,128)}, f32[4,1,16,64,128]{4,3,2,1,0:T(8,128)}, f32[4,1,16]{2,1,0:T(1,128)S(1)}, bf16[4,256,1,16,64...) while((s32[]{:T(128)}, ...), condition=%wide.region_5.6_spmd, body=%wide.region_0.5_spmd.sunk | while | flops 1231273984 | bytes 3897519 | solution.py:138
  86.3 6.4 %reshape.1230 = bf16[4,256,1,16,64]{4,3,1,0,2:T(8,128)(2,1)} reshape(bf16[1024,1024]{1,0:T(8,128)(2,1)} %param.24) | data formatting | bytes 4194304 | tf_op jit(solution)/shard_map/reshape | solution.py:127
  92.7 5.8 copy.254
  98.5 6.4 %reshape.1231 = bf16[4,256,1,16,64]{4,3,1,0,2:T(8,128)(2,1)} reshape(bf16[1024,1024]{1,0:T(8,128)(2,1)} %param.33) | data formatting | bytes 4194304 | tf_op jit(solution)/shard_map/reshape | solution.py:128
  105.0 5.9 copy.255
  110.8 22.1 %all_gather.16 = f32[16,1,16]{2,1,0:T(1,128)S(1)} all-gather(f32[1,1,16]{2,1,0:T(1,128)S(1)} %get-tuple-element.1052), channel_id=1, replica_groups=mesh['seq'=16,'head'=8] {'seq'}, dimensions={0}, use_global_device_ids=true | all-gather | bytes 1088 | tf_op jit(solution)/shard_map/all_gather | solution.py:18
  132.9 26.5 %all-gather.3.cloned.1.call-done = f32[16,1,16,64,128]{4,3,2,1,0:T(8,128)} async-done(((f32[1,1,16,64,128]{4,3,2,1,0:T(8,128)}), f32[16,1,16,64,128]{4,3,2,1,0:T(8,128)}) %all-gather.3.cloned.1.call-update) | async-done | bytes 8388624 | tf_op jit(solution)/shard_map/all_gather | solution.py:18
  159.5 19.3 %while.86 = (s32[]{:T(128)}, f32[1,16,64,128]{3,2,1,0:T(8,128)S(1)}, s32[]{:T(128)}, f32[16,1,16]{2,1,0:T(1,128)S(1)}, f32[16,1,16,64,128]{4,3,2,1,0:T(8,128)}, /*index=5*/s32[]{:T(128)}, s32[]{:T(128)}) while((s32[]{:T(128)}, f32[1,16,64,128]{3,2,1,0:T(8,128)S(1)}, s32[]{:T(128)}, f32[16,1,16]{2,1,0:T(1,128)S(1)}, ...), condition=%wide.region_7.8_spmd.clone, body=%wide.region_6.7_spmd.clone.sunk | while | flops 524292 | bytes 1573161 | solution.py:29
  186.0 61.7 %while.84 = (s32[]{:T(128)}, f32[4,256,1,16,64]{1,4,3,2,0:T(8,128)}, bf16[4,256,1,16,64]{1,4,3,2,0:T(8,128)(2,1)}, f32[4,1,16,64]{3,2,1,0:T(8,128)}, f32[4,1,16]...) while((s32[]{:T(128)}, ...), condition=%wide.region_17.18_spmd, body=%wide.region_8.17_spmd.sunk | while | flops 819768896 | bytes 22032168 | solution.py:192
  250.4 19.9 %all_gather.18 = f32[16,1,16]{2,1,0:T(1,128)S(1)} all-gather(f32[1,1,16]{2,1,0:T(1,128)S(1)} %copy-done.27), channel_id=1, replica_groups=mesh['seq'=16,'head'=8] {'seq'}, dimensions={0}, use_global_device_ids=true | all-gather | bytes 1088 | tf_op jit(solution)/shard_map/all_gather | solution.py:18
  271.0 6.2 %copy.280 = bf16[4,256,1,16,64]{4,3,1,0,2:T(8,128)(2,1)} copy(bf16[4,256,1,16,64]{1,4,3,2,0:T(8,128)(2,1)} %get-tuple-element.585) | data formatting | bytes 4194304
  277.2 6.5 %reshape.1233 = bf16[1024,1024]{1,0:T(8,128)(2,1)} reshape(bf16[4,256,1,16,64]{4,3,1,0,2:T(8,128)(2,1)} %copy.280) | data formatting | bytes 4194304
  284.2 36.7 %all-gather.5.cloned.1.call-done = f32[16,1,16,64,128]{4,3,2,1,0:T(8,128)} async-done(((f32[1,1,16,64,128]{4,3,2,1,0:T(8,128)}), f32[16,1,16,64,128]{4,3,2,1,0:T(8,128)}) %all-gather.5.cloned.1.call-update) | async-done | bytes 8388624 | tf_op jit(solution)/shard_map/all_gather | solution.py:18
  320.9 19.6 %while.87 = (s32[]{:T(128)}, f32[1,16,64,128]{3,2,1,0:T(8,128)S(1)}, s32[]{:T(128)}, f32[16,1,16]{2,1,0:T(1,128)S(1)}, f32[16,1,16,64,128]{4,3,2,1,0:T(8,128)}, ...) while((s32[]{:T(128)}, f32[1,16,64,128]{3,2,1,0:T(8,128)S(1)}, s32[]{:T(128)}, ...), condition=%wide.region_19.20_spmd.clone, body=%wide.region_18.19_spmd.clone.sunk | while | flops 524296 | bytes 1573223 | solution.py:29
  347.1 166.3 %while.85 = (s32[]{:T(128)}, f32[4,256,1,16,64]{1,4,3,2,0:T(8,128)}, bf16[4,256,1,128]{3,1,0,2:T(8,128)(2,1)}, bf16[4,256,1,128]{3,1,0,2:T(8,128)(2,1)}, f32[4,1...) while((s32[]{:T(128)}, ...), condition=%wide.region_35.36_spmd, body=%wide.region_20.35_spmd.sunk | while | flops 3458035968 | bytes 20655576 | solution.py:213
  353.0 5.9 bitcast_dynamic-update-slice_fusion.11
  361.3 5.7 multiply_reduce_fusion.9
  394.5 5.9 bitcast_dynamic-update-slice_fusion.11
  402.9 5.7 multiply_reduce_fusion.9
  436.1 5.9 bitcast_dynamic-update-slice_fusion.11
  444.4 5.7 multiply_reduce_fusion.9
  477.7 5.9 bitcast_dynamic-update-slice_fusion.11
  486.0 5.7 multiply_reduce_fusion.9
  518.1 4.8 all-to-all-start.2
  524.0 5.0 all-to-all-done.2
  534.7 39.5 %all-reduce = (f32[16]{0:T(128)}, f32[16]{0:T(128)}, f32[16]{0:T(128)}, f32[1024]{0:T(1024)}) all-reduce(f32[16]{0:T(128)S(1)} %fusion.152, f32[16]{0:T(128)S(1)} %get-tuple-element.1028, f32[16]{0:T(128)S(1)} %copy-done.28, f32[1024]{0:T(1024)S(1)} %copy-done.21), channel_id=1, replica_groups=mesh['seq'=16,'head'=8] {'seq'}, use_global_device_ids=true, to_apply=%region_37.38 | all-reduce | flops 1072 | bytes 8576 | tf_op jit(solution)/shard_map/psum | solution.py:244
  574.2 4.8 copy.279
  579.0 6.5 %reshape.1232 = bf16[1024,1024]{1,0:T(8,128)(2,1)} reshape(bf16[4,256,1,16,64]{4,3,1,0,2:T(8,128)(2,1)} %copy.279) | data formatting | bytes 4194304
  (733 shorter events, 301.5 us)
Async XLA Ops:
  7.2 17.5 %copy-start.9 = (f32[16,1024]{1,0:T(8,128)S(1)}, f32[16,1024]{1,0:T(8,128)}, u32[]{:S(2)}) copy-start(f32[16,1024]{1,0:T(8,128)} %param.27) | copy-start | bytes 196612
  7.2 17.5 %copy-start.23 = (f32[16]{0:T(128)S(1)}, f32[16]{0:T(128)}, u32[]{:S(2)}) copy-start(f32[16]{0:T(128)} %param.28) | copy-start | bytes 196
  8.9 11.0 %all-to-all-start = ((bf16[128,8,128]{2,0,1:T(8,128)(2,1)}), bf16[128,8,128]{2,0,1:T(8,128)(2,1)S(1)}, u32[]{:S(2)}, u32[]{:S(2)}) async-start(bf16[128,8,128]{2,0,1:T(8,128)(2,1)} %copy_bitcast_fusion.5), calls=%async_computation | async-start | bytes 524288 | tf_op jit(solution)/shard_map/all_to_all | solution.py:122
  16.2 15.7 %copy-start.25 = (f32[16]{0:T(128)}, f32[16]{0:T(128)S(1)}, u32[]{:S(2)}) copy-start(f32[16]{0:T(128)S(1)} %exponential_negate_fusion) | copy-start | bytes 196
  19.9 16.9 %all-to-all-start.1 = ((bf16[128,8,128]{2,0,1:T(8,128)(2,1)}), bf16[128,8,128]{2,0,1:T(8,128)(2,1)S(1)}, u32[]{:S(2)}, u32[]{:S(2)}) async-start(bf16[128,8,128]{2,0,1:T(8,128)(2,1)} %copy_bitcast_fusion.4), calls=%async_computation.1 | async-start | bytes 524288 | tf_op jit(solution)/shard_map/all_to_all | solution.py:121
  24.7 134.8 %all-gather.3.cloned.1.call-start = ((), (), s32[]{:S(2)}) async-start(), calls=%async_computation.4 | async-start | bytes 8912896 | tf_op jit(solution)/shard_map/all_gather | solution.py:18
  86.2 234.7 %all-gather.5.cloned.1.call-start = ((), (), s32[]{:S(2)}) async-start(), calls=%async_computation.5 | async-start | bytes 8912896 | tf_op jit(solution)/shard_map/all_gather | solution.py:18
  247.7 22.6 %copy-start.20 = (f32[4,1,16,64]{3,2,1,0:T(8,128)S(1)}, f32[4,1,16,64]{3,2,1,0:T(8,128)}, u32[]{:S(2)}) copy-start(f32[4,1,16,64]{3,2,1,0:T(8,128)} %get-tuple-element.591) | copy-start | bytes 49156
  349.9 10.0 %copy-start.14 = (f32[16,1]{0,1:T(1,128)}, f32[16,1]{0,1:T(1,128)S(1)}, u32[]{:S(2)}) copy-start(f32[16,1]{0,1:T(1,128)S(1)} %slice.307) | copy-start | bytes 196 | tf_op jit(solution)/shard_map/while
  350.1 9.9 %copy-start.8 = (pred[1,256]{1,0:T(4,128)(4,1)}, pred[1,256]{1,0:T(4,128)(4,1)S(1)}, u32[]{:S(2)}) copy-start(pred[1,256]{1,0:T(4,128)(4,1)S(1)} %slice.308) | copy-start | bytes 772 | tf_op jit(solution)/shard_map/while
  374.4 11.0 %copy-start.5 = (f32[256,16]{0,1:T(8,128)S(1)}, f32[256,16]{0,1:T(8,128)}, u32[]{:S(2)}) copy-start(f32[256,16]{0,1:T(8,128)} %get-tuple-element.1399) | copy-start | bytes 49156 | tf_op jit(solution)/shard_map/while
  391.5 10.1 %copy-start.14 = (f32[16,1]{0,1:T(1,128)}, f32[16,1]{0,1:T(1,128)S(1)}, u32[]{:S(2)}) copy-start(f32[16,1]{0,1:T(1,128)S(1)} %slice.307) | copy-start | bytes 196 | tf_op jit(solution)/shard_map/while
  391.6 10.0 %copy-start.8 = (pred[1,256]{1,0:T(4,128)(4,1)}, pred[1,256]{1,0:T(4,128)(4,1)S(1)}, u32[]{:S(2)}) copy-start(pred[1,256]{1,0:T(4,128)(4,1)S(1)} %slice.308) | copy-start | bytes 772 | tf_op jit(solution)/shard_map/while
  416.0 11.0 %copy-start.5 = (f32[256,16]{0,1:T(8,128)S(1)}, f32[256,16]{0,1:T(8,128)}, u32[]{:S(2)}) copy-start(f32[256,16]{0,1:T(8,128)} %get-tuple-element.1399) | copy-start | bytes 49156 | tf_op jit(solution)/shard_map/while
  433.1 10.0 %copy-start.14 = (f32[16,1]{0,1:T(1,128)}, f32[16,1]{0,1:T(1,128)S(1)}, u32[]{:S(2)}) copy-start(f32[16,1]{0,1:T(1,128)S(1)} %slice.307) | copy-start | bytes 196 | tf_op jit(solution)/shard_map/while
  433.2 9.9 %copy-start.8 = (pred[1,256]{1,0:T(4,128)(4,1)}, pred[1,256]{1,0:T(4,128)(4,1)S(1)}, u32[]{:S(2)}) copy-start(pred[1,256]{1,0:T(4,128)(4,1)S(1)} %slice.308) | copy-start | bytes 772 | tf_op jit(solution)/shard_map/while
  457.6 11.0 %copy-start.5 = (f32[256,16]{0,1:T(8,128)S(1)}, f32[256,16]{0,1:T(8,128)}, u32[]{:S(2)}) copy-start(f32[256,16]{0,1:T(8,128)} %get-tuple-element.1399) | copy-start | bytes 49156 | tf_op jit(solution)/shard_map/while
  474.6 10.0 %copy-start.14 = (f32[16,1]{0,1:T(1,128)}, f32[16,1]{0,1:T(1,128)S(1)}, u32[]{:S(2)}) copy-start(f32[16,1]{0,1:T(1,128)S(1)} %slice.307) | copy-start | bytes 196 | tf_op jit(solution)/shard_map/while
  474.8 9.9 %copy-start.8 = (pred[1,256]{1,0:T(4,128)(4,1)}, pred[1,256]{1,0:T(4,128)(4,1)S(1)}, u32[]{:S(2)}) copy-start(pred[1,256]{1,0:T(4,128)(4,1)S(1)} %slice.308) | copy-start | bytes 772 | tf_op jit(solution)/shard_map/while
  499.1 11.0 %copy-start.5 = (f32[256,16]{0,1:T(8,128)S(1)}, f32[256,16]{0,1:T(8,128)}, u32[]{:S(2)}) copy-start(f32[256,16]{0,1:T(8,128)} %get-tuple-element.1399) | copy-start | bytes 49156 | tf_op jit(solution)/shard_map/while
  507.6 5.8 copy-start.7
  513.4 9.6 %copy-start.18 = (f32[4,1,16,256]{3,0,2,1:T(4,128)S(1)}, f32[4,1,16,256]{3,0,2,1:T(4,128)}, u32[]{:S(2)}) copy-start(f32[4,1,16,256]{3,0,2,1:T(4,128)} %get-tuple-element.588) | copy-start | bytes 196612
  513.4 9.6 %copy-start.19 = (f32[4,1,16,256]{3,0,2,1:T(4,128)S(1)}, f32[4,1,16,256]{3,0,2,1:T(4,128)}, u32[]{:S(2)}) copy-start(f32[4,1,16,256]{3,0,2,1:T(4,128)} %get-tuple-element.589) | copy-start | bytes 196612
  513.4 9.5 %copy-start.26 = (f32[16]{0:T(128)S(1)}, f32[16]{0:T(128)}, u32[]{:S(2)}) copy-start(f32[16]{0:T(128)} %copy-done.25) | copy-start | bytes 196
  513.4 10.6 %copy-start.29 = (f32[16]{0:T(128)S(1)}, f32[16]{0:T(128)}, u32[]{:S(2)}) copy-start(f32[16]{0:T(128)} %param.29) | copy-start | bytes 196
  513.4 20.4 %copy-start.10 = (f32[16,1024]{1,0:T(8,128)S(1)}, f32[16,1024]{1,0:T(8,128)}, u32[]{:S(2)}) copy-start(f32[16,1024]{1,0:T(8,128)} %param.27) | copy-start | bytes 196612
  513.4 20.4 %copy-start.24 = (f32[16]{0:T(128)S(1)}, f32[16]{0:T(128)}, u32[]{:S(2)}) copy-start(f32[16]{0:T(128)} %param.28) | copy-start | bytes 196
  513.5 21.2 %copy-start.21 = (f32[1024]{0:T(1024)S(1)}, f32[1024]{0:T(1024)}, u32[]{:S(2)}) copy-start(f32[1024]{0:T(1024)} %reshape.1219) | copy-start | bytes 12292
  513.5 21.2 %copy-start.28 = (f32[16]{0:T(128)S(1)}, f32[16]{0:T(128)}, u32[]{:S(2)}) copy-start(f32[16]{0:T(128)} %reduce_sum.156) | copy-start | bytes 196
  518.1 10.9 %all-to-all-start.2 = ((bf16[8,128,128]{2,1,0:T(8,128)(2,1)}), bf16[8,128,128]{2,1,0:T(8,128)(2,1)S(1)}, u32[]{:S(2)}, u32[]{:S(2)}) async-start(bf16[8,128,128]{2,1,0:T(8,128)(2,1)} %bitcast.131), calls=%async_computation.2 | async-start | bytes 524288 | tf_op jit(solution)/shard_map/all_to_all | solution.py:241
  529.0 57.5 %all-to-all-start.3 = ((bf16[8,128,128]{2,1,0:T(8,128)(2,1)}), bf16[8,128,128]{2,1,0:T(8,128)(2,1)S(1)}, u32[]{:S(2)}, u32[]{:S(2)}) async-start(bf16[8,128,128]{2,1,0:T(8,128)(2,1)} %bitcast.134), calls=%async_computation.3 | async-start | bytes 524288 | tf_op jit(solution)/shard_map/all_to_all | solution.py:242
  579.0 8.6 %copy-start.1 = (bf16[128,1024]{1,0:T(8,128)(2,1)S(1)}, bf16[128,1024]{1,0:T(8,128)(2,1)}, u32[]{:S(2)}) copy-start(bf16[128,1024]{1,0:T(8,128)(2,1)} %param.26) | copy-start | bytes 786436
  (37 other events, 104.0 us)
Sparse Core Ops, SparseCore 0:
  86.3 73.1 all-gather.2
  250.4 70.3 all-gather.4
where the time goes:
time: 601 us; the launch traced here: 594 us
  local copies, waits for them, and re-layouts  141 us (23%)
  matrix products  129 us (21%)
  other arithmetic  128 us (21%)
  blocking collectives  81.6 us (14%)
  waiting for transfers between devices  71.9 us (12%)
  starting transfers between devices  19.4 us (3%)
  between operations  14.4 us (2%)
  loops' own time  8.15 us (1%)
    all_gather x2, waiting for transfers between devices, prefix_2(): everything = jax.tree.map(lambda part: lax.all_gather(part, axis), x)  63.2 us
    all_gather x2, blocking collectives, prefix_2(): everything = jax.tree.map(lambda part: lax.all_gather(part, axis), x)  42 us
    psum x1, blocking collectives, shards(): lax.psum((alog_part, bias_part, skip_part, gain_part), 'seq')  39.5 us
    select_n x32, other arithmetic, lap(): return jax.tree.map(lambda a, b: jnp.where(reached, a, b), new, before)  37.6 us
    unnamed x45, local copies, waits for them, and re-layouts  26.8 us
    dot_general x4, matrix products, backward_block(): jnp.einsum('gkts,tgkp->sgkp', score_values, grad_y, precision=PRECISE)  23.6 us
    dot_general x4, matrix products, backward_block(): cross = jnp.einsum('tgkp,sgkp->gkts', grad_y, x_float, precision=PRECISE)  22.8 us
    another operation x147, local copies, waits for them, and re-layouts  21.8 us
  transfers between devices with their start and end apart: 6, of which 4 were waited for; matrix products, arithmetic and copies ran while one was open for 11% of the time, Pallas kernels for 0%

commit v1 on v0

v1 whole, which is shorter than its diff:
```python
import jax
import jax.numpy as jnp
import numpy as np
from jax import lax
from jax.experimental import pallas as pl
from jax.experimental.pallas import tpu as pltpu
from jax.sharding import PartitionSpec as P

HEADS = 128
HEAD_DIM = 64
STATE = 128
PROJECTION_SETS = 8
EPSILON = 1e-05

T = 1024
H = 16
W = H * HEAD_DIM
L = 256
C = T // L
SEQ = 16
GRP = 8
ROWS = STATE // SEQ
F32 = jnp.float32
BF16 = jnp.bfloat16
STEP = 16

THR, PRE, SUF, KAP, TABLE = 0, 4, 9, 13, 24

NN = (((1,), (0,)), ((), ()))
NT = (((1,), (1,)), ((), ()))
TN = (((0,), (0,)), ((), ()))


def dot(a, b, dims):
    return lax.dot_general(a, b, dims, preferred_element_type=F32)


def split2(a):
    hi = a.astype(BF16)
    return hi, (a - hi.astype(F32)).astype(BF16)


def split3(a):
    hi, mid = split2(a)
    lo = (a - hi.astype(F32) - mid.astype(F32)).astype(BF16)
    return hi, mid, lo


def dot2(a, b, dims):
    return dot(a, b[0], dims) + dot(a, b[1], dims)


def dot3(a, b, dims):
    return dot(a[0], b[0], dims) + dot(a[0], b[1], dims) + dot(a[1], b[0], dims)


def rows_loop(body):
    def step(i, carry):
        body(pl.ds(pl.multiple_of(i * STEP, STEP), STEP))
        return carry

    lax.fori_loop(0, L // STEP, step, 0)


def prep_kernel(dt_ref, par_ref, st_ref, e3_ref, pk_ref, rf_ref, mask_ref, me_ref, mw_ref, thx_ref):
    bias = par_ref[:, 0:1]
    nega = -jnp.exp(par_ref[:, 1:2])
    row = lax.broadcasted_iota(jnp.int32, (L, L), 0)
    col = lax.broadcasted_iota(jnp.int32, (L, L), 1)
    tri = (row <= col).astype(F32).astype(BF16)
    causal = row >= col
    first = lax.broadcasted_iota(jnp.int32, (H, L), 0) == 0
    lane = lax.broadcasted_iota(jnp.int32, (H, 128), 1)
    ones = jnp.ones((H, L), BF16)
    thr, kap = [], []
    for c in range(C):
        at = slice(c * L, (c + 1) * L)
        pre = dt_ref[:, at] + bias
        dt = jax.nn.softplus(pre)
        rf_ref[0:H, at] = dt
        rf_ref[H : 2 * H, at] = jax.nn.sigmoid(pre)
        rate = dt * nega
        parts = dot(jnp.concatenate(split3(rate), 0), tri, NN)
        cum = parts[0:H] + parts[H : 2 * H] + parts[2 * H : 3 * H]
        starts = jnp.broadcast_to(st_ref[:, at].astype(F32), (H, L))
        seg = dot(starts.astype(BF16), tri, NN)
        cum_end = cum[:, L - 1 : L]
        seg_end = seg[:, L - 1 : L]
        half = 0.5 * cum_end
        alpha = jnp.exp(cum - half)
        beta = jnp.exp(half - cum)
        pk_ref[0:H, at], pk_ref[H : 2 * H, at] = split2(alpha)
        pk_ref[2 * H : 3 * H, at], pk_ref[3 * H : 4 * H, at] = split2(dt * beta)
        seg_first = jnp.where(first, seg, 0.0).astype(BF16)
        seg_col = dot(seg_first, ones, TN)
        mask = causal & (seg_col == seg[0:1, :])
        mask_ref[at, :] = mask.astype(F32).astype(BF16)
        to_end = jnp.where(first & (seg == seg_end), 1.0, 0.0).astype(BF16)
        from_start = jnp.where(first & (seg == 0.0), 1.0, 0.0).astype(BF16)
        me_ref[at, :] = dot(to_end, ones[:, :128], TN).astype(BF16)
        mw_ref[at, :] = dot(from_start, ones[:, :128], TN).astype(BF16)
        thr.append(jnp.where(seg_end == 0.0, jnp.exp(cum_end), 0.0))
        kap.append(jnp.exp(half))
    columns = list(thr)
    passed = jnp.ones((H, 1), F32)
    for c in range(C):
        columns.append(passed)
        passed = passed * thr[c]
    columns.append(passed)
    after = [None] * C
    passed = jnp.ones((H, 1), F32)
    for c in reversed(range(C)):
        after[c] = passed
        passed = passed * thr[c]
    columns += after + kap
    table = jnp.zeros((H, 128), F32)
    for k, v in enumerate(columns):
        table = jnp.where(lane == k, v, table)
    wide = dot(jnp.concatenate(split3(table), 0), e3_ref[...], TN)
    thx_ref[...] = wide[0:TABLE]


def table_row(thx_ref, base):
    return thx_ref[pl.ds(base, 1), :]


def expand_alpha(pk_ref, e3_ref):
    return dot(pk_ref[0 : 2 * H, :], e3_ref[0 : 2 * H, :], TN)


def expand_dtbeta(pk_ref, e3_ref):
    return dot(pk_ref[2 * H : 4 * H, :], e3_ref[0 : 2 * H, :], TN)


def states_kernel(x_ref, bc_ref, me_ref, pk_ref, e3_ref, thx_ref, sloc_ref, pay_ref, acc, ex, hi, lo):
    c = pl.program_id(0)

    @pl.when(c == 0)
    def _():
        acc[...] = jnp.zeros_like(acc)

    ex[...] = expand_dtbeta(pk_ref, e3_ref)

    def scale(at):
        hi[at, :], lo[at, :] = split2(x_ref[at, :].astype(F32) * ex[at, :])

    rows_loop(scale)
    b = bc_ref[:, :STATE] * me_ref[...]
    new = dot2(b, (hi[...], lo[...]), TN)
    acc[...] = table_row(thx_ref, THR + c) * acc[...] + table_row(thx_ref, KAP + c) * new
    sloc_ref[0] = acc[...]

    @pl.when(c == C - 1)
    def _():
        pay_ref[:, :W] = acc[...]
        total = thx_ref[PRE + C : PRE + C + 1, :]
        block = jnp.concatenate([total[:, 128 * r : 128 * (r + 1)] for r in range(ROWS)], 0)
        for d in range(SEQ):
            pay_ref[ROWS * d : ROWS * (d + 1), W:] = block


def through_row(got_ref, j):
    block = got_ref[ROWS * j : ROWS * (j + 1), W:]
    return jnp.concatenate([block[r : r + 1, :] for r in range(ROWS)], 1)


def scan_forward_kernel(got_ref, out_ref):
    acc = jnp.zeros((ROWS, W), F32)
    for j in range(SEQ):
        at = slice(ROWS * j, ROWS * (j + 1))
        out_ref[at, :] = acc
        acc = through_row(got_ref, j) * acc + got_ref[at, :W]


def scan_backward_kernel(got_ref, forward_ref, out_ref):
    acc = jnp.zeros((ROWS, W), F32)
    for j in reversed(range(SEQ)):
        at = slice(ROWS * j, ROWS * (j + 1))
        out_ref[at, :] = acc
        acc = through_row(forward_ref, j) * acc + got_ref[at, :]


def within_kernel(
    x_ref, bc_ref, mask_ref, mw_ref, pk_ref, e3_ref, thx_ref, sloc_ref, ys_ref, al, ex, hi, lo, res
):
    c = pl.program_id(0)
    ex[...] = expand_dtbeta(pk_ref, e3_ref)
    al[...] = expand_alpha(pk_ref, e3_ref)

    def scale(at):
        hi[at, :], lo[at, :] = split2(x_ref[at, :].astype(F32) * ex[at, :])

    rows_loop(scale)
    cc = bc_ref[:, STATE:]
    g = split2(dot(cc, bc_ref[:, :STATE], NT) * mask_ref[...].astype(F32))
    seen = jnp.where(c > 0, 1.0, 0.0) * table_row(thx_ref, KAP + c)
    state = split2(seen * sloc_ref[0])
    res[...] = dot3(g, (hi[...], lo[...]), NN) + dot2(cc * mw_ref[...], state, NN)

    def finish(at):
        ys_ref[at, :] = al[at, :] * res[at, :]

    rows_loop(finish)


def norm_kernel(
    ys_ref, x_ref, z_ref, go_ref, bc_ref, mw_ref, pk_ref, e3_ref, thx_ref, vec_ref, sin_ref,
    gy_ref, gz_ref, dloc_ref, r_ref, pay_ref, sums_ref, acc, gain_acc, skip_acc, al, res, hi, lo, rhi, rlo,
):
    step = pl.program_id(0)
    c = C - 1 - step

    @pl.when(step == 0)
    def _():
        acc[...] = jnp.zeros_like(acc)
        gain_acc[...] = jnp.zeros_like(gain_acc)
        skip_acc[...] = jnp.zeros_like(skip_acc)

    al[...] = expand_alpha(pk_ref, e3_ref)
    cm = bc_ref[:, STATE:] * mw_ref[...]
    kappa = table_row(thx_ref, KAP + c)
    state = split2((kappa * table_row(thx_ref, PRE + c)) * sin_ref[...])
    res[...] = dot2(cm, state, NN)
    gain = vec_ref[0:1, :]
    skip = vec_ref[1:2, :]

    def body(at):
        alpha = al[at, :]
        x = x_ref[at, :].astype(F32)
        z = z_ref[at, :].astype(F32)
        out = go_ref[at, :].astype(F32)
        ys = ys_ref[at, :] + alpha * res[at, :]
        y = ys + skip * x
        logistic = jax.nn.sigmoid(z)
        silu = z * logistic
        gated = y * silu
        inv = lax.rsqrt(jnp.sum(gated * gated, axis=1, keepdims=True) * (1.0 / W) + EPSILON)
        normed = gated * inv
        grad_normed = out * gain
        k = jnp.sum(grad_normed * normed, axis=1, keepdims=True) * (1.0 / W)
        grad_gated = inv * (grad_normed - normed * k)
        gy = grad_gated * silu
        gz = grad_gated * y * (logistic + silu * (1.0 - logistic))
        gz_ref[at, :] = gz.astype(BF16)
        gy_ref[at, :] = gy
        gpart = out * normed
        spart = gy * x
        gain_acc[...] += gpart[0:8] + gpart[8:16]
        skip_acc[...] += spart[0:8] + spart[8:16]
        hi[at, :], lo[at, :] = split2(gy * alpha)
        rhi[at, :], rlo[at, :] = split2(gy * ys)

    rows_loop(body)
    r_ref[...] = dot2(e3_ref[0:H, :], (rhi[...], rlo[...]), NT)
    back = kappa * dot2(cm, (hi[...], lo[...]), TN)
    dloc_ref[0] = acc[...]
    acc[...] = back + table_row(thx_ref, THR + c) * acc[...]

    @pl.when(step == C - 1)
    def _():
        pay_ref[...] = acc[...]
        sums_ref[0:1, :] = jnp.sum(gain_acc[...], axis=0, keepdims=True)
        sums_ref[1:2, :] = jnp.sum(skip_acc[...], axis=0, keepdims=True)
        sums_ref[2:8, :] = jnp.zeros((6, W), F32)


def local_kernel(
    gy_ref, x_ref, bc_ref, mask_ref, me_ref, mw_ref, pk_ref, e3_ref, thx_ref, vec_ref, sloc_ref, sin_ref, dloc_ref,
    gx_ref, u_ref, gbc_ref, al, ex, ghi, glo, xhi, xlo, res, rhi, rlo,
):
    c = pl.program_id(0)
    ex[...] = expand_dtbeta(pk_ref, e3_ref)
    al[...] = expand_alpha(pk_ref, e3_ref)

    def scale(at):
        xhi[at, :], xlo[at, :] = split2(x_ref[at, :].astype(F32) * ex[at, :])
        ghi[at, :], glo[at, :] = split2(gy_ref[at, :] * al[at, :])

    rows_loop(scale)
    b = bc_ref[:, :STATE]
    cc = bc_ref[:, STATE:]
    me = me_ref[...]
    mw = mw_ref[...]
    mask = mask_ref[...].astype(F32)
    gys = (ghi[...], glo[...])
    xs = (xhi[...], xlo[...])
    g = split2(dot(cc, b, NT) * mask)
    q = split2(dot3(gys, xs, NT) * mask)
    kappa = table_row(thx_ref, KAP + c)
    seen = jnp.where(c > 0, 1.0, 0.0) * kappa
    state = split2(seen * sloc_ref[0] + (kappa * table_row(thx_ref, PRE + c)) * sin_ref[...])
    dstate = split2(kappa * dloc_ref[0])
    res[...] = dot3(g, gys, TN) + dot2(b * me, dstate, NN)
    gb = dot(q[0], cc, TN) + dot(q[1], cc, TN) + me.astype(F32) * dot3(xs, dstate, NT)
    gc = dot(q[0], b, NN) + dot(q[1], b, NN) + mw.astype(F32) * dot3(gys, state, NT)
    gbc_ref[:, :STATE] = gb
    gbc_ref[:, STATE:] = gc
    skip = vec_ref[1:2, :]

    def finish(at):
        v = res[at, :]
        scaled = ex[at, :] * v
        gx_ref[at, :] = scaled + skip * gy_ref[at, :]
        rhi[at, :], rlo[at, :] = split2(scaled * x_ref[at, :].astype(F32))

    rows_loop(finish)
    u_ref[...] = dot2(e3_ref[0:H, :], (rhi[...], rlo[...]), NT)


def final_kernel(
    gx_ref, x_ref, bc_ref, me_ref, pk_ref, rf_ref, e3_ref, thx_ref, par_ref, sloc_ref, sin_ref, dloc_ref, din_ref,
    u_ref, r_ref, gbc_ref, sums_ref, gxo_ref, gdt_ref, gbco_ref, par_out_ref, ex, xhi, xlo, res, rhi, rlo, cols,
):
    c = pl.program_id(0)

    @pl.when(c == 0)
    def _():
        cols[...] = jnp.zeros_like(cols)

    ex[...] = expand_dtbeta(pk_ref, e3_ref)
    kappa = table_row(thx_ref, KAP + c)
    suffix = table_row(thx_ref, SUF + c)
    dstate = split2((kappa * suffix) * din_ref[...])
    me = me_ref[...]
    res[...] = dot2(bc_ref[:, :STATE] * me, dstate, NN)

    def body(at):
        xs = x_ref[at, :].astype(F32) * ex[at, :]
        xhi[at, :], xlo[at, :] = split2(xs)
        v = res[at, :]
        gxo_ref[at, :] = (gx_ref[at, :] + ex[at, :] * v).astype(BF16)
        rhi[at, :], rlo[at, :] = split2(xs * v)

    rows_loop(body)
    heads = e3_ref[0:H, :]
    gb = gbc_ref[:, :STATE] + me.astype(F32) * dot3((xhi[...], xlo[...]), dstate, NT)
    gbco_ref[:, :STATE] = gb.astype(BF16)
    gbco_ref[:, STATE:] = gbc_ref[:, STATE:].astype(BF16)
    u = u_ref[...] + dot2(heads, (rhi[...], rlo[...]), NT)
    state = sloc_ref[0] + table_row(thx_ref, PRE + 1 + c) * sin_ref[...]
    grad = dloc_ref[0] + suffix * din_ref[...]
    ends = jnp.broadcast_to(jnp.sum(state * grad, axis=0, keepdims=True), (H, W))
    end = sum(dot(heads, part, NT) for part in split3(ends))[:, 0:1]
    dt = rf_ref[0:H, :]
    grad_cum = r_ref[...] - u
    row = lax.broadcasted_iota(jnp.int32, (L, L), 0)
    col = lax.broadcasted_iota(jnp.int32, (L, L), 1)
    tri = (row >= col).astype(F32).astype(BF16)
    parts = dot(jnp.concatenate(split3(grad_cum), 0), tri, NN)
    grad_rate = parts[0:H] + parts[H : 2 * H] + parts[2 * H : 3 * H] + end
    nega = -jnp.exp(par_ref[:, 1:2])
    grad_dt = (u / dt + grad_rate * nega) * rf_ref[H : 2 * H, :]
    gdt_ref[...] = grad_dt
    alog_part = jnp.sum(grad_rate * dt, axis=1, keepdims=True) * nega
    bias_part = jnp.sum(grad_dt, axis=1, keepdims=True)
    lane = lax.broadcasted_iota(jnp.int32, (H, 128), 1)
    cols[...] += jnp.where(lane == 1, alog_part, 0.0) + jnp.where(lane == 2, bias_part, 0.0)

    @pl.when(c == C - 1)
    def _():
        skips = jnp.broadcast_to(sums_ref[1:2, :], (H, W))
        skip_part = sum(dot(heads, part, NT) for part in split3(skips))[:, 0:1]
        right = cols[...] + jnp.where(lane == 0, skip_part, 0.0)
        gains = sums_ref[0:1, :]
        left = jnp.concatenate([gains[:, 128 * r : 128 * (r + 1)] for r in range(8)], 0)
        left = jnp.concatenate([left, jnp.zeros((8, 128), F32)], 0)
        for d in range(SEQ):
            par_out_ref[H * d : H * (d + 1), :128] = left
            par_out_ref[H * d : H * (d + 1), 128:] = right


def head_matrix():
    one = np.arange(W)[None, :] // HEAD_DIM == np.arange(H)[:, None]
    return jnp.asarray(np.concatenate([one, one, one], 0), BF16)


def whole(shape):
    return pl.BlockSpec(shape, lambda i: (0,) * len(shape))


def shard_body(
    x_in, z_gate, b_proj, c_proj, dt_raw, dt_bias, a_log, skip, norm_weight, doc_starts, grad_out
):
    e3 = head_matrix()
    par = jnp.pad(jnp.stack([dt_bias, a_log], 1), ((0, 0), (0, 126)))
    vec = jnp.pad(
        jnp.stack([norm_weight, jnp.repeat(skip, HEAD_DIM)], 0), ((0, 6), (0, 0))
    )
    starts = doc_starts.reshape(1, T)
    mine = jnp.concatenate(
        [b_proj.reshape(128, GRP, STATE), c_proj.reshape(128, GRP, STATE)], 2
    ).transpose(1, 0, 2)
    bc = lax.all_to_all(mine, "head", split_axis=0, concat_axis=0, tiled=True).reshape(T, 2 * STATE)

    def call(kernel, outs, out_specs, in_specs, scratch, flops, name):
        return pl.pallas_call(
            kernel,
            grid=(C,),
            out_shape=outs,
            in_specs=in_specs,
            out_specs=out_specs,
            scratch_shapes=scratch,
            compiler_params=pltpu.CompilerParams(
                dimension_semantics=("arbitrary",), vmem_limit_bytes=40 * 2**20
            ),
            cost_estimate=pl.CostEstimate(flops=flops, bytes_accessed=8 * 2**20, transcendentals=0),
            name=name,
        )

    sds = jax.ShapeDtypeStruct
    pk, rf, mask, me, mw, thx = pl.pallas_call(
        prep_kernel,
        out_shape=(
            sds((4 * H, T), BF16),
            sds((2 * H, T), F32),
            sds((T, L), BF16),
            sds((T, 128), BF16),
            sds((T, 128), BF16),
            sds((TABLE, W), F32),
        ),
        compiler_params=pltpu.CompilerParams(vmem_limit_bytes=40 * 2**20),
        name="prep",
    )(dt_raw, par, starts, e3)

    def tok(width, flip=False):
        return pl.BlockSpec((L, width), (lambda i: (C - 1 - i, 0)) if flip else (lambda i: (i, 0)))

    def rowf(rows, flip=False):
        return pl.BlockSpec((rows, L), (lambda i: (0, C - 1 - i)) if flip else (lambda i: (0, i)))

    state_at = pl.BlockSpec((1, STATE, W), lambda i: (i, 0, 0))
    state_before = pl.BlockSpec((1, STATE, W), lambda i: (jnp.maximum(i - 1, 0), 0, 0))
    state_flip = pl.BlockSpec((1, STATE, W), lambda i: (C - 1 - i, 0, 0))
    e3_spec = whole((3 * H, W))
    thx_spec = whole((TABLE, W))
    vec_spec = whole((8, W))
    sin_spec = whole((STATE, W))
    big = pltpu.VMEM((L, W), F32)
    half = pltpu.VMEM((L, W), BF16)
    unit = 2 * T * L * W

    sloc, pay = call(
        states_kernel,
        (sds((C, STATE, W), F32), sds((STATE, W + 128), F32)),
        (state_at, whole((STATE, W + 128))),
        [tok(W), tok(2 * STATE), tok(128), rowf(4 * H), e3_spec, thx_spec],
        [pltpu.VMEM((STATE, W), F32), big, half, half],
        2 * unit,
        "states",
    )(x_in, bc, me, pk, e3, thx)

    def exchange(v):
        return lax.all_to_all(v, "seq", split_axis=0, concat_axis=0, tiled=True)

    got = exchange(pay)
    before = pl.pallas_call(
        scan_forward_kernel, out_shape=sds((STATE, W), F32), name="scan_forward"
    )(got)
    sin = exchange(before)

    ys = call(
        within_kernel,
        sds((T, W), F32),
        tok(W),
        [tok(W), tok(2 * STATE), tok(L), tok(128), rowf(4 * H), e3_spec, thx_spec, state_before],
        [big, big, half, half, big],
        6 * unit,
        "within",
    )(x_in, bc, mask, mw, pk, e3, thx, sloc)

    gy, gz, dloc, r, back, sums = call(
        norm_kernel,
        (
            sds((T, W), F32),
            sds((T, W), BF16),
            sds((C, STATE, W), F32),
            sds((H, T), F32),
            sds((STATE, W), F32),
            sds((8, W), F32),
        ),
        (tok(W, True), tok(W, True), state_flip, rowf(H, True), sin_spec, vec_spec),
        [
            tok(W, True), tok(W, True), tok(W, True), tok(W, True), tok(2 * STATE, True), tok(128, True),
            rowf(4 * H, True), e3_spec, thx_spec, vec_spec, sin_spec,
        ],
        [
            pltpu.VMEM((STATE, W), F32), pltpu.VMEM((8, W), F32), pltpu.VMEM((8, W), F32),
            big, big, half, half, half, half,
        ],
        6 * unit,
        "norm",
    )(ys, x_in, z_gate, grad_out, bc, mw, pk, e3, thx, vec, sin)

    got_back = exchange(back)
    behind = pl.pallas_call(
        scan_backward_kernel, out_shape=sds((STATE, W), F32), name="scan_backward"
    )(got_back, got)
    din = exchange(behind)

    gx_local, u, gbc_local = call(
        local_kernel,
        (sds((T, W), F32), sds((H, T), F32), sds((T, 2 * STATE), F32)),
        (tok(W), rowf(H), tok(2 * STATE)),
        [
            tok(W), tok(W), tok(2 * STATE), tok(L), tok(128), tok(128), rowf(4 * H), e3_spec, thx_spec, vec_spec,
            state_before, sin_spec, state_at,
        ],
        [big, big, half, half, half, half, big, half, half],
        12 * unit,
        "local",
    )(gy, x_in, bc, mask, me, mw, pk, e3, thx, vec, sloc, sin, dloc)

    grad_x, grad_dt, gbc, params = call(
        final_kernel,
        (sds((T, W), BF16), sds((H, T), F32), sds((T, 2 * STATE), BF16), sds((SEQ * H, 256), F32)),
        (tok(W), rowf(H), tok(2 * STATE), whole((SEQ * H, 256))),
        [
            tok(W), tok(W), tok(2 * STATE), tok(128), rowf(4 * H), rowf(2 * H), e3_spec, thx_spec, whole((H, 128)),
            state_at, sin_spec, state_at, sin_spec, rowf(H), rowf(H), tok(2 * STATE), vec_spec,
        ],
        [big, half, half, big, half, half, pltpu.VMEM((H, 128), F32)],
        5 * unit,
        "final",
    )(gx_local, x_in, bc, me, pk, rf, e3, thx, par, sloc, sin, dloc, din, u, r, gbc_local, sums)

    back_bc = lax.all_to_all(
        gbc.reshape(GRP, 128, 2 * STATE), "head", split_axis=0, concat_axis=0, tiled=True
    )
    grad_b = back_bc[:, :, :STATE].transpose(1, 0, 2).reshape(128, GRP * STATE)
    grad_c = back_bc[:, :, STATE:].transpose(1, 0, 2).reshape(128, GRP * STATE)
    summed = jnp.sum(exchange(params).reshape(SEQ, H, 256), axis=0)
    grad_gain = summed[:8, :128].reshape(W)
    grad_skip, grad_alog, grad_bias = summed[:, 128], summed[:, 129], summed[:, 130]
    return (grad_x, gz, grad_b, grad_c, grad_dt, grad_alog, grad_bias, grad_skip, grad_gain)


def solution(mesh):
    in_specs = (
        P("seq", "head"),
        P("seq", "head"),
        P(("seq", "head"), None),
        P(("seq", "head"), None),
        P("head", "seq"),
        P("head"),
        P("head"),
        P("head"),
        P("head"),
        P("seq"),
        P("seq", "head"),
    )
    out_specs = (
        P("seq", "head"),
        P("seq", "head"),
        P(("seq", "head"), None),
        P(("seq", "head"), None),
        P("head", "seq"),
        P("head"),
        P("head"),
        P("head"),
        P("head"),
    )
    return jax.shard_map(shard_body, mesh=mesh, in_specs=in_specs, out_specs=out_specs, check_vma=False)
```

time: 601 us -> 206 us (0.34)
  matrix products: 129 us -> 0 us
  other arithmetic: 128 us -> 0.9 us
  local copies, waits for them, and re-layouts: 141 us -> 46 us
  Pallas kernels: 0 us -> 72.4 us
  waiting for transfers between devices: 71.9 us -> 12.7 us
  blocking collectives: 81.6 us -> 52.4 us
  between operations: 14.4 us -> 0.88 us
  loops' own time: 8.15 us -> 0 us
    dot_general x56 -> x0, matrix products: 129 us -> none  [the longest x4 23.6 us: backward_block(): jnp.einsum('gkts,tgkp->sgkp', score_values, grad_y, precision=PRECISE)]
    pallas_call x0 -> x8, Pallas kernels: none -> 72.4 us  [the longest x1 22.8 us: shard_body(): call(norm_kernel, (sds((T, W), F32), sds((T, W), BF16), sds((C, STATE, W)...]
    all_gather x2 -> x0, waiting for transfers between devices: 63.2 us -> none  [prefix_2(): everything = jax.tree.map(lambda part: lax.all_gather(part, axis), x)]
    all_to_all x0 -> x3, blocking collectives: none -> 52.4 us  [exchange(): return lax.all_to_all(v, 'seq', split_axis=0, concat_axis=0, tiled=True)]
    all_gather x2 -> x0, blocking collectives: 42 us -> none  [prefix_2(): everything = jax.tree.map(lambda part: lax.all_gather(part, axis), x)]
    select_n x44 -> x0, other arithmetic: 41.3 us -> none  [the longest x32 37.6 us: lap(): return jax.tree.map(lambda a, b: jnp.where(reached, a, b), new, before)]
    psum x1 -> x0, blocking collectives: 39.5 us -> none  [shards(): lax.psum((alog_part, bias_part, skip_part, gain_part), 'seq')]
    reduce_sum x24 -> x1, other arithmetic: 30.9 us -> 0.02 us  [shard_body(): summed = jnp.sum(exchange(params).reshape(SEQ, H, 256), axis=0)]
  transfers between devices with their start and end apart: 6 -> 4, of which waited for: 4 -> 2; matrix products, arithmetic and copies ran while one was open for 11% -> 1% of each run, Pallas kernels for 0% -> 15%
where the time goes in v1:
time: 206 us; the launch traced here: 203 us
  Pallas kernels  72.4 us (35%)
  blocking collectives  52.4 us (25%)
  local copies, waits for them, and re-layouts  46 us (22%)
  starting transfers between devices  17.6 us (9%)
  waiting for transfers between devices  12.7 us (6%)
    all_to_all x3, blocking collectives, exchange(): return lax.all_to_all(v, 'seq', split_axis=0, concat_axis=0, tiled=True)  52.4 us
    unnamed x101, local copies, waits for them, and re-layouts  41.2 us
    pallas_call x1, Pallas kernels, shard_body(): call(norm_kernel, (sds((T, W), F32), sds((T, W), BF16), sds((C, STATE, W)...  22.8 us
    pallas_call x1, Pallas kernels, shard_body(): call(local_kernel, (sds((T, W), F32), sds((H, T), F32), sds((T, 2 * STATE...  20.3 us
    pallas_call x1, Pallas kernels, shard_body(): call(final_kernel, (sds((T, W), BF16), sds((H, T), F32), sds((T, 2 * STAT...  12.2 us
    all_to_all x2, starting transfers between devices, exchange(): return lax.all_to_all(v, 'seq', split_axis=0, concat_axis=0, tiled=True)  7.83 us
    pallas_call x1, Pallas kernels, shard_body(): call(within_kernel, sds((T, W), F32), tok(W), [tok(W), tok(2 * STATE), to...  7.77 us
    all_to_all x1, waiting for transfers between devices, shard_body(): lax.all_to_all(gbc.reshape(GRP, 128, 2 * STATE), 'head', split_axis=0, co...  7.6 us
  transfers between devices with their start and end apart: 4, of which 2 were waited for; matrix products, arithmetic and copies ran while one was open for 1% of the time, Pallas kernels for 15%

profile of v1, /device:TPU:8, one launch (start us, length us, event | category | flops | bytes accessed | tf_op | source)
XLA Modules:
  0.0 202.9 jit_solution(1934256828143852052)
XLA Ops:
  1.6 1.1 copy_bitcast_fusion.2
  3.6 4.9 %all-to-all-start = ((bf16[8,128,256]{2,1,0:T(8,128)(2,1)}), bf16[8,128,256]{2,1,0:T(8,128)(2,1)S(1)}, u32[]{:S(2)}, u32[]{:S(2)}) async-start(bf16[8,128,256]{2,1,0:T(8,128)(2,1)} %maximum_bitcast_fusion), calls=%async_computation | async-start | bytes 1048576 | tf_op jit(solution)/shard_map/all_to_all | solution.py:393
  8.6 1.5 prep.1
  12.3 5.1 %all-to-all-done = bf16[8,128,256]{2,1,0:T(8,128)(2,1)S(1)} async-done(((bf16[8,128,256]{2,1,0:T(8,128)(2,1)}), bf16[8,128,256]{2,1,0:T(8,128)(2,1)S(1)}, u32[]{:S(2)}, u32[]{:S(2)}) %all-to-all-start) | async-done | bytes 524320 | tf_op jit(solution)/shard_map/all_to_all | solution.py:393
  17.4 3.8 %states.1 = (f32[4,128,1024]{2,1,0:T(8,128)S(1)}, f32[128,1152]{1,0:T(8,128)S(1)}) custom-call(bf16[1024,1024]{1,0:T(8,128)(2,1)S(1)} %copy-done.1, bf16[1024,256]{1,0:T(8,128)(2,1)S(1)} %bitcast.41, bf16[1024,128]{1,0:T(8,128)(2,1)S(1)} %get-tuple-element.34.me_ref, bf16[64,1024]{1,0:T(8,128)(2,1)S(1)} %get-tuple-element.32.pk_ref, ...), custom_call_target="tpu_custom_call" | custom-call | flops 1073741824 | bytes 8388608 | tf_op jit(solution)/shard_map/states/pallas_call | solution.py:442
  21.2 1.3 copy-done.6
  22.5 19.9 %all_to_all.63 = f32[16,8,1152]{2,1,0:T(8,128)} all-to-all(f32[16,8,1152]{2,1,0:T(8,128)S(1)} %bitcast.49), channel_id=1, replica_groups=mesh['seq'=16,'head'=8] {'seq'}, dimensions={0} | all-to-all | bytes 1179648 | tf_op jit(solution)/shard_map/all_to_all | solution.py:453
  42.4 1.9 scan_forward.1
  44.4 3.6 %all-to-all-start.2 = ((f32[16,8,1024]{2,1,0:T(8,128)}), f32[16,8,1024]{2,1,0:T(8,128)S(1)}, u32[]{:S(2)}, u32[]{:S(2)}) async-start(f32[16,8,1024]{2,1,0:T(8,128)} %bitcast.58), calls=%async_computation.2 | async-start | bytes 1048576 | tf_op jit(solution)/shard_map/all_to_all | solution.py:453
  48.8 1.6 copy-done.7
  53.1 1.0 copy-done.45
  54.2 7.8 %within.1.ys_ref = f32[1024,1024]{1,0:T(8,128)S(1)} custom-call(bf16[1024,1024]{1,0:T(8,128)(2,1)S(1)} %copy-done.1, bf16[1024,256]{1,0:T(8,128)(2,1)S(1)} %bitcast.42, bf16[1024,256]{1,0:T(8,128)(2,1)S(1)} %copy-done.45, bf16[1024,128]{1,0:T(8,128)(2,1)S(1)} %copy-done.31, bf16[64,1024]{1,0:T(8,128)(2,1)S(1)} %copy-done.17, ...), custom_call_target="tpu_custom_call" | custom-call | flops 3221225472 | bytes 8388608 | tf_op jit(solution)/shard_map/within/pallas_call | solution.py:461
  61.9 2.0 copy-done.3
  64.0 1.6 copy-done.4
  65.5 1.6 copy-done.5
  69.9 22.8 %norm.1 = (f32[1024,1024]{1,0:T(8,128)}, bf16[1024,1024]{1,0:T(8,128)(2,1)}, f32[4,128,1024]{2,1,0:T(8,128)S(1)}, f32[16,1024]{1,0:T(8,128)S(1)}, f32[128,1024]{1,0:T(8,128)S(1)}, /*index=5*/f32[8,1024]{1,0:T(8,128)S(1)}) custom-call(f32[1024,1024]{1,0:T(8,128)} %copy-done.3, bf16[1024,1024]{1,0:T(8,128)(2,1)S(1)} %copy-done.1, ...), custom_call_target="tpu_custom_call" | custom-call | flops 3221225472 | bytes 8388608 | tf_op jit(solution)/shard_map/norm/pallas_call | solution.py:471
  92.7 1.4 copy-done.10
  94.0 17.1 %all_to_all.64 = f32[16,8,1024]{2,1,0:T(8,128)} all-to-all(f32[16,8,1024]{2,1,0:T(8,128)S(1)} %bitcast.51), channel_id=1, replica_groups=mesh['seq'=16,'head'=8] {'seq'}, dimensions={0} | all-to-all | bytes 1048576 | tf_op jit(solution)/shard_map/all_to_all | solution.py:453
  111.2 2.1 %scan_backward.1 = f32[128,1024]{1,0:T(8,128)} custom-call(f32[128,1024]{1,0:T(8,128)} %bitcast.57, f32[128,1152]{1,0:T(8,128)} %bitcast.55), custom_call_target="tpu_custom_call" | custom-call | tf_op jit(solution)/shard_map/scan_backward/pallas_call | solution.py:495
  113.3 4.3 %all-to-all-start.4 = ((f32[16,8,1024]{2,1,0:T(8,128)}), f32[16,8,1024]{2,1,0:T(8,128)}, u32[]{:S(2)}, u32[]{:S(2)}) async-start(f32[16,8,1024]{2,1,0:T(8,128)} %bitcast.56), calls=%async_computation.4 | async-start | bytes 1048576 | tf_op jit(solution)/shard_map/all_to_all | solution.py:453
  117.6 1.6 copy-done.8
  119.2 1.6 copy-done.11
  124.5 1.0 copy-done.46
  125.5 20.3 %local.1 = (f32[1024,1024]{1,0:T(8,128)S(1)}, f32[16,1024]{1,0:T(8,128)S(1)}, f32[1024,256]{1,0:T(8,128)S(1)}) custom-call(f32[1024,1024]{1,0:T(8,128)} %get-tuple-element.37.gy_ref, bf16[1024,1024]{1,0:T(8,128)(2,1)S(1)} %copy-done.1, bf16[1024,256]{1,0:T(8,128)(2,1)S(1)} %bitcast.44, bf16[1024,256]{1,0:T(8,128)(2,1)S(1)} %copy-done.46, ...), custom_call_target="tpu_custom_call" | custom-call | flops 6442450944 | bytes 8388608 | tf_op jit(solution)/shard_map/local/pallas_call | solution.py:500
  145.8 2.0 copy-done.2
  149.4 1.6 copy-done.9
  151.0 1.6 copy-done.12
  152.6 1.2 copy-done.14
  159.9 12.2 %final.1 = (bf16[1024,1024]{1,0:T(8,128)(2,1)}, f32[16,1024]{1,0:T(8,128)}, bf16[1024,256]{1,0:T(8,128)(2,1)S(1)}, f32[256,256]{1,0:T(8,128)S(1)}) custom-call(f32[1024,1024]{1,0:T(8,128)} %copy-done.2, bf16[1024,1024]{1,0:T(8,128)(2,1)S(1)} %copy-done.1, bf16[1024,256]{1,0:T(8,128)(2,1)S(1)} %bitcast.45, bf16[1024,128]{1,0:T(8,128)(2,1)S(1)} %copy-done.29, ...), custom_call_target="tpu_custom_call" | custom-call | flops 2684354560 | bytes 8388608 | tf_op jit(solution)/shard_map/final/pallas_call | solution.py:513
  172.1 15.3 %all_to_all.65 = f32[16,16,256]{2,1,0:T(8,128)S(1)} all-to-all(f32[16,16,256]{2,1,0:T(8,128)S(1)} %bitcast.52), channel_id=1, replica_groups=mesh['seq'=16,'head'=8] {'seq'}, dimensions={0} | all-to-all | bytes 524288 | tf_op jit(solution)/shard_map/all_to_all | solution.py:453
  187.4 4.9 %all-to-all-start.5 = ((bf16[8,128,256]{2,1,0:T(8,128)(2,1)}), bf16[8,128,256]{2,1,0:T(8,128)(2,1)S(1)}, u32[]{:S(2)}, u32[]{:S(2)}) async-start(bf16[8,128,256]{2,1,0:T(8,128)(2,1)} %bitcast.50), calls=%async_computation.5 | async-start | bytes 1048576 | tf_op jit(solution)/shard_map/all_to_all | solution.py:526
  193.6 7.6 %all-to-all-done.5 = bf16[8,128,256]{2,1,0:T(8,128)(2,1)S(1)} async-done(((bf16[8,128,256]{2,1,0:T(8,128)(2,1)}), bf16[8,128,256]{2,1,0:T(8,128)(2,1)S(1)}, u32[]{:S(2)}, u32[]{:S(2)}) %all-to-all-start.5) | async-done | bytes 524320 | tf_op jit(solution)/shard_map/all_to_all | solution.py:526
  (101 shorter events, 24.8 us)
Async XLA Ops:
  0.6 1.0 copy-start
  0.7 7.9 %copy-start.15 = (bf16[48,1024]{1,0:T(8,128)(2,1)S(1)}, bf16[48,1024]{1,0:T(8,128)(2,1)}, u32[]{:S(2)}) copy-start(bf16[48,1024]{1,0:T(8,128)(2,1)} %constant.6.clone.e3_ref) | copy-start | bytes 294916
  0.7 7.8 %copy-start.48 = (f32[16]{0:T(128)S(1)}, f32[16]{0:T(128)}, u32[]{:S(2)}) copy-start(f32[16]{0:T(128)} %param.18) | copy-start | bytes 196
  0.7 7.8 %copy-start.49 = (f32[16]{0:T(128)S(1)}, f32[16]{0:T(128)}, u32[]{:S(2)}) copy-start(f32[16]{0:T(128)} %param.17) | copy-start | bytes 196
  0.7 7.9 %copy-start.43 = (s32[1024]{0:T(1024)S(1)}, s32[1024]{0:T(1024)}, u32[]{:S(2)}) copy-start(s32[1024]{0:T(1024)} %param.21) | copy-start | bytes 12292
  0.7 7.9 %copy-start.40 = (f32[16,1024]{1,0:T(8,128)S(1)}, f32[16,1024]{1,0:T(8,128)}, u32[]{:S(2)}) copy-start(f32[16,1024]{1,0:T(8,128)} %dt_ref.1) | copy-start | bytes 196612
  0.7 16.7 %copy-start.1 = (bf16[1024,1024]{1,0:T(8,128)(2,1)S(1)}, bf16[1024,1024]{1,0:T(8,128)(2,1)}, u32[]{:S(2)}) copy-start(bf16[1024,1024]{1,0:T(8,128)(2,1)} %x_ref.9) | copy-start | bytes 6291460
  3.6 13.8 %all-to-all-start = ((bf16[8,128,256]{2,1,0:T(8,128)(2,1)}), bf16[8,128,256]{2,1,0:T(8,128)(2,1)S(1)}, u32[]{:S(2)}, u32[]{:S(2)}) async-start(bf16[8,128,256]{2,1,0:T(8,128)(2,1)} %maximum_bitcast_fusion), calls=%async_computation | async-start | bytes 1048576 | tf_op jit(solution)/shard_map/all_to_all | solution.py:393
  12.3 30.1 %copy-start.16 = (bf16[64,1024]{1,0:T(8,128)(2,1)}, bf16[64,1024]{1,0:T(8,128)(2,1)S(1)}, u32[]{:S(2)}) copy-start(bf16[64,1024]{1,0:T(8,128)(2,1)S(1)} %get-tuple-element.32.pk_ref) | copy-start | bytes 393220
  12.3 30.1 %copy-start.22 = (f32[24,1024]{1,0:T(8,128)}, f32[24,1024]{1,0:T(8,128)S(1)}, u32[]{:S(2)}) copy-start(f32[24,1024]{1,0:T(8,128)S(1)} %get-tuple-element.33.thx_ref) | copy-start | bytes 294916
  12.3 30.1 %copy-start.27 = (bf16[1024,128]{1,0:T(8,128)(2,1)}, bf16[1024,128]{1,0:T(8,128)(2,1)S(1)}, u32[]{:S(2)}) copy-start(bf16[1024,128]{1,0:T(8,128)(2,1)S(1)} %get-tuple-element.34.me_ref) | copy-start | bytes 786436
  21.2 1.3 copy-start.6
  22.5 26.3 %copy-start.47 = (f32[1024]{0:T(1024)S(1)}, f32[1024]{0:T(1024)}, u32[]{:S(2)}) copy-start(f32[1024]{0:T(1024)} %param.20) | copy-start | bytes 12292
  44.4 19.6 %all-to-all-start.2 = ((f32[16,8,1024]{2,1,0:T(8,128)}), f32[16,8,1024]{2,1,0:T(8,128)S(1)}, u32[]{:S(2)}, u32[]{:S(2)}) async-start(f32[16,8,1024]{2,1,0:T(8,128)} %bitcast.58), calls=%async_computation.2 | async-start | bytes 1048576 | tf_op jit(solution)/shard_map/all_to_all | solution.py:453
  48.8 1.6 copy-start.7
  53.1 1.0 copy-start.45
  61.9 2.0 copy-start.3
  64.0 1.6 copy-start.4
  65.5 1.6 copy-start.5
  92.7 1.4 copy-start.10
  94.0 17.1 %copy-start.36 = (f32[16,1024]{1,0:T(8,128)}, f32[16,1024]{1,0:T(8,128)S(1)}, u32[]{:S(2)}) copy-start(f32[16,1024]{1,0:T(8,128)S(1)} %get-tuple-element.43.r_ref) | copy-start | bytes 196612
  94.0 17.1 %copy-start.41 = (f32[8,1024]{1,0:T(8,128)}, f32[8,1024]{1,0:T(8,128)S(1)}, u32[]{:S(2)}) copy-start(f32[8,1024]{1,0:T(8,128)S(1)} %get-tuple-element.45.sums_ref) | copy-start | bytes 98308
  113.3 36.1 %all-to-all-start.4 = ((f32[16,8,1024]{2,1,0:T(8,128)}), f32[16,8,1024]{2,1,0:T(8,128)}, u32[]{:S(2)}, u32[]{:S(2)}) async-start(f32[16,8,1024]{2,1,0:T(8,128)} %bitcast.56), calls=%async_computation.4 | async-start | bytes 1048576 | tf_op jit(solution)/shard_map/all_to_all | solution.py:453
  117.6 1.6 copy-start.8
  119.2 1.6 copy-start.11
  124.5 1.0 copy-start.46
  145.8 2.0 copy-start.2
  149.4 1.6 copy-start.9
  151.0 1.6 copy-start.12
  152.6 1.2 copy-start.14
  172.1 15.3 %copy-start.21 = (bf16[1024,256]{1,0:T(8,128)(2,1)}, bf16[1024,256]{1,0:T(8,128)(2,1)S(1)}, u32[]{:S(2)}) copy-start(bf16[1024,256]{1,0:T(8,128)(2,1)S(1)} %get-tuple-element.48) | copy-start | bytes 1572868
  187.4 13.8 %all-to-all-start.5 = ((bf16[8,128,256]{2,1,0:T(8,128)(2,1)}), bf16[8,128,256]{2,1,0:T(8,128)(2,1)S(1)}, u32[]{:S(2)}, u32[]{:S(2)}) async-start(bf16[8,128,256]{2,1,0:T(8,128)(2,1)} %bitcast.50), calls=%async_computation.5 | async-start | bytes 1048576 | tf_op jit(solution)/shard_map/all_to_all | solution.py:526
  (22 other events, 19.0 us)

commit v2 on v1

--- a/solution.py
+++ b/solution.py
@@ -1,3 +1,5 @@
+import functools
+
 import jax
 import jax.numpy as jnp
 import numpy as np
@@ -54,12 +56,12 @@
     return dot(a[0], b[0], dims) + dot(a[0], b[1], dims) + dot(a[1], b[0], dims)
 
 
-def rows_loop(body):
+def rows_loop(body, unroll=16):
     def step(i, carry):
         body(pl.ds(pl.multiple_of(i * STEP, STEP), STEP))
         return carry
 
-    lax.fori_loop(0, L // STEP, step, 0)
+    lax.fori_loop(0, L // STEP, step, 0, unroll=unroll)
 
 
 def prep_kernel(dt_ref, par_ref, st_ref, e3_ref, pk_ref, rf_ref, mask_ref, me_ref, mw_ref, thx_ref):
@@ -181,9 +183,10 @@
 
 
 def within_kernel(
-    x_ref, bc_ref, mask_ref, mw_ref, pk_ref, e3_ref, thx_ref, sloc_ref, ys_ref, al, ex, hi, lo, res
+    first, x_ref, bc_ref, mask_ref, mw_ref, pk_ref, e3_ref, thx_ref, sloc_ref, *refs
 ):
-    c = pl.program_id(0)
+    ys_ref, al, ex, hi, lo, res = refs[-6:]
+    c = pl.program_id(0) + first
     ex[...] = expand_dtbeta(pk_ref, e3_ref)
     al[...] = expand_alpha(pk_ref, e3_ref)
 
@@ -234,11 +237,12 @@
         logistic = jax.nn.sigmoid(z)
         silu = z * logistic
         gated = y * silu
-        inv = lax.rsqrt(jnp.sum(gated * gated, axis=1, keepdims=True) * (1.0 / W) + EPSILON)
+        grad_normed = out * gain
+        square = jnp.sum(gated * gated, axis=1, keepdims=True) * (1.0 / W)
+        cross = jnp.sum(grad_normed * gated, axis=1, keepdims=True) * (1.0 / W)
+        inv = lax.rsqrt(square + EPSILON)
         normed = gated * inv
-        grad_normed = out * gain
-        k = jnp.sum(grad_normed * normed, axis=1, keepdims=True) * (1.0 / W)
-        grad_gated = inv * (grad_normed - normed * k)
+        grad_gated = inv * (grad_normed - normed * (inv * cross))
         gy = grad_gated * silu
         gz = grad_gated * y * (logistic + silu * (1.0 - logistic))
         gz_ref[at, :] = gz.astype(BF16)
@@ -265,10 +269,11 @@
 
 
 def local_kernel(
-    gy_ref, x_ref, bc_ref, mask_ref, me_ref, mw_ref, pk_ref, e3_ref, thx_ref, vec_ref, sloc_ref, sin_ref, dloc_ref,
-    gx_ref, u_ref, gbc_ref, al, ex, ghi, glo, xhi, xlo, res, rhi, rlo,
+    first, gy_ref, x_ref, bc_ref, mask_ref, me_ref, mw_ref, pk_ref, e3_ref, thx_ref, vec_ref, sloc_ref, sin_ref,
+    dloc_ref, *refs,
 ):
-    c = pl.program_id(0)
+    gx_ref, u_ref, gbc_ref, al, ex, ghi, glo, xhi, xlo, res, rhi, rlo = refs[-12:]
+    c = pl.program_id(0) + first
     ex[...] = expand_dtbeta(pk_ref, e3_ref)
     al[...] = expand_alpha(pk_ref, e3_ref)
 
@@ -307,9 +312,9 @@
     u_ref[...] = dot2(e3_ref[0:H, :], (rhi[...], rlo[...]), NT)
 
 
-def final_kernel(
-    gx_ref, x_ref, bc_ref, me_ref, pk_ref, rf_ref, e3_ref, thx_ref, par_ref, sloc_ref, sin_ref, dloc_ref, din_ref,
-    u_ref, r_ref, gbc_ref, sums_ref, gxo_ref, gdt_ref, gbco_ref, par_out_ref, ex, xhi, xlo, res, rhi, rlo, cols,
+def steps_kernel(
+    x_ref, bc_ref, me_ref, pk_ref, rf_ref, e3_ref, thx_ref, par_ref, sloc_ref, sin_ref, dloc_ref, din_ref,
+    u_ref, r_ref, sums_ref, gdt_ref, par_out_ref, ex, res, rhi, rlo, cols,
 ):
     c = pl.program_id(0)
 
@@ -321,21 +326,14 @@
     kappa = table_row(thx_ref, KAP + c)
     suffix = table_row(thx_ref, SUF + c)
     dstate = split2((kappa * suffix) * din_ref[...])
-    me = me_ref[...]
-    res[...] = dot2(bc_ref[:, :STATE] * me, dstate, NN)
+    res[...] = dot2(bc_ref[:, :STATE] * me_ref[...], dstate, NN)
 
     def body(at):
         xs = x_ref[at, :].astype(F32) * ex[at, :]
-        xhi[at, :], xlo[at, :] = split2(xs)
-        v = res[at, :]
-        gxo_ref[at, :] = (gx_ref[at, :] + ex[at, :] * v).astype(BF16)
-        rhi[at, :], rlo[at, :] = split2(xs * v)
+        rhi[at, :], rlo[at, :] = split2(xs * res[at, :])
 
     rows_loop(body)
     heads = e3_ref[0:H, :]
-    gb = gbc_ref[:, :STATE] + me.astype(F32) * dot3((xhi[...], xlo[...]), dstate, NT)
-    gbco_ref[:, :STATE] = gb.astype(BF16)
-    gbco_ref[:, STATE:] = gbc_ref[:, STATE:].astype(BF16)
     u = u_ref[...] + dot2(heads, (rhi[...], rlo[...]), NT)
     state = sloc_ref[0] + table_row(thx_ref, PRE + 1 + c) * sin_ref[...]
     grad = dloc_ref[0] + suffix * din_ref[...]
@@ -369,6 +367,28 @@
             par_out_ref[H * d : H * (d + 1), 128:] = right
 
 
+def final_kernel(
+    gx_ref, x_ref, bc_ref, me_ref, pk_ref, e3_ref, thx_ref, din_ref, gbc_ref,
+    gxo_ref, gbco_ref, ex, xhi, xlo, res,
+):
+    c = pl.program_id(0)
+    ex[...] = expand_dtbeta(pk_ref, e3_ref)
+    factor = table_row(thx_ref, KAP + c) * table_row(thx_ref, SUF + c)
+    dstate = split2(factor * din_ref[...])
+    me = me_ref[...]
+    res[...] = dot2(bc_ref[:, :STATE] * me, dstate, NN)
+
+    def body(at):
+        scale = ex[at, :]
+        xhi[at, :], xlo[at, :] = split2(x_ref[at, :].astype(F32) * scale)
+        gxo_ref[at, :] = (gx_ref[at, :] + scale * res[at, :]).astype(BF16)
+
+    rows_loop(body)
+    gb = gbc_ref[:, :STATE] + me.astype(F32) * dot3((xhi[...], xlo[...]), dstate, NT)
+    gbco_ref[:, :STATE] = gb.astype(BF16)
+    gbco_ref[:, STATE:] = gbc_ref[:, STATE:].astype(BF16)
+
+
 def head_matrix():
     one = np.arange(W)[None, :] // HEAD_DIM == np.arange(H)[:, None]
     return jnp.asarray(np.concatenate([one, one, one], 0), BF16)
@@ -392,16 +412,17 @@
     ).transpose(1, 0, 2)
     bc = lax.all_to_all(mine, "head", split_axis=0, concat_axis=0, tiled=True).reshape(T, 2 * STATE)
 
-    def call(kernel, outs, out_specs, in_specs, scratch, flops, name):
+    def call(kernel, outs, out_specs, in_specs, scratch, flops, name, steps=C, aliases={}):
         return pl.pallas_call(
             kernel,
-            grid=(C,),
+            grid=(steps,),
+            input_output_aliases=aliases,
             out_shape=outs,
             in_specs=in_specs,
             out_specs=out_specs,
             scratch_shapes=scratch,
             compiler_params=pltpu.CompilerParams(
-                dimension_semantics=("arbitrary",), vmem_limit_bytes=40 * 2**20
+                dimension_semantics=("arbitrary",), vmem_limit_bytes=60 * 2**20
             ),
             cost_estimate=pl.CostEstimate(flops=flops, bytes_accessed=8 * 2**20, transcendentals=0),
             name=name,
@@ -418,19 +439,28 @@
             sds((T, 128), BF16),
             sds((TABLE, W), F32),
         ),
-        compiler_params=pltpu.CompilerParams(vmem_limit_bytes=40 * 2**20),
+        compiler_params=pltpu.CompilerParams(vmem_limit_bytes=60 * 2**20),
         name="prep",
     )(dt_raw, par, starts, e3)
 
-    def tok(width, flip=False):
-        return pl.BlockSpec((L, width), (lambda i: (C - 1 - i, 0)) if flip else (lambda i: (i, 0)))
-
-    def rowf(rows, flip=False):
-        return pl.BlockSpec((rows, L), (lambda i: (0, C - 1 - i)) if flip else (lambda i: (0, i)))
-
-    state_at = pl.BlockSpec((1, STATE, W), lambda i: (i, 0, 0))
-    state_before = pl.BlockSpec((1, STATE, W), lambda i: (jnp.maximum(i - 1, 0), 0, 0))
-    state_flip = pl.BlockSpec((1, STATE, W), lambda i: (C - 1 - i, 0, 0))
+    def at_chunk(shape, axis, order=lambda i: i):
+        def index(i):
+            return tuple(order(i) if a == axis else 0 for a in range(len(shape)))
+
+        return pl.BlockSpec(shape, index)
+
+    def reverse(i):
+        return C - 1 - i
+
+    def tok(width, order=lambda i: i):
+        return at_chunk((L, width), 0, order)
+
+    def rowf(rows, order=lambda i: i):
+        return at_chunk((rows, L), 1, order)
+
+    def stat(order=lambda i: i):
+        return at_chunk((1, STATE, W), 0, order)
+
     e3_spec = whole((3 * H, W))
     thx_spec = whole((TABLE, W))
     vec_spec = whole((8, W))
@@ -442,7 +472,7 @@
     sloc, pay = call(
         states_kernel,
         (sds((C, STATE, W), F32), sds((STATE, W + 128), F32)),
-        (state_at, whole((STATE, W + 128))),
+        (stat(), whole((STATE, W + 128))),
         [tok(W), tok(2 * STATE), tok(128), rowf(4 * H), e3_spec, thx_spec],
         [pltpu.VMEM((STATE, W), F32), big, half, half],
         2 * unit,
@@ -452,21 +482,35 @@
     def exchange(v):
         return lax.all_to_all(v, "seq", split_axis=0, concat_axis=0, tiled=True)
 
+    any_spec = pl.BlockSpec(memory_space=pl.ANY)
+
+    def within(first, *earlier):
+        def order(i):
+            return i + first
+
+        return call(
+            functools.partial(within_kernel, first),
+            sds((T, W), F32),
+            tok(W, order),
+            [
+                tok(W, order), tok(2 * STATE, order), tok(L, order), tok(128, order), rowf(4 * H, order),
+                e3_spec, thx_spec, stat(lambda i: jnp.maximum(i + first - 1, 0)),
+            ]
+            + [any_spec] * len(earlier),
+            [big, big, half, half, big],
+            3 * unit,
+            "within",
+            C // 2,
+            {8: 0} if earlier else {},
+        )(x_in, bc, mask, mw, pk, e3, thx, sloc, *earlier)
+
     got = exchange(pay)
+    ys, got = lax.optimization_barrier((within(0), got))
     before = pl.pallas_call(
         scan_forward_kernel, out_shape=sds((STATE, W), F32), name="scan_forward"
     )(got)
     sin = exchange(before)
-
-    ys = call(
-        within_kernel,
-        sds((T, W), F32),
-        tok(W),
-        [tok(W), tok(2 * STATE), tok(L), tok(128), rowf(4 * H), e3_spec, thx_spec, state_before],
-        [big, big, half, half, big],
-        6 * unit,
-        "within",
-    )(x_in, bc, mask, mw, pk, e3, thx, sloc)
+    ys = within(C // 2, ys)
 
     gy, gz, dloc, r, back, sums = call(
         norm_kernel,
@@ -478,10 +522,10 @@
             sds((STATE, W), F32),
             sds((8, W), F32),
         ),
-        (tok(W, True), tok(W, True), state_flip, rowf(H, True), sin_spec, vec_spec),
-        [
-            tok(W, True), tok(W, True), tok(W, True), tok(W, True), tok(2 * STATE, True), tok(128, True),
-            rowf(4 * H, True), e3_spec, thx_spec, vec_spec, sin_spec,
+        (tok(W, reverse), tok(W, reverse), stat(reverse), rowf(H, reverse), sin_spec, vec_spec),
+        [tok(W, reverse)] * 4
+        + [
+            tok(2 * STATE, reverse), tok(128, reverse), rowf(4 * H, reverse), e3_spec, thx_spec, vec_spec, sin_spec,
         ],
         [
             pltpu.VMEM((STATE, W), F32), pltpu.VMEM((8, W), F32), pltpu.VMEM((8, W), F32),
@@ -491,44 +535,65 @@
         "norm",
     )(ys, x_in, z_gate, grad_out, bc, mw, pk, e3, thx, vec, sin)
 
+    def local(first, *earlier):
+        def order(i):
+            return i + first
+
+        return call(
+            functools.partial(local_kernel, first),
+            (sds((T, W), F32), sds((H, T), F32), sds((T, 2 * STATE), F32)),
+            (tok(W, order), rowf(H, order), tok(2 * STATE, order)),
+            [
+                tok(W, order), tok(W, order), tok(2 * STATE, order), tok(L, order), tok(128, order), tok(128, order),
+                rowf(4 * H, order), e3_spec, thx_spec, vec_spec,
+                stat(lambda i: jnp.maximum(i + first - 1, 0)), sin_spec, stat(order),
+            ]
+            + [any_spec] * len(earlier),
+            [big, big, half, half, half, half, big, half, half],
+            6 * unit,
+            "local",
+            C // 2,
+            {13 + k: k for k in range(len(earlier))},
+        )(gy, x_in, bc, mask, me, mw, pk, e3, thx, vec, sloc, sin, dloc, *earlier)
+
     got_back = exchange(back)
+    partly, got_back = lax.optimization_barrier((local(0), got_back))
     behind = pl.pallas_call(
         scan_backward_kernel, out_shape=sds((STATE, W), F32), name="scan_backward"
     )(got_back, got)
     din = exchange(behind)
-
-    gx_local, u, gbc_local = call(
-        local_kernel,
-        (sds((T, W), F32), sds((H, T), F32), sds((T, 2 * STATE), F32)),
-        (tok(W), rowf(H), tok(2 * STATE)),
+    gx_local, u, gbc_local = local(C // 2, *partly)
+
+    grad_dt, params = call(
+        steps_kernel,
+        (sds((H, T), F32), sds((SEQ * H, 256), F32)),
+        (rowf(H), whole((SEQ * H, 256))),
         [
-            tok(W), tok(W), tok(2 * STATE), tok(L), tok(128), tok(128), rowf(4 * H), e3_spec, thx_spec, vec_spec,
-            state_before, sin_spec, state_at,
+            tok(W), tok(2 * STATE), tok(128), rowf(4 * H), rowf(2 * H), e3_spec, thx_spec, whole((H, 128)),
+            stat(), sin_spec, stat(), sin_spec, rowf(H), rowf(H), vec_spec,
         ],
-        [big, big, half, half, half, half, big, half, half],
-        12 * unit,
-        "local",
-    )(gy, x_in, bc, mask, me, mw, pk, e3, thx, vec, sloc, sin, dloc)
-
-    grad_x, grad_dt, gbc, params = call(
+        [big, big, half, half, pltpu.VMEM((H, 128), F32)],
+        3 * unit,
+        "steps",
+    )(x_in, bc, me, pk, rf, e3, thx, par, sloc, sin, dloc, din, u, r, sums)
+    params = exchange(params)
+
+    grad_x, gbc = call(
         final_kernel,
-        (sds((T, W), BF16), sds((H, T), F32), sds((T, 2 * STATE), BF16), sds((SEQ * H, 256), F32)),
-        (tok(W), rowf(H), tok(2 * STATE), whole((SEQ * H, 256))),
-        [
-            tok(W), tok(W), tok(2 * STATE), tok(128), rowf(4 * H), rowf(2 * H), e3_spec, thx_spec, whole((H, 128)),
-            state_at, sin_spec, state_at, sin_spec, rowf(H), rowf(H), tok(2 * STATE), vec_spec,
-        ],
-        [big, half, half, big, half, half, pltpu.VMEM((H, 128), F32)],
-        5 * unit,
+        (sds((T, W), BF16), sds((T, 2 * STATE), BF16)),
+        (tok(W), tok(2 * STATE)),
+        [tok(W), tok(W), tok(2 * STATE), tok(128), rowf(4 * H), e3_spec, thx_spec, sin_spec, tok(2 * STATE)],
+        [big, half, half, big],
+        4 * unit,
         "final",
-    )(gx_local, x_in, bc, me, pk, rf, e3, thx, par, sloc, sin, dloc, din, u, r, gbc_local, sums)
+    )(gx_local, x_in, bc, me, pk, e3, thx, din, gbc_local)
 
     back_bc = lax.all_to_all(
         gbc.reshape(GRP, 128, 2 * STATE), "head", split_axis=0, concat_axis=0, tiled=True
     )
     grad_b = back_bc[:, :, :STATE].transpose(1, 0, 2).reshape(128, GRP * STATE)
     grad_c = back_bc[:, :, STATE:].transpose(1, 0, 2).reshape(128, GRP * STATE)
-    summed = jnp.sum(exchange(params).reshape(SEQ, H, 256), axis=0)
+    summed = jnp.sum(params.reshape(SEQ, H, 256), axis=0)
     grad_gain = summed[:8, :128].reshape(W)
     grad_skip, grad_alog, grad_bias = summed[:, 128], summed[:, 129], summed[:, 130]
     return (grad_x, gz, grad_b, grad_c, grad_dt, grad_alog, grad_bias, grad_skip, grad_gain)

time: 206 us -> 150 us (0.73)
  blocking collectives: 52.4 us -> 0 us
  local copies, waits for them, and re-layouts: 46 us -> 9.88 us
  starting transfers between devices: 17.6 us -> 37.6 us
  waiting for transfers between devices: 12.7 us -> 26 us
    all_to_all x3 -> x0, blocking collectives: 52.4 us -> none  [exchange(): return lax.all_to_all(v, 'seq', split_axis=0, concat_axis=0, tiled=True)]
    unnamed x101 -> x21, local copies, waits for them, and re-layouts: 41.2 us -> 5.14 us
    all_to_all x2 -> x5, starting transfers between devices: 7.83 us -> 27.8 us  [exchange(): return lax.all_to_all(v, 'seq', split_axis=0, concat_axis=0, tiled=True)]
    all_to_all x2 -> x5, waiting for transfers between devices: 0.01 us -> 13.6 us  [exchange(): return lax.all_to_all(v, 'seq', split_axis=0, concat_axis=0, tiled=True)]
    pallas_call x1, Pallas kernels: 22.8 us -> 13.2 us  [shard_body(): call(norm_kernel, (sds((T, W), F32), sds((T, W), BF16), sds((C, STATE, W)...]
    pallas_call x3 -> x6, Pallas kernels: 40.2 us -> 45.6 us  [the longest x2 18.4 us: local(): call(functools.partial(local_kernel, first), (sds((T, W), F32), sds((H, T...]
  transfers between devices with their start and end apart: 4 -> 7, of which waited for: 2 -> 7; matrix products, arithmetic and copies ran while one was open for 1% -> 2% of each run, Pallas kernels for 15% -> 27%
where the time goes in v2:
time: 150 us; the launch traced here: 148 us
  Pallas kernels  71.8 us (48%)
  starting transfers between devices  37.6 us (25%)
  waiting for transfers between devices  26 us (17%)
  local copies, waits for them, and re-layouts  9.88 us (7%)
  other arithmetic  1.52 us (1%)
    all_to_all x5, starting transfers between devices, exchange(): return lax.all_to_all(v, 'seq', split_axis=0, concat_axis=0, tiled=True)  27.8 us
    pallas_call x2, Pallas kernels, local(): call(functools.partial(local_kernel, first), (sds((T, W), F32), sds((H, T...  18.4 us
    all_to_all x5, waiting for transfers between devices, exchange(): return lax.all_to_all(v, 'seq', split_axis=0, concat_axis=0, tiled=True)  13.6 us
    pallas_call x1, Pallas kernels, shard_body(): call(norm_kernel, (sds((T, W), F32), sds((T, W), BF16), sds((C, STATE, W)...  13.2 us
    pallas_call x2, Pallas kernels, within(): call(functools.partial(within_kernel, first), sds((T, W), F32), tok(W, or...  10.2 us
    pallas_call x1, Pallas kernels, shard_body(): call(steps_kernel, (sds((H, T), F32), sds((SEQ * H, 256), F32)), (rowf(H)...  9.37 us
    pallas_call x1, Pallas kernels, shard_body(): call(final_kernel, (sds((T, W), BF16), sds((T, 2 * STATE), BF16)), (tok(W...  7.67 us
    all_to_all x1, waiting for transfers between devices, shard_body(): lax.all_to_all(gbc.reshape(GRP, 128, 2 * STATE), 'head', split_axis=0, co...  7.6 us
  transfers between devices with their start and end apart: 7, of which 7 were waited for; matrix products, arithmetic and copies ran while one was open for 2% of the time, Pallas kernels for 27%

profile of v2, /device:TPU:8, one launch (start us, length us, event | category | flops | bytes accessed | tf_op | source)
XLA Modules:
  0.0 147.5 jit_solution(10842625989564872914)
XLA Ops:
  0.7 0.9 copy-done
  1.6 1.1 copy_bitcast_fusion.2
  2.7 0.9 maximum_bitcast_fusion
  3.5 4.9 %all-to-all-start = ((bf16[8,128,256]{2,1,0:T(8,128)(2,1)}), bf16[8,128,256]{2,1,0:T(8,128)(2,1)S(1)}, u32[]{:S(2)}, u32[]{:S(2)}) async-start(bf16[8,128,256]{2,1,0:T(8,128)(2,1)} %maximum_bitcast_fusion), calls=%async_computation | async-start | bytes 1048576 | tf_op jit(solution)/shard_map/all_to_all | solution.py:413
  9.2 3.4 %prep.1 = (bf16[64,1024]{1,0:T(8,128)(2,1)}, f32[32,1024]{1,0:T(8,128)}, bf16[1024,256]{1,0:T(8,128)(2,1)}, bf16[1024,128]{1,0:T(8,128)(2,1)}, bf16[1024,128]{1,0:T(8,128)(2,1)}, /*index=5*/f32[24,1024]{1,0:T(8,128)}) custom-call(f32[16,1024]{1,0:T(8,128)} %dt_ref.1, f32[16,128]{1,0:T(8,128)} %pad.8.par_ref, s32[1,1024]{1,0:T(1,128)} %bitcast.66, ...), custom_call_target="tpu_custom_call" | custom-call | tf_op jit(solution)/shard_map/prep/pallas_call | solution.py:432
  12.6 4.7 %all-to-all-done = bf16[8,128,256]{2,1,0:T(8,128)(2,1)S(1)} async-done(((bf16[8,128,256]{2,1,0:T(8,128)(2,1)}), bf16[8,128,256]{2,1,0:T(8,128)(2,1)S(1)}, u32[]{:S(2)}, u32[]{:S(2)}) %all-to-all-start) | async-done | bytes 524320 | tf_op jit(solution)/shard_map/all_to_all | solution.py:413
  17.3 0.8 copy-done.1
  18.2 5.6 %states.1 = (f32[4,128,1024]{2,1,0:T(8,128)}, f32[128,1152]{1,0:T(8,128)}) custom-call(bf16[1024,1024]{1,0:T(8,128)(2,1)} %x_ref.15, bf16[1024,256]{1,0:T(8,128)(2,1)} %bitcast.41, bf16[1024,128]{1,0:T(8,128)(2,1)} %get-tuple-element.43.me_ref, bf16[64,1024]{1,0:T(8,128)(2,1)} %get-tuple-element.41.pk_ref, bf16[48,1024]{1,0:T(8,128)(2,1)} %constant.6.clone.e3_ref, ...), custom_call_target="tpu_custom_call" | custom-call | flops 1073741824 | bytes 8388608 | tf_op jit(solution)/shard_map/states/pallas_call | solution.py:472
  23.7 7.9 %all-to-all-start.1 = ((f32[16,8,1152]{2,1,0:T(8,128)}), f32[16,8,1152]{2,1,0:T(8,128)S(1)}, u32[]{:S(2)}, u32[]{:S(2)}) async-start(f32[16,8,1152]{2,1,0:T(8,128)} %bitcast.60), calls=%async_computation.1 | async-start | bytes 1179648 | tf_op jit(solution)/shard_map/all_to_all | solution.py:483
  31.6 5.1 %within.2.refs_0_ = f32[1024,1024]{1,0:T(8,128)} custom-call(bf16[1024,1024]{1,0:T(8,128)(2,1)} %x_ref.15, bf16[1024,256]{1,0:T(8,128)(2,1)} %bitcast.42, bf16[1024,256]{1,0:T(8,128)(2,1)} %get-tuple-element.39.mask_ref, bf16[1024,128]{1,0:T(8,128)(2,1)} %get-tuple-element.40.mw_ref, bf16[64,1024]{1,0:T(8,128)(2,1)} %get-tuple-element.41.pk_ref, ...), custom_call_target="tpu_custom_call" | custom-call | flops 1610612736 | bytes 8388608 | tf_op jit(solution)/shard_map/within/pallas_call | solution.py:491
  36.7 6.6 %all-to-all-done.1 = f32[16,8,1152]{2,1,0:T(8,128)S(1)} async-done(((f32[16,8,1152]{2,1,0:T(8,128)}), f32[16,8,1152]{2,1,0:T(8,128)S(1)}, u32[]{:S(2)}, u32[]{:S(2)}) %all-to-all-start.1) | async-done | bytes 589856 | tf_op jit(solution)/shard_map/all_to_all | solution.py:483
  43.3 0.8 copy-done.3
  44.1 1.9 %scan_forward.1 = f32[128,1024]{1,0:T(8,128)} custom-call(f32[128,1152]{1,0:T(8,128)} %bitcast.53), custom_call_target="tpu_custom_call" | custom-call | tf_op jit(solution)/shard_map/scan_forward/pallas_call | solution.py:509
  46.0 3.8 %all-to-all-start.2 = ((f32[16,8,1024]{2,1,0:T(8,128)}), f32[16,8,1024]{2,1,0:T(8,128)S(1)}, u32[]{:S(2)}, u32[]{:S(2)}) async-start(f32[16,8,1024]{2,1,0:T(8,128)} %bitcast.59), calls=%async_computation.2 | async-start | bytes 1048576 | tf_op jit(solution)/shard_map/all_to_all | solution.py:483
  50.6 5.1 %within.3.ys_ref = f32[1024,1024]{1,0:T(8,128)} custom-call(bf16[1024,1024]{1,0:T(8,128)(2,1)} %x_ref.15, bf16[1024,256]{1,0:T(8,128)(2,1)} %bitcast.43, bf16[1024,256]{1,0:T(8,128)(2,1)} %get-tuple-element.39.mask_ref, bf16[1024,128]{1,0:T(8,128)(2,1)} %get-tuple-element.40.mw_ref, ...), custom_call_target="tpu_custom_call", output_to_operand_aliasing={{}: (8, {})} | custom-call | flops 1610612736 | bytes 8388608 | tf_op jit(solution)/shard_map/within/pallas_call | solution.py:491
  55.8 4.4 %all-to-all-done.2 = f32[16,8,1024]{2,1,0:T(8,128)S(1)} async-done(((f32[16,8,1024]{2,1,0:T(8,128)}), f32[16,8,1024]{2,1,0:T(8,128)S(1)}, u32[]{:S(2)}, u32[]{:S(2)}) %all-to-all-start.2) | async-done | bytes 524320 | tf_op jit(solution)/shard_map/all_to_all | solution.py:483
  61.0 13.2 %norm.1 = (f32[1024,1024]{1,0:T(8,128)}, bf16[1024,1024]{1,0:T(8,128)(2,1)}, f32[4,128,1024]{2,1,0:T(8,128)}, f32[16,1024]{1,0:T(8,128)}, f32[128,1024]{1,0:T(8,128)}, /*index=5*/f32[8,1024]{1,0:T(8,128)}) custom-call(f32[1024,1024]{1,0:T(8,128)} %within.3.ys_ref, bf16[1024,1024]{1,0:T(8,128)(2,1)} %x_ref.15, bf16[1024,1024]{1,0:T(8,128)(2,1)} %z_ref.1, ...), custom_call_target="tpu_custom_call" | custom-call | flops 3221225472 | bytes 8388608 | tf_op jit(solution)/shard_map/norm/pallas_call | solution.py:515
  74.1 3.6 %all-to-all-start.3 = ((f32[16,8,1024]{2,1,0:T(8,128)}), f32[16,8,1024]{2,1,0:T(8,128)S(1)}, u32[]{:S(2)}, u32[]{:S(2)}) async-start(f32[16,8,1024]{2,1,0:T(8,128)} %bitcast.62), calls=%async_computation.3 | async-start | bytes 1048576 | tf_op jit(solution)/shard_map/all_to_all | solution.py:483
  77.7 9.1 %local.2 = (f32[1024,1024]{1,0:T(8,128)}, f32[16,1024]{1,0:T(8,128)}, f32[1024,256]{1,0:T(8,128)}) custom-call(f32[1024,1024]{1,0:T(8,128)} %get-tuple-element.48.gy_ref, bf16[1024,1024]{1,0:T(8,128)(2,1)} %x_ref.15, bf16[1024,256]{1,0:T(8,128)(2,1)} %bitcast.45, bf16[1024,256]{1,0:T(8,128)(2,1)} %get-tuple-element.39.mask_ref, ...), custom_call_target="tpu_custom_call" | custom-call | flops 3221225472 | bytes 8388608 | tf_op jit(solution)/shard_map/local/pallas_call | solution.py:542
  86.8 1.0 all-to-all-done.3
  87.8 0.8 copy-done.5
  88.6 2.1 %scan_backward.1 = f32[128,1024]{1,0:T(8,128)} custom-call(f32[128,1024]{1,0:T(8,128)} %bitcast.58, f32[128,1152]{1,0:T(8,128)} %bitcast.54), custom_call_target="tpu_custom_call" | custom-call | tf_op jit(solution)/shard_map/scan_backward/pallas_call | solution.py:561
  90.7 6.2 %all-to-all-start.4 = ((f32[16,8,1024]{2,1,0:T(8,128)}), f32[16,8,1024]{2,1,0:T(8,128)S(1)}, u32[]{:S(2)}, u32[]{:S(2)}) async-start(f32[16,8,1024]{2,1,0:T(8,128)} %bitcast.57), calls=%async_computation.4 | async-start | bytes 1048576 | tf_op jit(solution)/shard_map/all_to_all | solution.py:483
  96.9 9.3 %local.3 = (f32[1024,1024]{1,0:T(8,128)}, f32[16,1024]{1,0:T(8,128)}, f32[1024,256]{1,0:T(8,128)}) custom-call(f32[1024,1024]{1,0:T(8,128)} %get-tuple-element.48.gy_ref, bf16[1024,1024]{1,0:T(8,128)(2,1)} %x_ref.15, bf16[1024,256]{1,0:T(8,128)(2,1)} %bitcast.46, ...), custom_call_target="tpu_custom_call", output_to_operand_aliasing={{0}: (13, {}), {1}: (14, {}), {2}: (15, {})} | custom-call | flops 3221225472 | bytes 8388608 | tf_op jit(solution)/shard_map/local/pallas_call | solution.py:542
  106.1 0.8 all-to-all-done.4
  107.0 0.8 copy-done.4
  107.8 9.4 %steps.1 = (f32[16,1024]{1,0:T(8,128)}, f32[256,256]{1,0:T(8,128)}) custom-call(bf16[1024,1024]{1,0:T(8,128)(2,1)} %x_ref.15, bf16[1024,256]{1,0:T(8,128)(2,1)} %bitcast.47, bf16[1024,128]{1,0:T(8,128)(2,1)} %get-tuple-element.43.me_ref, bf16[64,1024]{1,0:T(8,128)(2,1)} %get-tuple-element.41.pk_ref, f32[32,1024]{1,0:T(8,128)} %get-tuple-element.63.rf_ref, ...), custom_call_target="tpu_custom_call" | custom-call | flops 1610612736 | bytes 8388608 | tf_op jit(solution)/shard_map/steps/pallas_call | solution.py:567
  117.2 6.4 %all-to-all-start.6 = ((f32[16,16,256]{2,1,0:T(8,128)}), f32[16,16,256]{2,1,0:T(8,128)S(1)}, u32[]{:S(2)}, u32[]{:S(2)}) async-start(f32[16,16,256]{2,1,0:T(8,128)} %bitcast.63), calls=%async_computation.6 | async-start | bytes 524288 | tf_op jit(solution)/shard_map/all_to_all | solution.py:483
  123.6 7.7 %final.1 = (bf16[1024,1024]{1,0:T(8,128)(2,1)}, bf16[1024,256]{1,0:T(8,128)(2,1)}) custom-call(f32[1024,1024]{1,0:T(8,128)} %get-tuple-element.57.gx_ref, bf16[1024,1024]{1,0:T(8,128)(2,1)} %x_ref.15, bf16[1024,256]{1,0:T(8,128)(2,1)} %bitcast.48, bf16[1024,128]{1,0:T(8,128)(2,1)} %get-tuple-element.43.me_ref, bf16[64,1024]{1,0:T(8,128)(2,1)} %get-tuple-element.41.pk_ref, ...), custom_call_target="tpu_custom_call" | custom-call | flops 2147483648 | bytes 8388608 | tf_op jit(solution)/shard_map/final/pallas_call | solution.py:581
  131.3 0.8 all-to-all-done.6
  132.1 4.9 %all-to-all-start.5 = ((bf16[8,128,256]{2,1,0:T(8,128)(2,1)}), bf16[8,128,256]{2,1,0:T(8,128)(2,1)S(1)}, u32[]{:S(2)}, u32[]{:S(2)}) async-start(bf16[8,128,256]{2,1,0:T(8,128)(2,1)} %bitcast.61), calls=%async_computation.5 | async-start | bytes 1048576 | tf_op jit(solution)/shard_map/all_to_all | solution.py:591
  138.2 7.6 %all-to-all-done.5 = bf16[8,128,256]{2,1,0:T(8,128)(2,1)S(1)} async-done(((bf16[8,128,256]{2,1,0:T(8,128)(2,1)}), bf16[8,128,256]{2,1,0:T(8,128)(2,1)S(1)}, u32[]{:S(2)}, u32[]{:S(2)}) %all-to-all-start.5) | async-done | bytes 524320 | tf_op jit(solution)/shard_map/all_to_all | solution.py:591
  (27 shorter events, 5.3 us)
Async XLA Ops:
  0.6 1.0 copy-start
  0.7 7.8 %copy-start.8 = (f32[16]{0:T(128)S(1)}, f32[16]{0:T(128)}, u32[]{:S(2)}) copy-start(f32[16]{0:T(128)} %param.18) | copy-start | bytes 196
  0.7 7.8 %copy-start.9 = (f32[16]{0:T(128)S(1)}, f32[16]{0:T(128)}, u32[]{:S(2)}) copy-start(f32[16]{0:T(128)} %param.17) | copy-start | bytes 196
  3.5 13.8 %all-to-all-start = ((bf16[8,128,256]{2,1,0:T(8,128)(2,1)}), bf16[8,128,256]{2,1,0:T(8,128)(2,1)S(1)}, u32[]{:S(2)}, u32[]{:S(2)}) async-start(bf16[8,128,256]{2,1,0:T(8,128)(2,1)} %maximum_bitcast_fusion), calls=%async_computation | async-start | bytes 1048576 | tf_op jit(solution)/shard_map/all_to_all | solution.py:413
  17.3 0.8 copy-start.1
  23.7 19.6 %all-to-all-start.1 = ((f32[16,8,1152]{2,1,0:T(8,128)}), f32[16,8,1152]{2,1,0:T(8,128)S(1)}, u32[]{:S(2)}, u32[]{:S(2)}) async-start(f32[16,8,1152]{2,1,0:T(8,128)} %bitcast.60), calls=%async_computation.1 | async-start | bytes 1179648 | tf_op jit(solution)/shard_map/all_to_all | solution.py:483
  36.7 13.2 %copy-start.7 = (f32[16]{0:T(128)S(1)}, f32[16]{0:T(128)}, u32[]{:S(2)}) copy-start(f32[16]{0:T(128)} %param.19) | copy-start | bytes 196
  36.7 13.3 %copy-start.6 = (f32[1024]{0:T(1024)S(1)}, f32[1024]{0:T(1024)}, u32[]{:S(2)}) copy-start(f32[1024]{0:T(1024)} %param.20) | copy-start | bytes 12292
  43.3 0.8 copy-start.3
  46.0 14.1 %all-to-all-start.2 = ((f32[16,8,1024]{2,1,0:T(8,128)}), f32[16,8,1024]{2,1,0:T(8,128)S(1)}, u32[]{:S(2)}, u32[]{:S(2)}) async-start(f32[16,8,1024]{2,1,0:T(8,128)} %bitcast.59), calls=%async_computation.2 | async-start | bytes 1048576 | tf_op jit(solution)/shard_map/all_to_all | solution.py:483
  60.2 0.8 copy-start.2
  74.1 13.6 %all-to-all-start.3 = ((f32[16,8,1024]{2,1,0:T(8,128)}), f32[16,8,1024]{2,1,0:T(8,128)S(1)}, u32[]{:S(2)}, u32[]{:S(2)}) async-start(f32[16,8,1024]{2,1,0:T(8,128)} %bitcast.62), calls=%async_computation.3 | async-start | bytes 1048576 | tf_op jit(solution)/shard_map/all_to_all | solution.py:483
  87.8 0.8 copy-start.5
  90.7 16.3 %all-to-all-start.4 = ((f32[16,8,1024]{2,1,0:T(8,128)}), f32[16,8,1024]{2,1,0:T(8,128)S(1)}, u32[]{:S(2)}, u32[]{:S(2)}) async-start(f32[16,8,1024]{2,1,0:T(8,128)} %bitcast.57), calls=%async_computation.4 | async-start | bytes 1048576 | tf_op jit(solution)/shard_map/all_to_all | solution.py:483
  107.0 0.8 copy-start.4
  117.2 14.9 %all-to-all-start.6 = ((f32[16,16,256]{2,1,0:T(8,128)}), f32[16,16,256]{2,1,0:T(8,128)S(1)}, u32[]{:S(2)}, u32[]{:S(2)}) async-start(f32[16,16,256]{2,1,0:T(8,128)} %bitcast.63), calls=%async_computation.6 | async-start | bytes 524288 | tf_op jit(solution)/shard_map/all_to_all | solution.py:483
  132.1 13.8 %all-to-all-start.5 = ((bf16[8,128,256]{2,1,0:T(8,128)(2,1)}), bf16[8,128,256]{2,1,0:T(8,128)(2,1)S(1)}, u32[]{:S(2)}, u32[]{:S(2)}) async-start(bf16[8,128,256]{2,1,0:T(8,128)(2,1)} %bitcast.61), calls=%async_computation.5 | async-start | bytes 1048576 | tf_op jit(solution)/shard_map/all_to_all | solution.py:591

commit v3 on v1

v3 whole, which is shorter than its diff:
```python
import jax
import jax.numpy as jnp
import numpy as np
from jax import lax
from jax.experimental import pallas as pl
from jax.experimental.pallas import tpu as pltpu
from jax.sharding import PartitionSpec as P

HEADS = 128
HEAD_DIM = 64
STATE = 128
PROJECTION_SETS = 8
EPSILON = 1e-05

T = 1024
H = 16
W = H * HEAD_DIM
L = 256
C = T // L
SEQ = 16
GRP = 8
ROWS = STATE // SEQ
F32 = jnp.float32
BF16 = jnp.bfloat16
STEP = 16
VMEM_LIMIT = 60 * 2**20
VMEM_NEAR = 48 * 2**20

THR, KAP, PRE, TOTAL, TABLE = 0, 4, 8, 12, 16
ALPHA, DTBETA, TO_END, FROM_START = 0, 1, 2, 3

NN = (((1,), (0,)), ((), ()))
NT = (((1,), (1,)), ((), ()))
TN = (((0,), (0,)), ((), ()))


def dot(a, b, dims):
    return lax.dot_general(a, b, dims, preferred_element_type=F32)


def split2(a):
    hi = a.astype(BF16)
    return hi, (a - hi.astype(F32)).astype(BF16)


def split3(a):
    hi, mid = split2(a)
    lo = (a - hi.astype(F32) - mid.astype(F32)).astype(BF16)
    return hi, mid, lo


def joined(a, b, dims):
    ((ka,), (kb,)), _ = dims
    return dot(jnp.concatenate(a, ka), jnp.concatenate(b, kb), dims)


def dot2(a, b, dims):
    return joined([a, a], b, dims)


def dot3(a, b, dims):
    return joined([a[0], a[0], a[1]], [b[0], b[1], b[0]], dims)


def dot3_wide(a, b):
    both = dot(a[0], jnp.concatenate(b, 0), NT)
    return both[:, :STATE] + both[:, STATE:] + dot(a[1], b[0], NT)


def each_rows(body):
    for i in range(L // STEP):
        body(slice(STEP * i, STEP * (i + 1)))


class Views:
    def __init__(self, buffers, kinds, c):
        for name, ref in buffers.items():
            kind = kinds[name]
            if kind in ("tok", "near_tok"):
                ref = ref.at[pl.ds(pl.multiple_of(c * L, L), L), :]
            elif kind == "row":
                ref = ref.at[:, pl.ds(pl.multiple_of(c * L, L), L)]
            elif kind == "state":
                ref = ref.at[c]
            setattr(self, name, ref)


def staged(body, ins, outs, scratch, name, flops, backward=False, begin=None, end=None):
    kinds = {k: kind for k, (_, kind) in ins.items()}
    kinds.update({k: kind for k, (_, _, kind) in outs.items()})
    kinds.update({k: "row" if s == (H, T) else "all" for k, (s, _) in scratch.items()})
    n, m = len(ins), len(outs)
    moving = ("tok", "state")
    here = [k for k in ins if kinds[k] in ("near", "near_tok")]
    copied = [k for k in outs if kinds[k] == "copy"]
    buffered_in = [k for k in ins if k not in here]
    buffered_out = [k for k in outs if k not in copied]

    def part(ref, kind, c):
        if kind == "tok":
            return ref.at[pl.ds(pl.multiple_of(c * L, L), L), :]
        return ref.at[c]

    def kernel(*refs):
        far_in = dict(zip(ins, refs[:n]))
        far_out = dict(zip(outs, refs[n : n + m]))
        near = dict(zip([*buffered_in, *buffered_out, *scratch], refs[n + m : -1]))
        near.update({k: far_in[k] for k in here})
        sems = refs[-1]
        slot = {k: i for i, k in enumerate([*ins, *outs])}

        def copy_in(k, c):
            return pltpu.make_async_copy(part(far_in[k], kinds[k], c), part(near[k], kinds[k], c), sems.at[slot[k], c])

        def copy_out(k, c):
            return pltpu.make_async_copy(part(near[k], kinds[k], c), part(far_out[k], kinds[k], c), sems.at[slot[k], c])

        once = [
            pltpu.make_async_copy(far_in[k], near[k], sems.at[slot[k], 0])
            for k in buffered_in
            if kinds[k] not in moving
        ]
        passed = [
            pltpu.make_async_copy(near[k.removesuffix("_copy")], far_out[k], sems.at[slot[k], 0]) for k in copied
        ]
        for copy in once:
            copy.start()
        for c in reversed(range(C)) if backward else range(C):
            for k in ins:
                if kinds[k] in moving:
                    copy_in(k, c).start()
        for copy in passed:
            copy.start()
        for copy in once:
            copy.wait()
        whole = Views(near, {k: "all" for k in near}, 0)
        if begin is not None:
            begin(whole)

        def step(i, carry):
            c = C - 1 - i if backward else i
            for k in ins:
                if kinds[k] in moving:
                    copy_in(k, c).wait()
            body(c, Views(near, kinds, c))
            for k in outs:
                if kinds[k] in moving:
                    copy_out(k, c).start()
            return carry

        lax.fori_loop(0, C, step, 0)
        if end is not None:
            end(whole)
        once = [
            pltpu.make_async_copy(near[k], far_out[k], sems.at[slot[k], 0])
            for k in buffered_out
            if kinds[k] not in moving
        ]
        for copy in once:
            copy.start()
        for c in range(C):
            for k in outs:
                if kinds[k] in moving:
                    copy_out(k, c).wait()
        for copy in once + passed:
            copy.wait()

    far = pl.BlockSpec(memory_space=pl.ANY)
    return pl.pallas_call(
        kernel,
        out_shape=tuple(pltpu.HBM(s, d) for s, d, _ in outs.values()),
        in_specs=[pl.BlockSpec(memory_space=pltpu.VMEM) if k in here else far for k in ins],
        out_specs=tuple([far] * m),
        scratch_shapes=[
            *[pltpu.VMEM(ins[k][0].shape, ins[k][0].dtype) for k in buffered_in],
            *[pltpu.VMEM(*outs[k][:2]) for k in buffered_out],
            *[pltpu.VMEM(s, d) for s, d in scratch.values()],
            pltpu.SemaphoreType.DMA((n + m, C)),
        ],
        compiler_params=pltpu.CompilerParams(vmem_limit_bytes=VMEM_NEAR if here else VMEM_LIMIT),
        cost_estimate=pl.CostEstimate(flops=flops, bytes_accessed=8 * 2**20, transcendentals=0),
        name=name,
    )(*[pltpu.with_memory_space_constraint(ins[k][0], pltpu.VMEM if k in here else pltpu.HBM) for k in ins])


def expand(pk, which, e3):
    return dot(pk[2 * H * which : 2 * H * (which + 1), :], e3[0 : 2 * H, :], TN)


def prep_kernel(dt_ref, par_ref, st_ref, e3_ref, pk_ref, rf_ref, mask_ref, me_ref, mw_ref, thx_ref):
    bias = par_ref[:, 0:1]
    nega = -jnp.exp(par_ref[:, 1:2])
    row = lax.broadcasted_iota(jnp.int32, (L, L), 0)
    col = lax.broadcasted_iota(jnp.int32, (L, L), 1)
    tri = (row <= col).astype(F32).astype(BF16)
    causal = row >= col
    first = lax.broadcasted_iota(jnp.int32, (H, L), 0) == 0
    lane = lax.broadcasted_iota(jnp.int32, (H, 128), 1)
    ones = jnp.ones((H, L), BF16)
    thr, kap, leave, enter = [], [], [], []

    def put(which, at, value):
        base = 2 * H * which
        pk_ref[base : base + H, at], pk_ref[base + H : base + 2 * H, at] = split2(value)

    for c in range(C):
        at = slice(c * L, (c + 1) * L)
        pre = dt_ref[:, at] + bias
        dt = jax.nn.softplus(pre)
        rf_ref[0:H, at] = dt
        rf_ref[H : 2 * H, at] = jax.nn.sigmoid(pre)
        rate = dt * nega
        parts = dot(jnp.concatenate(split3(rate), 0), tri, NN)
        cum = parts[0:H] + parts[H : 2 * H] + parts[2 * H : 3 * H]
        starts = jnp.broadcast_to(st_ref[:, at].astype(F32), (H, L))
        seg = dot(starts.astype(BF16), tri, NN)
        cum_end = cum[:, L - 1 : L]
        seg_end = seg[:, L - 1 : L]
        half = 0.5 * cum_end
        put(ALPHA, at, jnp.exp(cum - half))
        put(DTBETA, at, dt * jnp.exp(half - cum))
        leave.append(jnp.where(seg == seg_end, dt * jnp.exp(cum_end - cum), 0.0))
        enter.append(jnp.where(seg == 0.0, jnp.exp(cum), 0.0))
        seg_first = jnp.where(first, seg, 0.0).astype(BF16)
        seg_col = dot(seg_first, ones, TN)
        mask = causal & (seg_col == seg[0:1, :])
        mask_ref[at, :] = mask.astype(F32).astype(BF16)
        to_end = jnp.where(first & (seg == seg_end), 1.0, 0.0).astype(BF16)
        from_start = jnp.where(first & (seg == 0.0), 1.0, 0.0).astype(BF16)
        me_ref[at, :] = dot(to_end, ones[:, :128], TN).astype(BF16)
        mw_ref[at, :] = dot(from_start, ones[:, :128], TN).astype(BF16)
        thr.append(jnp.where(seg_end == 0.0, jnp.exp(cum_end), 0.0))
        kap.append(jnp.exp(half))
    passed = jnp.ones((H, 1), F32)
    before = []
    for c in range(C):
        before.append(passed)
        put(FROM_START, slice(c * L, (c + 1) * L), enter[c] * passed)
        passed = passed * thr[c]
    columns = [*thr, *kap, *before, passed]
    passed = jnp.ones((H, 1), F32)
    for c in reversed(range(C)):
        put(TO_END, slice(c * L, (c + 1) * L), leave[c] * passed)
        passed = passed * thr[c]
    table = jnp.zeros((H, 128), F32)
    for k, v in enumerate(columns):
        table = jnp.where(lane == k, v, table)
    wide = dot(jnp.concatenate(split3(table), 0), e3_ref[...], TN)
    thx_ref[...] = wide[0:TABLE]


def states_body(c, r):
    scale = expand(r.pk, TO_END, r.e3)

    def rows(at):
        r.hi[at, :], r.lo[at, :] = split2(r.x[at, :].astype(F32) * scale[at, :])

    each_rows(rows)
    new = dot2(r.bc[:, :STATE], (r.hi[...], r.lo[...]), TN)
    r.acc[...] += new


def clear(r):
    r.acc[...] = jnp.zeros((STATE, W), F32)


def states_end(r):
    r.pay[:, :W] = r.acc[...]
    total = r.thx[TOTAL : TOTAL + 1, :]
    block = jnp.concatenate([total[:, 128 * k : 128 * (k + 1)] for k in range(ROWS)], 0)
    for d in range(SEQ):
        r.pay[ROWS * d : ROWS * (d + 1), W:] = block


def through_row(got_ref, j):
    block = got_ref[ROWS * j : ROWS * (j + 1), W:]
    return jnp.concatenate([block[k : k + 1, :] for k in range(ROWS)], 1)


def scan_forward_kernel(got_ref, out_ref, through_ref):
    acc = jnp.zeros((ROWS, W), F32)
    for j in range(SEQ):
        at = slice(ROWS * j, ROWS * (j + 1))
        out_ref[at, :] = acc
        through = through_row(got_ref, j)
        through_ref[j : j + 1, :] = through
        acc = through * acc + got_ref[at, :W]


def scan_backward_kernel(got_ref, through_ref, out_ref):
    acc = jnp.zeros((ROWS, W), F32)
    for j in reversed(range(SEQ)):
        at = slice(ROWS * j, ROWS * (j + 1))
        out_ref[at, :] = acc
        acc = through_ref[j : j + 1, :] * acc + got_ref[at, :]


def within_body(c, r):
    ex = expand(r.pk, DTBETA, r.e3)
    al = expand(r.pk, ALPHA, r.e3)
    fin = expand(r.pk, TO_END, r.e3)

    def scale(at):
        x = r.x[at, :].astype(F32)
        r.hi[at, :], r.lo[at, :] = split2(x * ex[at, :])
        r.xhi[at, :], r.xlo[at, :] = split2(x * fin[at, :])

    each_rows(scale)
    b = r.bc[:, :STATE]
    cc = r.bc[:, STATE:]
    g = split2(dot(cc, b, NT) * r.mask[...].astype(F32))
    xs = (r.hi[...], r.lo[...])
    kappa = r.thx[pl.ds(KAP + c, 1), :]
    r.sloc[...] = r.acc[...]
    res = dot3(g, xs, NN) + dot2(cc * r.mw[...], split2(kappa * r.acc[...]), NN)
    r.ys[...] = al * res
    r.acc[...] = r.thx[pl.ds(THR + c, 1), :] * r.acc[...] + kappa * dot2(b * r.me[...], xs, TN)


def norm_begin(r):
    r.shi[...], r.slo[...] = split2(r.sin[...])
    r.gain_acc[...] = jnp.zeros((8, W), F32)
    r.skip_acc[...] = jnp.zeros((8, W), F32)
    r.back[...] = jnp.zeros((STATE, W), F32)


def norm_body(c, r):
    cc = r.bc[:, STATE:]
    win = expand(r.pk, FROM_START, r.e3)
    res = dot2(cc, (r.shi[...], r.slo[...]), NN)
    gain = r.vec[0:1, :]
    skip = r.vec[1:2, :]

    def body(at):
        weight = win[at, :]
        x = r.x[at, :].astype(F32)
        z = r.z[at, :].astype(F32)
        out = r.go[at, :].astype(F32)
        ys = r.ys[at, :] + weight * res[at, :]
        y = ys + skip * x
        logistic = jax.nn.sigmoid(z)
        silu = z * logistic
        gated = y * silu
        grad_normed = out * gain
        square = jnp.sum(gated * gated, axis=1, keepdims=True) * (1.0 / W)
        cross = jnp.sum(grad_normed * gated, axis=1, keepdims=True) * (1.0 / W)
        inv = lax.rsqrt(square + EPSILON)
        normed = gated * inv
        grad_gated = inv * (grad_normed - normed * (inv * cross))
        gy = grad_gated * silu
        gz = grad_gated * y * (logistic + silu * (1.0 - logistic))
        r.gz[at, :] = gz.astype(BF16)
        r.gy[at, :] = gy
        gpart = out * normed
        spart = gy * x
        r.gain_acc[...] += gpart[0:8] + gpart[8:16]
        r.skip_acc[...] += spart[0:8] + spart[8:16]
        r.hi[at, :], r.lo[at, :] = split2(gy * weight)
        r.rhi[at, :], r.rlo[at, :] = split2(gy * ys)

    each_rows(body)
    r.r[...] = dot2(r.e3[0:H, :], (r.rhi[...], r.rlo[...]), NT)
    new = dot2(cc, (r.hi[...], r.lo[...]), TN)
    r.back[...] += new


def norm_end(r):
    r.sums[0:1, :] = jnp.sum(r.gain_acc[...], axis=0, keepdims=True)
    r.sums[1:2, :] = jnp.sum(r.skip_acc[...], axis=0, keepdims=True)
    r.sums[2:8, :] = jnp.zeros((6, W), F32)


def local_x_body(c, r):
    ex = expand(r.pk, DTBETA, r.e3)
    al = expand(r.pk, ALPHA, r.e3)

    def scale(at):
        r.ghi[at, :], r.glo[at, :] = split2(r.gy[at, :] * al[at, :])

    each_rows(scale)
    b = r.bc[:, :STATE]
    cc = r.bc[:, STATE:]
    gys = (r.ghi[...], r.glo[...])
    g = split2(dot(cc, b, NT) * r.mask[...].astype(F32))
    kappa = r.thx[pl.ds(KAP + c, 1), :]
    r.dloc[...] = r.acc[...]
    res = dot3(g, gys, TN) + dot2(b * r.me[...], split2(kappa * r.acc[...]), NN)
    skip = r.vec[1:2, :]

    def finish(at):
        scaled = ex[at, :] * res[at, :]
        r.gx[at, :] = scaled + skip * r.gy[at, :]
        r.rhi[at, :], r.rlo[at, :] = split2(scaled * r.x[at, :].astype(F32))

    each_rows(finish)
    r.u[...] = dot2(r.e3[0:H, :], (r.rhi[...], r.rlo[...]), NT)
    r.acc[...] = r.thx[pl.ds(THR + c, 1), :] * r.acc[...] + kappa * dot2(cc * r.mw[...], gys, TN)


def local_bc_body(c, r):
    ex = expand(r.pk, DTBETA, r.e3)
    al = expand(r.pk, ALPHA, r.e3)

    def scale(at):
        r.xhi[at, :], r.xlo[at, :] = split2(r.x[at, :].astype(F32) * ex[at, :])
        r.ghi[at, :], r.glo[at, :] = split2(r.gy[at, :] * al[at, :])

    each_rows(scale)
    b = r.bc[:, :STATE]
    cc = r.bc[:, STATE:]
    gys = (r.ghi[...], r.glo[...])
    xs = (r.xhi[...], r.xlo[...])
    q = split2(dot3(gys, xs, NT) * r.mask[...].astype(F32))
    kappa = r.thx[pl.ds(KAP + c, 1), :]
    state = split2(kappa * (r.sloc[...] + r.thx[pl.ds(PRE + c, 1), :] * r.sin[...]))
    dstate = split2(kappa * r.dloc[...])
    gb = joined(q, [cc, cc], TN) + r.me[...].astype(F32) * dot3_wide(xs, dstate)
    gc = joined(q, [b, b], NN) + r.mw[...].astype(F32) * dot3_wide(gys, state)
    r.gbc[:, :STATE] = gb
    r.gbc[:, STATE:] = gc


def final_begin(r):
    r.dhi[...], r.dlo[...] = split2(r.din[...])


def final_bc_body(c, r):
    gb = r.gbc[:, :STATE] + dot3_wide((r.xhi[...], r.xlo[...]), (r.dhi[...], r.dlo[...]))
    r.out[:, :STATE] = gb.astype(BF16)
    r.out[:, STATE:] = r.gbc[:, STATE:].astype(BF16)


def final_x_body(c, r):
    fin = expand(r.pk, TO_END, r.e3)
    v = dot2(r.bc[:, :STATE], (r.dhi[...], r.dlo[...]), NN)

    def body(at):
        scaled = fin[at, :] * v[at, :]
        r.gxo[at, :] = (r.gx[at, :] + scaled).astype(BF16)
        r.rhi[at, :], r.rlo[at, :] = split2(scaled * r.x[at, :].astype(F32))

    each_rows(body)
    r.uu[...] = r.u[...] + dot2(r.e3[0:H, :], (r.rhi[...], r.rlo[...]), NT)


def final_x_end(r):
    heads = r.e3[0:H, :]
    state = r.pay[:, :W] + r.thx[TOTAL : TOTAL + 1, :] * r.sin[...]
    ends = jnp.broadcast_to(jnp.sum(state * r.din[...], axis=0, keepdims=True), (H, W))
    carry = sum(dot(heads, part, NT) for part in split3(ends))[:, 0:1]
    row = lax.broadcasted_iota(jnp.int32, (L, L), 0)
    col = lax.broadcasted_iota(jnp.int32, (L, L), 1)
    tri = (row >= col).astype(F32).astype(BF16)
    nega = -jnp.exp(r.par[:, 1:2])
    alog_part = jnp.zeros((H, 1), F32)
    bias_part = jnp.zeros((H, 1), F32)
    for c in reversed(range(C)):
        at = slice(c * L, (c + 1) * L)
        u = r.uu[:, at]
        dt = r.rf[0:H, at]
        parts = dot(jnp.concatenate(split3(r.r[:, at] - u), 0), tri, NN)
        later = parts[0:H] + parts[H : 2 * H] + parts[2 * H : 3 * H]
        grad_rate = later + carry
        carry = carry + later[:, 0:1]
        grad_dt = (u / dt + grad_rate * nega) * r.rf[H : 2 * H, at]
        r.gdt[:, at] = grad_dt
        alog_part += jnp.sum(grad_rate * dt, axis=1, keepdims=True)
        bias_part += jnp.sum(grad_dt, axis=1, keepdims=True)
    skips = jnp.broadcast_to(r.sums[1:2, :], (H, W))
    skip_part = sum(dot(heads, part, NT) for part in split3(skips))[:, 0:1]
    lane = lax.broadcasted_iota(jnp.int32, (H, 128), 1)
    right = jnp.where(
        lane == 0, skip_part, jnp.where(lane == 1, alog_part * nega, jnp.where(lane == 2, bias_part, 0.0))
    )
    gains = r.sums[0:1, :]
    left = jnp.concatenate([gains[:, 128 * k : 128 * (k + 1)] for k in range(8)], 0)
    left = jnp.concatenate([left, jnp.zeros((8, 128), F32)], 0)
    for d in range(SEQ):
        r.params[H * d : H * (d + 1), :128] = left
        r.params[H * d : H * (d + 1), 128:] = right


def head_matrix():
    one = np.arange(W)[None, :] // HEAD_DIM == np.arange(H)[:, None]
    return jnp.asarray(np.concatenate([one, one, one], 0), BF16)


def shard_body(
    x_in, z_gate, b_proj, c_proj, dt_raw, dt_bias, a_log, skip, norm_weight, doc_starts, grad_out
):
    e3 = head_matrix()
    par = jnp.pad(jnp.stack([dt_bias, a_log], 1), ((0, 0), (0, 126)))
    vec = jnp.pad(
        jnp.stack([norm_weight, jnp.repeat(skip, HEAD_DIM)], 0), ((0, 6), (0, 0))
    )
    starts = doc_starts.reshape(1, T)
    mine = jnp.concatenate(
        [b_proj.reshape(128, GRP, STATE), c_proj.reshape(128, GRP, STATE)], 2
    ).transpose(1, 0, 2)
    bc = lax.all_to_all(mine, "head", split_axis=0, concat_axis=0, tiled=True).reshape(T, 2 * STATE)

    sds = pltpu.HBM
    pk, rf, mask, me, mw, thx = pl.pallas_call(
        prep_kernel,
        out_shape=(
            sds((8 * H, T), BF16),
            sds((2 * H, T), F32),
            sds((T, L), BF16),
            sds((T, 128), BF16),
            sds((T, 128), BF16),
            sds((TABLE, W), F32),
        ),
        compiler_params=pltpu.CompilerParams(vmem_limit_bytes=VMEM_LIMIT),
        name="prep",
    )(*[pltpu.with_memory_space_constraint(a, pltpu.HBM) for a in (dt_raw, par, starts, e3)])

    state = ((STATE, W), F32)
    half = ((L, W), BF16)
    unit = 2 * T * L * W
    common = {"e3": (e3, "all"), "pk": (pk, "row"), "thx": (thx, "all")}
    x = {"x": (x_in, "tok")}
    masks = {"mask": (mask, "tok"), "me": (me, "tok"), "mw": (mw, "tok")}

    pay, bc = staged(
        states_body,
        common | {"bc": (bc, "near_tok")} | x,
        {"pay": ((STATE, W + 128), F32, "all"), "bc_copy": ((T, 2 * STATE), BF16, "copy")},
        {"acc": state, "hi": half, "lo": half},
        "states",
        2 * unit,
        begin=clear,
        end=states_end,
    )

    def scan(kernel, name, outs, got, *others):
        return pl.pallas_call(
            kernel,
            out_shape=outs,
            in_specs=[pl.BlockSpec(memory_space=pltpu.VMEM)] * (1 + len(others)),
            compiler_params=pltpu.CompilerParams(vmem_limit_bytes=16 * 2**20),
            name=name,
        )(
            pltpu.with_memory_space_constraint(got, pltpu.VMEM),
            *[pltpu.with_memory_space_constraint(a, pltpu.HBM) for a in others],
        )

    def exchange(v):
        return lax.all_to_all(v, "seq", split_axis=0, concat_axis=0, tiled=True)

    bcs = {"bc": (bc, "tok")}
    got = exchange(pay)
    ys, sloc, xhi, xlo = staged(
        within_body,
        common | bcs | masks | x,
        {
            "ys": ((T, W), F32, "tok"),
            "sloc": ((C, STATE, W), F32, "state"),
            "xhi": ((T, W), BF16, "tok"),
            "xlo": ((T, W), BF16, "tok"),
        },
        {"acc": state, "hi": half, "lo": half},
        "within",
        7 * unit,
        begin=clear,
    )
    (ys, sloc, xhi, xlo), got = lax.optimization_barrier(((ys, sloc, xhi, xlo), got))
    before, through = scan(
        scan_forward_kernel, "scan_forward", (sds((STATE, W), F32), sds((SEQ, W), F32)), got
    )
    sin = exchange(before)

    gy, gz, r, back, sums, sin = staged(
        norm_body,
        common
        | {"vec": (vec, "all"), "sin": (sin, "near")}
        | bcs
        | {"ys": (ys, "tok"), "z": (z_gate, "tok"), "go": (grad_out, "tok")}
        | x,
        {
            "gy": ((T, W), F32, "tok"),
            "gz": ((T, W), BF16, "tok"),
            "r": ((H, T), F32, "row"),
            "back": ((STATE, W), F32, "all"),
            "sums": ((8, W), F32, "all"),
            "sin_copy": ((STATE, W), F32, "copy"),
        },
        {
            "gain_acc": ((8, W), F32),
            "skip_acc": ((8, W), F32),
            "shi": ((STATE, W), BF16),
            "slo": ((STATE, W), BF16),
            "hi": half,
            "lo": half,
            "rhi": half,
            "rlo": half,
        },
        "norm",
        6 * unit,
        begin=norm_begin,
        end=norm_end,
    )

    got_back = exchange(back)
    gx, u, dloc = staged(
        local_x_body,
        common | {"vec": (vec, "all")} | bcs | masks | {"gy": (gy, "tok")} | x,
        {
            "gx": ((T, W), F32, "tok"),
            "u": ((H, T), F32, "row"),
            "dloc": ((C, STATE, W), F32, "state"),
        },
        {"acc": state, "ghi": half, "glo": half, "rhi": half, "rlo": half},
        "local_x",
        7 * unit,
        backward=True,
        begin=clear,
    )
    dloc, got_back = lax.optimization_barrier((dloc, got_back))
    behind = scan(scan_backward_kernel, "scan_backward", sds((STATE, W), F32), got_back, through)
    din = exchange(behind)
    (gbc,) = staged(
        local_bc_body,
        common
        | {"sin": (sin, "all")}
        | bcs
        | masks
        | {"gy": (gy, "tok"), "sloc": (sloc, "state"), "dloc": (dloc, "state")}
        | x,
        {"gbc": ((T, 2 * STATE), F32, "tok")},
        {"ghi": half, "glo": half, "xhi": half, "xlo": half},
        "local_bc",
        7 * unit,
    )

    gbc, din = lax.optimization_barrier((gbc, din))
    gbc, din = staged(
        final_bc_body,
        {"din": (din, "near"), "gbc": (gbc, "tok"), "xhi": (xhi, "tok"), "xlo": (xlo, "tok")},
        {"out": ((T, 2 * STATE), BF16, "tok"), "din_copy": ((STATE, W), F32, "copy")},
        {"dhi": ((STATE, W), BF16), "dlo": ((STATE, W), BF16)},
        "final_bc",
        2 * unit,
        begin=final_begin,
    )
    gbc, gx = lax.optimization_barrier((gbc, gx))
    back_bc = lax.all_to_all(
        gbc.reshape(GRP, 128, 2 * STATE), "head", split_axis=0, concat_axis=0, tiled=True
    )
    grad_x, grad_dt, params = staged(
        final_x_body,
        common
        | {
            "din": (din, "all"),
            "sin": (sin, "all"),
            "pay": (pay, "all"),
            "par": (par, "all"),
            "sums": (sums, "all"),
            "rf": (rf, "row"),
            "r": (r, "row"),
            "u": (u, "row"),
        }
        | bcs
        | {"gx": (gx, "tok")}
        | x,
        {
            "gxo": ((T, W), BF16, "tok"),
            "gdt": ((H, T), F32, "row"),
            "params": ((SEQ * H, 256), F32, "all"),
        },
        {
            "uu": ((H, T), F32),
            "dhi": ((STATE, W), BF16),
            "dlo": ((STATE, W), BF16),
            "rhi": half,
            "rlo": half,
        },
        "final_x",
        3 * unit,
        begin=final_begin,
        end=final_x_end,
    )
    params, back_bc = lax.optimization_barrier((params, back_bc))
    grad_b = back_bc[:, :, :STATE].transpose(1, 0, 2).reshape(128, GRP * STATE)
    grad_c = back_bc[:, :, STATE:].transpose(1, 0, 2).reshape(128, GRP * STATE)
    summed = jnp.sum(exchange(params).reshape(SEQ, H, 256), axis=0)
    grad_gain = summed[:8, :128].reshape(W)
    grad_skip, grad_alog, grad_bias = summed[:, 128], summed[:, 129], summed[:, 130]
    return (grad_x, gz, grad_b, grad_c, grad_dt, grad_alog, grad_bias, grad_skip, grad_gain)


def solution(mesh):
    in_specs = (
        P("seq", "head"),
        P("seq", "head"),
        P(("seq", "head"), None),
        P(("seq", "head"), None),
        P("head", "seq"),
        P("head"),
        P("head"),
        P("head"),
        P("head"),
        P("seq"),
        P("seq", "head"),
    )
    out_specs = (
        P("seq", "head"),
        P("seq", "head"),
        P(("seq", "head"), None),
        P(("seq", "head"), None),
        P("head", "seq"),
        P("head"),
        P("head"),
        P("head"),
        P("head"),
    )
    return jax.shard_map(shard_body, mesh=mesh, in_specs=in_specs, out_specs=out_specs, check_vma=False)
```

time: 206 us -> 140 us (0.68)
  blocking collectives: 52.4 us -> 0 us
  local copies, waits for them, and re-layouts: 46 us -> 5.81 us
  starting transfers between devices: 17.6 us -> 39.9 us
  waiting for transfers between devices: 12.7 us -> 25.1 us
  Pallas kernels: 72.4 us -> 65 us
    all_to_all x3 -> x0, blocking collectives: 52.4 us -> none  [exchange(): return lax.all_to_all(v, 'seq', split_axis=0, concat_axis=0, tiled=True)]
    unnamed x101 -> x11, local copies, waits for them, and re-layouts: 41.2 us -> 1.08 us
    all_to_all x2 -> x5, starting transfers between devices: 7.83 us -> 30.1 us  [exchange(): return lax.all_to_all(v, 'seq', split_axis=0, concat_axis=0, tiled=True)]
    all_to_all x2 -> x5, waiting for transfers between devices: 0.01 us -> 19.7 us  [exchange(): return lax.all_to_all(v, 'seq', split_axis=0, concat_axis=0, tiled=True)]
    pallas_call x8 -> x10, Pallas kernels: 72.4 us -> 65 us  [the longest x7 59 us: staged(): pl.pallas_call(kernel, out_shape=tuple((pltpu.HBM(s, d) for s, d, _ in ou...]
    all_to_all x1, waiting for transfers between devices: 7.6 us -> 0.63 us  [shard_body(): lax.all_to_all(gbc.reshape(GRP, 128, 2 * STATE), 'head', split_axis=0, co...]
  transfers between devices with their start and end apart: 4 -> 7, of which waited for: 2 -> 5; matrix products, arithmetic and copies ran while one was open for 1% -> 2% of each run, Pallas kernels for 15% -> 30%
where the time goes in v3:
time: 140 us; the launch traced here: 138 us
  Pallas kernels  65 us (46%)
  starting transfers between devices  39.9 us (28%)
  waiting for transfers between devices  25.1 us (18%)
  local copies, waits for them, and re-layouts  5.81 us (4%)
  other arithmetic  1.52 us (1%)
    pallas_call x7, Pallas kernels, staged(): pl.pallas_call(kernel, out_shape=tuple((pltpu.HBM(s, d) for s, d, _ in ou...  59 us
    all_to_all x5, starting transfers between devices, exchange(): return lax.all_to_all(v, 'seq', split_axis=0, concat_axis=0, tiled=True)  30.1 us
    all_to_all x5, waiting for transfers between devices, exchange(): return lax.all_to_all(v, 'seq', split_axis=0, concat_axis=0, tiled=True)  19.7 us
    all_to_all x1, starting transfers between devices, shard_body(): lax.all_to_all(mine, 'head', split_axis=0, concat_axis=0, tiled=True)  4.92 us
    all_to_all x1, starting transfers between devices, shard_body(): lax.all_to_all(gbc.reshape(GRP, 128, 2 * STATE), 'head', split_axis=0, co...  4.88 us
    all_to_all x1, waiting for transfers between devices, shard_body(): lax.all_to_all(mine, 'head', split_axis=0, concat_axis=0, tiled=True)  4.72 us
    pallas_call x1, Pallas kernels, shard_body(): pl.pallas_call(prep_kernel, out_shape=(sds((8 * H, T), BF16), sds((2 * H,...  3.47 us
  transfers between devices with their start and end apart: 7, of which 5 were waited for; matrix products, arithmetic and copies ran while one was open for 2% of the time, Pallas kernels for 30%

profile of v3, /device:TPU:8, one launch (start us, length us, event | category | flops | bytes accessed | tf_op | source)
XLA Modules:
  0.0 138.2 jit_solution(14122168572914873307)
XLA Ops:
  0.7 0.9 copy-done
  1.6 1.1 copy_bitcast_fusion.2
  2.7 0.9 maximum_bitcast_fusion
  3.5 4.9 %all-to-all-start = ((bf16[8,128,256]{2,1,0:T(8,128)(2,1)}), bf16[8,128,256]{2,1,0:T(8,128)(2,1)S(1)}, u32[]{:S(2)}, u32[]{:S(2)}) async-start(bf16[8,128,256]{2,1,0:T(8,128)(2,1)} %maximum_bitcast_fusion), calls=%async_computation | async-start | bytes 1048576 | tf_op jit(solution)/shard_map/all_to_all | solution.py:500
  8.6 0.6 pad.8.par_ref.refs_6_
  9.2 3.5 %prep.1 = (bf16[128,1024]{1,0:T(8,128)(2,1)}, f32[32,1024]{1,0:T(8,128)}, bf16[1024,256]{1,0:T(8,128)(2,1)}, bf16[1024,128]{1,0:T(8,128)(2,1)}, bf16[1024,128]{1,0:T(8,128)(2,1)}, /*index=5*/f32[16,1024]{1,0:T(8,128)}) custom-call(f32[16,1024]{1,0:T(8,128)} %dt_ref.1, f32[16,128]{1,0:T(8,128)} %pad.8.par_ref.refs_6_, s32[1,1024]{1,0:T(1,128)} %bitcast.54, ...), custom_call_target="tpu_custom_call" | custom-call | tf_op jit(solution)/shard_map/prep/pallas_call | solution.py:503
  12.6 4.7 %all-to-all-done = bf16[8,128,256]{2,1,0:T(8,128)(2,1)S(1)} async-done(((bf16[8,128,256]{2,1,0:T(8,128)(2,1)}), bf16[8,128,256]{2,1,0:T(8,128)(2,1)S(1)}, u32[]{:S(2)}, u32[]{:S(2)}) %all-to-all-start) | async-done | bytes 524320 | tf_op jit(solution)/shard_map/all_to_all | solution.py:500
  17.3 4.8 %states.1 = (f32[128,1152]{1,0:T(8,128)}, bf16[1024,256]{1,0:T(8,128)(2,1)}) custom-call(bf16[48,1024]{1,0:T(8,128)(2,1)} %constant.6.clone.e3_ref.refs_0_, bf16[128,1024]{1,0:T(8,128)(2,1)} %get-tuple-element.50.refs_1_, f32[16,1024]{1,0:T(8,128)} %get-tuple-element.51.refs_2_, bf16[1024,256]{1,0:T(8,128)(2,1)S(1)} %bitcast.45, bf16[1024,1024]{1,0:T(8,128)(2,1)} %refs_13_.1), custom_call_target="tpu_custom_call" | custom-call | flops 1073741824 | bytes 8388608 | tf_op jit(solution)/shard_map/states/pallas_call | solution.py:169
  22.1 7.9 %all-to-all-start.1 = ((f32[16,8,1152]{2,1,0:T(8,128)}), f32[16,8,1152]{2,1,0:T(8,128)S(1)}, u32[]{:S(2)}, u32[]{:S(2)}) async-start(f32[16,8,1152]{2,1,0:T(8,128)} %bitcast.46), calls=%async_computation.1 | async-start | bytes 1179648 | tf_op jit(solution)/shard_map/all_to_all | solution.py:548
  30.0 8.7 %within.1 = (f32[1024,1024]{1,0:T(8,128)}, f32[4,128,1024]{2,1,0:T(8,128)}, bf16[1024,1024]{1,0:T(8,128)(2,1)}, bf16[1024,1024]{1,0:T(8,128)(2,1)}) custom-call(bf16[48,1024]{1,0:T(8,128)(2,1)} %constant.6.clone.e3_ref.refs_0_, bf16[128,1024]{1,0:T(8,128)(2,1)} %get-tuple-element.50.refs_1_, f32[16,1024]{1,0:T(8,128)} %get-tuple-element.51.refs_2_, ...), custom_call_target="tpu_custom_call" | custom-call | flops 3758096384 | bytes 8388608 | tf_op jit(solution)/shard_map/within/pallas_call | solution.py:169
  38.7 3.0 %all-to-all-done.1 = f32[16,8,1152]{2,1,0:T(8,128)S(1)} async-done(((f32[16,8,1152]{2,1,0:T(8,128)}), f32[16,8,1152]{2,1,0:T(8,128)S(1)}, u32[]{:S(2)}, u32[]{:S(2)}) %all-to-all-start.1) | async-done | bytes 589856 | tf_op jit(solution)/shard_map/all_to_all | solution.py:548
  41.7 0.9 scan_forward.1
  42.6 4.2 %all-to-all-start.2 = ((f32[16,8,1024]{2,1,0:T(8,128)}), f32[16,8,1024]{2,1,0:T(8,128)S(1)}, u32[]{:S(2)}, u32[]{:S(2)}) async-start(f32[16,8,1024]{2,1,0:T(8,128)} %bitcast.50), calls=%async_computation.2 | async-start | bytes 1048576 | tf_op jit(solution)/shard_map/all_to_all | solution.py:548
  47.0 0.6 select_maximum_fusion.refs_3_
  47.6 9.9 %all-to-all-done.2 = f32[16,8,1024]{2,1,0:T(8,128)S(1)} async-done(((f32[16,8,1024]{2,1,0:T(8,128)}), f32[16,8,1024]{2,1,0:T(8,128)S(1)}, u32[]{:S(2)}, u32[]{:S(2)}) %all-to-all-start.2) | async-done | bytes 524320 | tf_op jit(solution)/shard_map/all_to_all | solution.py:548
  57.6 11.6 %norm.1 = (f32[1024,1024]{1,0:T(8,128)}, bf16[1024,1024]{1,0:T(8,128)(2,1)}, f32[16,1024]{1,0:T(8,128)}, f32[128,1024]{1,0:T(8,128)}, f32[8,1024]{1,0:T(8,128)}, /*index=5*/f32[128,1024]{1,0:T(8,128)}) custom-call(bf16[48,1024]{1,0:T(8,128)(2,1)} %constant.6.clone.e3_ref.refs_0_, bf16[128,1024]{1,0:T(8,128)(2,1)} %get-tuple-element.50.refs_1_, ...), custom_call_target="tpu_custom_call" | custom-call | flops 3221225472 | bytes 8388608 | tf_op jit(solution)/shard_map/norm/pallas_call | solution.py:169
  69.1 3.6 %all-to-all-start.3 = ((f32[16,8,1024]{2,1,0:T(8,128)}), f32[16,8,1024]{2,1,0:T(8,128)S(1)}, u32[]{:S(2)}, u32[]{:S(2)}) async-start(f32[16,8,1024]{2,1,0:T(8,128)} %bitcast.49), calls=%async_computation.3 | async-start | bytes 1048576 | tf_op jit(solution)/shard_map/all_to_all | solution.py:548
  72.7 10.1 %local_x.1 = (f32[1024,1024]{1,0:T(8,128)}, f32[16,1024]{1,0:T(8,128)}, f32[4,128,1024]{2,1,0:T(8,128)}) custom-call(bf16[48,1024]{1,0:T(8,128)(2,1)} %constant.6.clone.e3_ref.refs_0_, bf16[128,1024]{1,0:T(8,128)(2,1)} %get-tuple-element.50.refs_1_, f32[16,1024]{1,0:T(8,128)} %get-tuple-element.51.refs_2_, f32[8,1024]{1,0:T(8,128)} %select_maximum_fusion.refs_3_, ...), custom_call_target="tpu_custom_call" | custom-call | flops 3758096384 | bytes 8388608 | tf_op jit(solution)/shard_map/local_x/pallas_call | solution.py:169
  82.9 1.7 %scan_backward.1 = f32[128,1024]{1,0:T(8,128)} custom-call(f32[128,1024]{1,0:T(8,128)S(1)} %bitcast.43, f32[16,1024]{1,0:T(8,128)} %get-tuple-element.71.through_ref), custom_call_target="tpu_custom_call" | custom-call | tf_op jit(solution)/shard_map/scan_backward/pallas_call | solution.py:536
  84.6 7.2 %all-to-all-start.4 = ((f32[16,8,1024]{2,1,0:T(8,128)}), f32[16,8,1024]{2,1,0:T(8,128)S(1)}, u32[]{:S(2)}, u32[]{:S(2)}) async-start(f32[16,8,1024]{2,1,0:T(8,128)} %bitcast.47), calls=%async_computation.4 | async-start | bytes 1048576 | tf_op jit(solution)/shard_map/all_to_all | solution.py:548
  91.7 11.4 %local_bc.1.refs_1_ = f32[1024,256]{1,0:T(8,128)} custom-call(bf16[48,1024]{1,0:T(8,128)(2,1)} %constant.6.clone.e3_ref.refs_0_, bf16[128,1024]{1,0:T(8,128)(2,1)} %get-tuple-element.50.refs_1_, f32[16,1024]{1,0:T(8,128)} %get-tuple-element.51.refs_2_, f32[128,1024]{1,0:T(8,128)} %get-tuple-element.64.refs_3_.refs_4_, ...), custom_call_target="tpu_custom_call" | custom-call | flops 3758096384 | bytes 8388608 | tf_op jit(solution)/shard_map/local_bc/pallas_call | solution.py:169
  103.1 4.2 %final_bc.1 = (bf16[1024,256]{1,0:T(8,128)(2,1)}, f32[128,1024]{1,0:T(8,128)}) custom-call(f32[128,1024]{1,0:T(8,128)S(1)} %bitcast.44, f32[1024,256]{1,0:T(8,128)} %local_bc.1.refs_1_, bf16[1024,1024]{1,0:T(8,128)(2,1)} %get-tuple-element.74.refs_2_, bf16[1024,1024]{1,0:T(8,128)(2,1)} %get-tuple-element.75.refs_3_), custom_call_target="tpu_custom_call" | custom-call | flops 1073741824 | bytes 8388608 | tf_op jit(solution)/shard_map/final_bc/pallas_call | solution.py:169
  107.3 4.9 %all-to-all-start.5 = ((bf16[8,128,256]{2,1,0:T(8,128)(2,1)}), bf16[8,128,256]{2,1,0:T(8,128)(2,1)S(1)}, u32[]{:S(2)}, u32[]{:S(2)}) async-start(bf16[8,128,256]{2,1,0:T(8,128)(2,1)} %bitcast.48), calls=%async_computation.5 | async-start | bytes 1048576 | tf_op jit(solution)/shard_map/all_to_all | solution.py:646
  112.2 8.3 %final_x.1 = (bf16[1024,1024]{1,0:T(8,128)(2,1)}, f32[16,1024]{1,0:T(8,128)}, f32[256,256]{1,0:T(8,128)}) custom-call(bf16[48,1024]{1,0:T(8,128)(2,1)} %constant.6.clone.e3_ref.refs_0_, bf16[128,1024]{1,0:T(8,128)(2,1)} %get-tuple-element.50.refs_1_, f32[16,1024]{1,0:T(8,128)} %get-tuple-element.51.refs_2_, f32[128,1024]{1,0:T(8,128)} %get-tuple-element.76.refs_3_, ...), custom_call_target="tpu_custom_call" | custom-call | flops 1610612736 | bytes 8388608 | tf_op jit(solution)/shard_map/final_x/pallas_call | solution.py:169
  120.5 0.6 all-to-all-done.5
  121.1 7.2 %all-to-all-start.6 = ((f32[16,16,256]{2,1,0:T(8,128)}), f32[16,16,256]{2,1,0:T(8,128)S(1)}, u32[]{:S(2)}, u32[]{:S(2)}) async-start(f32[16,16,256]{2,1,0:T(8,128)} %bitcast.52), calls=%async_computation.6 | async-start | bytes 524288 | tf_op jit(solution)/shard_map/all_to_all | solution.py:548
  128.4 0.1 slice_bitcast_fusion
  128.5 0.8 copy.52
  129.3 0.8 copy.53
  130.1 6.8 %all-to-all-done.6 = f32[16,16,256]{2,1,0:T(8,128)S(1)} async-done(((f32[16,16,256]{2,1,0:T(8,128)}), f32[16,16,256]{2,1,0:T(8,128)S(1)}, u32[]{:S(2)}, u32[]{:S(2)}) %all-to-all-start.6) | async-done | bytes 262176 | tf_op jit(solution)/shard_map/all_to_all | solution.py:548
  136.9 0.6 slice_bitcast_fusion.2
  137.5 0.7 slice_reduce_fusion
  (16 shorter events, 0.3 us)
Async XLA Ops:
  0.6 1.0 copy-start
  0.7 7.8 %copy-start.4 = (f32[16]{0:T(128)S(1)}, f32[16]{0:T(128)}, u32[]{:S(2)}) copy-start(f32[16]{0:T(128)} %param.17) | copy-start | bytes 196
  0.7 7.8 %copy-start.3 = (f32[16]{0:T(128)S(1)}, f32[16]{0:T(128)}, u32[]{:S(2)}) copy-start(f32[16]{0:T(128)} %param.18) | copy-start | bytes 196
  3.5 13.8 %all-to-all-start = ((bf16[8,128,256]{2,1,0:T(8,128)(2,1)}), bf16[8,128,256]{2,1,0:T(8,128)(2,1)S(1)}, u32[]{:S(2)}, u32[]{:S(2)}) async-start(bf16[8,128,256]{2,1,0:T(8,128)(2,1)} %maximum_bitcast_fusion), calls=%async_computation | async-start | bytes 1048576 | tf_op jit(solution)/shard_map/all_to_all | solution.py:500
  22.1 19.6 %all-to-all-start.1 = ((f32[16,8,1152]{2,1,0:T(8,128)}), f32[16,8,1152]{2,1,0:T(8,128)S(1)}, u32[]{:S(2)}, u32[]{:S(2)}) async-start(f32[16,8,1152]{2,1,0:T(8,128)} %bitcast.46), calls=%async_computation.1 | async-start | bytes 1179648 | tf_op jit(solution)/shard_map/all_to_all | solution.py:548
  30.0 16.8 %copy-start.2 = (f32[16]{0:T(128)S(1)}, f32[16]{0:T(128)}, u32[]{:S(2)}) copy-start(f32[16]{0:T(128)} %param.19) | copy-start | bytes 196
  30.0 17.0 %copy-start.1 = (f32[1024]{0:T(1024)S(1)}, f32[1024]{0:T(1024)}, u32[]{:S(2)}) copy-start(f32[1024]{0:T(1024)} %param.20) | copy-start | bytes 12292
  42.6 15.0 %all-to-all-start.2 = ((f32[16,8,1024]{2,1,0:T(8,128)}), f32[16,8,1024]{2,1,0:T(8,128)S(1)}, u32[]{:S(2)}, u32[]{:S(2)}) async-start(f32[16,8,1024]{2,1,0:T(8,128)} %bitcast.50), calls=%async_computation.2 | async-start | bytes 1048576 | tf_op jit(solution)/shard_map/all_to_all | solution.py:548
  69.1 13.7 %all-to-all-start.3 = ((f32[16,8,1024]{2,1,0:T(8,128)}), f32[16,8,1024]{2,1,0:T(8,128)S(1)}, u32[]{:S(2)}, u32[]{:S(2)}) async-start(f32[16,8,1024]{2,1,0:T(8,128)} %bitcast.49), calls=%async_computation.3 | async-start | bytes 1048576 | tf_op jit(solution)/shard_map/all_to_all | solution.py:548
  84.6 18.5 %all-to-all-start.4 = ((f32[16,8,1024]{2,1,0:T(8,128)}), f32[16,8,1024]{2,1,0:T(8,128)S(1)}, u32[]{:S(2)}, u32[]{:S(2)}) async-start(f32[16,8,1024]{2,1,0:T(8,128)} %bitcast.47), calls=%async_computation.4 | async-start | bytes 1048576 | tf_op jit(solution)/shard_map/all_to_all | solution.py:548
  107.3 13.8 %all-to-all-start.5 = ((bf16[8,128,256]{2,1,0:T(8,128)(2,1)}), bf16[8,128,256]{2,1,0:T(8,128)(2,1)S(1)}, u32[]{:S(2)}, u32[]{:S(2)}) async-start(bf16[8,128,256]{2,1,0:T(8,128)(2,1)} %bitcast.48), calls=%async_computation.5 | async-start | bytes 1048576 | tf_op jit(solution)/shard_map/all_to_all | solution.py:646
  121.1 15.8 %all-to-all-start.6 = ((f32[16,16,256]{2,1,0:T(8,128)}), f32[16,16,256]{2,1,0:T(8,128)S(1)}, u32[]{:S(2)}, u32[]{:S(2)}) async-start(f32[16,16,256]{2,1,0:T(8,128)} %bitcast.52), calls=%async_computation.6 | async-start | bytes 524288 | tf_op jit(solution)/shard_map/all_to_all | solution.py:548

commit v4 on v3

--- a/solution.py
+++ b/solution.py
@@ -26,8 +26,9 @@
 VMEM_LIMIT = 60 * 2**20
 VMEM_NEAR = 48 * 2**20
 
-THR, KAP, PRE, TOTAL, TABLE = 0, 4, 8, 12, 16
-ALPHA, DTBETA, TO_END, FROM_START = 0, 1, 2, 3
+THR, KAP, PRE, TOTAL, BY_ALOG, BY_BIAS, TABLE = 0, 4, 8, 12, 13, 14, 16
+ALPHA, DTBETA, TO_END, FROM_START, END_ALOG, END_BIAS = 0, 1, 2, 3, 4, 5
+SKIPS, ALOGS, BIASES = 0, 2, 4
 
 NN = (((1,), (0,)), ((), ()))
 NT = (((1,), (1,)), ((), ()))
@@ -88,7 +89,7 @@
 def staged(body, ins, outs, scratch, name, flops, backward=False, begin=None, end=None):
     kinds = {k: kind for k, (_, kind) in ins.items()}
     kinds.update({k: kind for k, (_, _, kind) in outs.items()})
-    kinds.update({k: "row" if s == (H, T) else "all" for k, (s, _) in scratch.items()})
+    kinds.update({k: "row" if shape == (H, T) else "all" for k, (shape, _) in scratch.items()})
     n, m = len(ins), len(outs)
     moving = ("tok", "state")
     here = [k for k in ins if kinds[k] in ("near", "near_tok")]
@@ -118,8 +119,9 @@
         once = [
             pltpu.make_async_copy(far_in[k], near[k], sems.at[slot[k], 0])
             for k in buffered_in
-            if kinds[k] not in moving
+            if kinds[k] in ("row", "all")
         ]
+        late = [pltpu.make_async_copy(far_in[k], near[k], sems.at[slot[k], 0]) for k in ins if kinds[k] == "late"]
         passed = [
             pltpu.make_async_copy(near[k.removesuffix("_copy")], far_out[k], sems.at[slot[k], 0]) for k in copied
         ]
@@ -129,7 +131,7 @@
             for k in ins:
                 if kinds[k] in moving:
                     copy_in(k, c).start()
-        for copy in passed:
+        for copy in late + passed:
             copy.start()
         for copy in once:
             copy.wait()
@@ -149,6 +151,8 @@
             return carry
 
         lax.fori_loop(0, C, step, 0)
+        for copy in late:
+            copy.wait()
         if end is not None:
             end(whole)
         once = [
@@ -197,7 +201,7 @@
     first = lax.broadcasted_iota(jnp.int32, (H, L), 0) == 0
     lane = lax.broadcasted_iota(jnp.int32, (H, 128), 1)
     ones = jnp.ones((H, L), BF16)
-    thr, kap, leave, enter = [], [], [], []
+    thr, kap, leave, enter, rest, ratio, sig_rest, rate_sum, sig_sum = [], [], [], [], [], [], [], [], []
 
     def put(which, at, value):
         base = 2 * H * which
@@ -208,10 +212,12 @@
         pre = dt_ref[:, at] + bias
         dt = jax.nn.softplus(pre)
         rf_ref[0:H, at] = dt
-        rf_ref[H : 2 * H, at] = jax.nn.sigmoid(pre)
+        sig = jax.nn.sigmoid(pre)
+        rf_ref[H : 2 * H, at] = sig
         rate = dt * nega
-        parts = dot(jnp.concatenate(split3(rate), 0), tri, NN)
+        parts = dot(jnp.concatenate(split3(rate) + split3(sig), 0), tri, NN)
         cum = parts[0:H] + parts[H : 2 * H] + parts[2 * H : 3 * H]
+        sig_cum = parts[3 * H : 4 * H] + parts[4 * H : 5 * H] + parts[5 * H : 6 * H]
         starts = jnp.broadcast_to(st_ref[:, at].astype(F32), (H, L))
         seg = dot(starts.astype(BF16), tri, NN)
         cum_end = cum[:, L - 1 : L]
@@ -220,6 +226,11 @@
         put(ALPHA, at, jnp.exp(cum - half))
         put(DTBETA, at, dt * jnp.exp(half - cum))
         leave.append(jnp.where(seg == seg_end, dt * jnp.exp(cum_end - cum), 0.0))
+        rest.append(cum_end - cum)
+        ratio.append(sig / dt)
+        sig_rest.append(sig_cum[:, L - 1 : L] - sig_cum)
+        rate_sum.append(cum_end)
+        sig_sum.append(sig_cum[:, L - 1 : L])
         enter.append(jnp.where(seg == 0.0, jnp.exp(cum), 0.0))
         seg_first = jnp.where(first, seg, 0.0).astype(BF16)
         seg_col = dot(seg_first, ones, TN)
@@ -237,11 +248,19 @@
         before.append(passed)
         put(FROM_START, slice(c * L, (c + 1) * L), enter[c] * passed)
         passed = passed * thr[c]
-    columns = [*thr, *kap, *before, passed]
+    columns = [*thr, *kap, *before, passed, passed * sum(rate_sum), passed * nega * sum(sig_sum)]
     passed = jnp.ones((H, 1), F32)
+    rate_after = jnp.zeros((H, 1), F32)
+    sig_after = jnp.zeros((H, 1), F32)
     for c in reversed(range(C)):
-        put(TO_END, slice(c * L, (c + 1) * L), leave[c] * passed)
+        at = slice(c * L, (c + 1) * L)
+        to_shard_end = leave[c] * passed
+        put(TO_END, at, to_shard_end)
+        put(END_ALOG, at, to_shard_end * (rest[c] + rate_after))
+        put(END_BIAS, at, to_shard_end * (ratio[c] + nega * (sig_rest[c] + sig_after)))
         passed = passed * thr[c]
+        rate_after += rate_sum[c]
+        sig_after += sig_sum[c]
     table = jnp.zeros((H, 128), F32)
     for k, v in enumerate(columns):
         table = jnp.where(lane == k, v, table)
@@ -249,15 +268,17 @@
     thx_ref[...] = wide[0:TABLE]
 
 
+def scale_body(c, r):
+    scale = expand(r.pk, TO_END, r.e3)
+
+    def rows(at):
+        r.xhi[at, :], r.xlo[at, :] = split2(r.x[at, :].astype(F32) * scale[at, :])
+
+    each_rows(rows)
+
+
 def states_body(c, r):
-    scale = expand(r.pk, TO_END, r.e3)
-
-    def rows(at):
-        r.hi[at, :], r.lo[at, :] = split2(r.x[at, :].astype(F32) * scale[at, :])
-
-    each_rows(rows)
-    new = dot2(r.bc[:, :STATE], (r.hi[...], r.lo[...]), TN)
-    r.acc[...] += new
+    r.acc[...] += dot2(r.bc[:, :STATE], (r.xhi[...], r.xlo[...]), TN)
 
 
 def clear(r):
@@ -270,6 +291,25 @@
     block = jnp.concatenate([total[:, 128 * k : 128 * (k + 1)] for k in range(ROWS)], 0)
     for d in range(SEQ):
         r.pay[ROWS * d : ROWS * (d + 1), W:] = block
+
+
+def moments_body(c, r):
+    by_alog = expand(r.pk, END_ALOG, r.e3)
+    by_bias = expand(r.pk, END_BIAS, r.e3)
+
+    def rows(at):
+        x = r.x[at, :].astype(F32)
+        r.hi[at, :], r.lo[at, :] = split2(x * by_alog[at, :])
+        r.hi2[at, :], r.lo2[at, :] = split2(x * by_bias[at, :])
+
+    each_rows(rows)
+    b = r.bc[:, :STATE]
+    r.moments[:, :W] += dot2(b, (r.hi[...], r.lo[...]), TN)
+    r.moments[:, W:] += dot2(b, (r.hi2[...], r.lo2[...]), TN)
+
+
+def moments_begin(r):
+    r.moments[...] = jnp.zeros((STATE, 2 * W), F32)
 
 
 def through_row(got_ref, j):
@@ -287,23 +327,44 @@
         acc = through * acc + got_ref[at, :W]
 
 
-def scan_backward_kernel(got_ref, through_ref, out_ref):
+def scan_backward_kernel(got_ref, through_ref, loc_ref, sums_ref, e3_ref, out_ref):
     acc = jnp.zeros((ROWS, W), F32)
+    by_alog = jnp.zeros((ROWS, W), F32)
+    by_bias = jnp.zeros((ROWS, W), F32)
     for j in reversed(range(SEQ)):
         at = slice(ROWS * j, ROWS * (j + 1))
-        out_ref[at, :] = acc
-        acc = through_ref[j : j + 1, :] * acc + got_ref[at, :]
+        out_ref[at, :W] = acc
+        by_alog += acc * got_ref[at, W : 2 * W]
+        by_bias += acc * got_ref[at, 2 * W :]
+        acc = through_ref[j : j + 1, :] * acc + got_ref[at, :W]
+    row = lax.broadcasted_iota(jnp.int32, (H, W), 0)
+    vector = jnp.where(
+        row == 0,
+        jnp.sum(by_alog, axis=0, keepdims=True),
+        jnp.where(row == 1, jnp.sum(by_bias, axis=0, keepdims=True), 0.0),
+    )
+    heads = e3_ref[0:H, :]
+    far = sum(dot(heads, part, NT) for part in split3(vector))
+    lane = lax.broadcasted_iota(jnp.int32, (ROWS, 128), 1)
+    right = jnp.zeros((ROWS, 128), F32)
+    for k in range(2):
+        at = slice(ROWS * k, ROWS * (k + 1))
+        right = jnp.where(lane == SKIPS + k, loc_ref[at, 0:1], right)
+        right = jnp.where(lane == ALOGS + k, loc_ref[at, 1:2] + far[at, 0:1], right)
+        right = jnp.where(lane == BIASES + k, loc_ref[at, 2:3] + far[at, 1:2], right)
+    gains = sums_ref[0:1, :]
+    left = jnp.concatenate([gains[:, 128 * k : 128 * (k + 1)] for k in range(8)], 0)
+    for d in range(SEQ):
+        out_ref[ROWS * d : ROWS * (d + 1), W : W + 128] = left
+        out_ref[ROWS * d : ROWS * (d + 1), W + 128 :] = right
 
 
 def within_body(c, r):
     ex = expand(r.pk, DTBETA, r.e3)
     al = expand(r.pk, ALPHA, r.e3)
-    fin = expand(r.pk, TO_END, r.e3)
 
     def scale(at):
-        x = r.x[at, :].astype(F32)
-        r.hi[at, :], r.lo[at, :] = split2(x * ex[at, :])
-        r.xhi[at, :], r.xlo[at, :] = split2(x * fin[at, :])
+        r.hi[at, :], r.lo[at, :] = split2(r.x[at, :].astype(F32) * ex[at, :])
 
     each_rows(scale)
     b = r.bc[:, :STATE]
@@ -321,7 +382,7 @@
     r.shi[...], r.slo[...] = split2(r.sin[...])
     r.gain_acc[...] = jnp.zeros((8, W), F32)
     r.skip_acc[...] = jnp.zeros((8, W), F32)
-    r.back[...] = jnp.zeros((STATE, W), F32)
+    r.back[:, :W] = jnp.zeros((STATE, W), F32)
 
 
 def norm_body(c, r):
@@ -361,10 +422,12 @@
     each_rows(body)
     r.r[...] = dot2(r.e3[0:H, :], (r.rhi[...], r.rlo[...]), NT)
     new = dot2(cc, (r.hi[...], r.lo[...]), TN)
-    r.back[...] += new
+    r.back[:, :W] += new
 
 
 def norm_end(r):
+    r.back[:, W : 2 * W] = r.moments[:, :W] + r.thx[BY_ALOG : BY_ALOG + 1, :] * r.sin[...]
+    r.back[:, 2 * W :] = r.moments[:, W:] + r.thx[BY_BIAS : BY_BIAS + 1, :] * r.sin[...]
     r.sums[0:1, :] = jnp.sum(r.gain_acc[...], axis=0, keepdims=True)
     r.sums[1:2, :] = jnp.sum(r.skip_acc[...], axis=0, keepdims=True)
     r.sums[2:8, :] = jnp.zeros((6, W), F32)
@@ -394,6 +457,8 @@
 
     each_rows(finish)
     r.u[...] = dot2(r.e3[0:H, :], (r.rhi[...], r.rlo[...]), NT)
+    state = split2(kappa * (r.sloc[...] + r.thx[pl.ds(PRE + c, 1), :] * r.sin[...]))
+    r.gcs[...] = r.mw[...].astype(F32) * dot3_wide(gys, state)
     r.acc[...] = r.thx[pl.ds(THR + c, 1), :] * r.acc[...] + kappa * dot2(cc * r.mw[...], gys, TN)
 
 
@@ -412,22 +477,27 @@
     xs = (r.xhi[...], r.xlo[...])
     q = split2(dot3(gys, xs, NT) * r.mask[...].astype(F32))
     kappa = r.thx[pl.ds(KAP + c, 1), :]
-    state = split2(kappa * (r.sloc[...] + r.thx[pl.ds(PRE + c, 1), :] * r.sin[...]))
     dstate = split2(kappa * r.dloc[...])
     gb = joined(q, [cc, cc], TN) + r.me[...].astype(F32) * dot3_wide(xs, dstate)
-    gc = joined(q, [b, b], NN) + r.mw[...].astype(F32) * dot3_wide(gys, state)
-    r.gbc[:, :STATE] = gb
-    r.gbc[:, STATE:] = gc
+    r.gb[...] = gb
+    r.gc[...] = (r.gcs[...] + joined(q, [b, b], NN)).astype(BF16)
 
 
 def final_begin(r):
-    r.dhi[...], r.dlo[...] = split2(r.din[...])
+    r.dhi[...], r.dlo[...] = split2(r.din[:, :W])
 
 
 def final_bc_body(c, r):
-    gb = r.gbc[:, :STATE] + dot3_wide((r.xhi[...], r.xlo[...]), (r.dhi[...], r.dlo[...]))
+    gb = r.gb[...] + dot3_wide((r.xhi[...], r.xlo[...]), (r.dhi[...], r.dlo[...]))
     r.out[:, :STATE] = gb.astype(BF16)
-    r.out[:, STATE:] = r.gbc[:, STATE:].astype(BF16)
+    r.out[:, STATE:] = r.gc[...]
+
+
+def final_bc_end(r):
+    total = r.din[0:ROWS, W:]
+    for d in range(1, SEQ):
+        total += r.din[ROWS * d : ROWS * (d + 1), W:]
+    r.params[...] = total
 
 
 def final_x_body(c, r):
@@ -443,41 +513,67 @@
     r.uu[...] = r.u[...] + dot2(r.e3[0:H, :], (r.rhi[...], r.rlo[...]), NT)
 
 
-def final_x_end(r):
-    heads = r.e3[0:H, :]
-    state = r.pay[:, :W] + r.thx[TOTAL : TOTAL + 1, :] * r.sin[...]
-    ends = jnp.broadcast_to(jnp.sum(state * r.din[...], axis=0, keepdims=True), (H, W))
-    carry = sum(dot(heads, part, NT) for part in split3(ends))[:, 0:1]
+def time_sums(r, u_ref, carry, write):
     row = lax.broadcasted_iota(jnp.int32, (L, L), 0)
     col = lax.broadcasted_iota(jnp.int32, (L, L), 1)
     tri = (row >= col).astype(F32).astype(BF16)
     nega = -jnp.exp(r.par[:, 1:2])
-    alog_part = jnp.zeros((H, 1), F32)
-    bias_part = jnp.zeros((H, 1), F32)
     for c in reversed(range(C)):
         at = slice(c * L, (c + 1) * L)
-        u = r.uu[:, at]
+        u = u_ref[:, at]
         dt = r.rf[0:H, at]
         parts = dot(jnp.concatenate(split3(r.r[:, at] - u), 0), tri, NN)
         later = parts[0:H] + parts[H : 2 * H] + parts[2 * H : 3 * H]
         grad_rate = later + carry
         carry = carry + later[:, 0:1]
-        grad_dt = (u / dt + grad_rate * nega) * r.rf[H : 2 * H, at]
+        write(at, (u / dt + grad_rate * nega) * r.rf[H : 2 * H, at], grad_rate * dt * nega)
+
+
+def local_x_end(r):
+    sums = [jnp.zeros((H, 1), F32)] * 2
+
+    def write(at, grad_dt, grad_alog):
+        sums[0] += jnp.sum(grad_alog, axis=1, keepdims=True)
+        sums[1] += jnp.sum(grad_dt, axis=1, keepdims=True)
+
+    time_sums(r, r.u, jnp.zeros((H, 1), F32), write)
+    skips = jnp.broadcast_to(r.sums[1:2, :], (H, W))
+    skip_part = sum(dot(r.e3[0:H, :], part, NT) for part in split3(skips))[:, 0:1]
+    lane = lax.broadcasted_iota(jnp.int32, (H, 128), 1)
+    r.loc[...] = jnp.where(
+        lane == 0, skip_part, jnp.where(lane == 1, sums[0], jnp.where(lane == 2, sums[1], 0.0))
+    )
+
+
+def final_x_end(r):
+    state = r.pay[:, :W] + r.thx[TOTAL : TOTAL + 1, :] * r.sin[...]
+    ends = jnp.broadcast_to(jnp.sum(state * r.din[:, :W], axis=0, keepdims=True), (H, W))
+    carry = sum(dot(r.e3[0:H, :], part, NT) for part in split3(ends))[:, 0:1]
+
+    def write(at, grad_dt, grad_alog):
         r.gdt[:, at] = grad_dt
-        alog_part += jnp.sum(grad_rate * dt, axis=1, keepdims=True)
-        bias_part += jnp.sum(grad_dt, axis=1, keepdims=True)
-    skips = jnp.broadcast_to(r.sums[1:2, :], (H, W))
-    skip_part = sum(dot(heads, part, NT) for part in split3(skips))[:, 0:1]
-    lane = lax.broadcasted_iota(jnp.int32, (H, 128), 1)
-    right = jnp.where(
-        lane == 0, skip_part, jnp.where(lane == 1, alog_part * nega, jnp.where(lane == 2, bias_part, 0.0))
-    )
-    gains = r.sums[0:1, :]
-    left = jnp.concatenate([gains[:, 128 * k : 128 * (k + 1)] for k in range(8)], 0)
-    left = jnp.concatenate([left, jnp.zeros((8, 128), F32)], 0)
-    for d in range(SEQ):
-        r.params[H * d : H * (d + 1), :128] = left
-        r.params[H * d : H * (d + 1), 128:] = right
+
+    time_sums(r, r.uu, carry, write)
+
+
+def pack_kernel(b_ref, c_ref, out_ref):
+    for g in range(GRP):
+        at = slice(STATE * g, STATE * (g + 1))
+        out_ref[g, :, :STATE] = b_ref[:, at]
+        out_ref[g, :, STATE:] = c_ref[:, at]
+
+
+def unpack_kernel(in_ref, b_ref, c_ref, sems):
+    copies = []
+    for g in range(GRP):
+        at = slice(STATE * g, STATE * (g + 1))
+        for k, ref in enumerate((b_ref, c_ref)):
+            source = in_ref.at[g, :, STATE * k : STATE * (k + 1)]
+            copies.append(pltpu.make_async_copy(source, ref.at[:, at], sems.at[k, g]))
+    for copy in copies:
+        copy.start()
+    for copy in copies:
+        copy.wait()
 
 
 def head_matrix():
@@ -494,16 +590,20 @@
         jnp.stack([norm_weight, jnp.repeat(skip, HEAD_DIM)], 0), ((0, 6), (0, 0))
     )
     starts = doc_starts.reshape(1, T)
-    mine = jnp.concatenate(
-        [b_proj.reshape(128, GRP, STATE), c_proj.reshape(128, GRP, STATE)], 2
-    ).transpose(1, 0, 2)
+    far = pl.BlockSpec(memory_space=pl.ANY)
+    mine = pl.pallas_call(
+        pack_kernel,
+        out_shape=pltpu.HBM((GRP, 128, 2 * STATE), BF16),
+        compiler_params=pltpu.CompilerParams(vmem_limit_bytes=VMEM_LIMIT),
+        name="pack",
+    )(*[pltpu.with_memory_space_constraint(a, pltpu.HBM) for a in (b_proj, c_proj)])
     bc = lax.all_to_all(mine, "head", split_axis=0, concat_axis=0, tiled=True).reshape(T, 2 * STATE)
 
     sds = pltpu.HBM
     pk, rf, mask, me, mw, thx = pl.pallas_call(
         prep_kernel,
         out_shape=(
-            sds((8 * H, T), BF16),
+            sds((12 * H, T), BF16),
             sds((2 * H, T), F32),
             sds((T, L), BF16),
             sds((T, 128), BF16),
@@ -521,11 +621,20 @@
     x = {"x": (x_in, "tok")}
     masks = {"mask": (mask, "tok"), "me": (me, "tok"), "mw": (mw, "tok")}
 
+    xhi, xlo = staged(
+        scale_body,
+        {"e3": (e3, "all"), "pk": (pk, "row")} | x,
+        {"xhi": ((T, W), BF16, "tok"), "xlo": ((T, W), BF16, "tok")},
+        {},
+        "scale",
+        unit,
+    )
+    xhi, xlo, bc = lax.optimization_barrier((xhi, xlo, bc))
     pay, bc = staged(
         states_body,
-        common | {"bc": (bc, "near_tok")} | x,
+        {"thx": (thx, "all"), "bc": (bc, "near_tok"), "xhi": (xhi, "tok"), "xlo": (xlo, "tok")},
         {"pay": ((STATE, W + 128), F32, "all"), "bc_copy": ((T, 2 * STATE), BF16, "copy")},
-        {"acc": state, "hi": half, "lo": half},
+        {"acc": state},
         "states",
         2 * unit,
         begin=clear,
@@ -549,25 +658,34 @@
 
     bcs = {"bc": (bc, "tok")}
     got = exchange(pay)
-    ys, sloc, xhi, xlo = staged(
+    ys, sloc = staged(
         within_body,
         common | bcs | masks | x,
         {
             "ys": ((T, W), F32, "tok"),
             "sloc": ((C, STATE, W), F32, "state"),
-            "xhi": ((T, W), BF16, "tok"),
-            "xlo": ((T, W), BF16, "tok"),
         },
         {"acc": state, "hi": half, "lo": half},
         "within",
         7 * unit,
         begin=clear,
     )
-    (ys, sloc, xhi, xlo), got = lax.optimization_barrier(((ys, sloc, xhi, xlo), got))
+    ys, sloc, got = lax.optimization_barrier((ys, sloc, got))
     before, through = scan(
         scan_forward_kernel, "scan_forward", (sds((STATE, W), F32), sds((SEQ, W), F32)), got
     )
     sin = exchange(before)
+    tied, _ = lax.optimization_barrier((x_in, got))
+    (moments,) = staged(
+        moments_body,
+        {"e3": (e3, "all"), "pk": (pk, "row")} | bcs | {"x": (tied, "tok")},
+        {"moments": ((STATE, 2 * W), F32, "all")},
+        {"hi": half, "lo": half, "hi2": half, "lo2": half},
+        "moments",
+        4 * unit,
+        begin=moments_begin,
+    )
+    moments, sin = lax.optimization_barrier((moments, sin))
 
     gy, gz, r, back, sums, sin = staged(
         norm_body,
@@ -575,12 +693,13 @@
         | {"vec": (vec, "all"), "sin": (sin, "near")}
         | bcs
         | {"ys": (ys, "tok"), "z": (z_gate, "tok"), "go": (grad_out, "tok")}
-        | x,
+        | x
+        | {"moments": (moments, "late")},
         {
             "gy": ((T, W), F32, "tok"),
             "gz": ((T, W), BF16, "tok"),
             "r": ((H, T), F32, "row"),
-            "back": ((STATE, W), F32, "all"),
+            "back": ((STATE, 3 * W), F32, "all"),
             "sums": ((8, W), F32, "all"),
             "sin_copy": ((STATE, W), F32, "copy"),
         },
@@ -601,52 +720,79 @@
     )
 
     got_back = exchange(back)
-    gx, u, dloc = staged(
+    gx, u, dloc, gcs, loc = staged(
         local_x_body,
-        common | {"vec": (vec, "all")} | bcs | masks | {"gy": (gy, "tok")} | x,
+        common
+        | {
+            "vec": (vec, "all"),
+            "sin": (sin, "all"),
+            "par": (par, "all"),
+            "sums": (sums, "all"),
+            "rf": (rf, "row"),
+            "r": (r, "row"),
+        }
+        | bcs
+        | masks
+        | {"gy": (gy, "tok"), "sloc": (sloc, "state")}
+        | x,
         {
             "gx": ((T, W), F32, "tok"),
             "u": ((H, T), F32, "row"),
             "dloc": ((C, STATE, W), F32, "state"),
+            "gcs": ((T, STATE), F32, "tok"),
+            "loc": ((H, 128), F32, "all"),
         },
         {"acc": state, "ghi": half, "glo": half, "rhi": half, "rlo": half},
         "local_x",
         7 * unit,
         backward=True,
         begin=clear,
+        end=local_x_end,
     )
     dloc, got_back = lax.optimization_barrier((dloc, got_back))
-    behind = scan(scan_backward_kernel, "scan_backward", sds((STATE, W), F32), got_back, through)
+    behind = scan(
+        scan_backward_kernel, "scan_backward", sds((STATE, W + 256), F32), got_back, through, loc, sums, e3
+    )
     din = exchange(behind)
-    (gbc,) = staged(
+    gb, gc = staged(
         local_bc_body,
         common
-        | {"sin": (sin, "all")}
         | bcs
         | masks
-        | {"gy": (gy, "tok"), "sloc": (sloc, "state"), "dloc": (dloc, "state")}
+        | {"gy": (gy, "tok"), "dloc": (dloc, "state"), "gcs": (gcs, "tok")}
         | x,
-        {"gbc": ((T, 2 * STATE), F32, "tok")},
+        {"gb": ((T, STATE), F32, "tok"), "gc": ((T, STATE), BF16, "tok")},
         {"ghi": half, "glo": half, "xhi": half, "xlo": half},
         "local_bc",
-        7 * unit,
-    )
-
-    gbc, din = lax.optimization_barrier((gbc, din))
-    gbc, din = staged(
+        5 * unit,
+    )
+
+    gb, din = lax.optimization_barrier((gb, din))
+    gbc, din, params = staged(
         final_bc_body,
-        {"din": (din, "near"), "gbc": (gbc, "tok"), "xhi": (xhi, "tok"), "xlo": (xlo, "tok")},
-        {"out": ((T, 2 * STATE), BF16, "tok"), "din_copy": ((STATE, W), F32, "copy")},
+        {
+            "din": (din, "near"),
+            "gb": (gb, "tok"),
+            "gc": (gc, "tok"),
+            "xhi": (xhi, "tok"),
+            "xlo": (xlo, "tok"),
+        },
+        {
+            "out": ((T, 2 * STATE), BF16, "tok"),
+            "din_copy": ((STATE, W + 256), F32, "copy"),
+            "params": ((ROWS, 256), F32, "all"),
+        },
         {"dhi": ((STATE, W), BF16), "dlo": ((STATE, W), BF16)},
         "final_bc",
         2 * unit,
         begin=final_begin,
+        end=final_bc_end,
     )
     gbc, gx = lax.optimization_barrier((gbc, gx))
     back_bc = lax.all_to_all(
         gbc.reshape(GRP, 128, 2 * STATE), "head", split_axis=0, concat_axis=0, tiled=True
     )
-    grad_x, grad_dt, params = staged(
+    grad_x, grad_dt = staged(
         final_x_body,
         common
         | {
@@ -654,7 +800,6 @@
             "sin": (sin, "all"),
             "pay": (pay, "all"),
             "par": (par, "all"),
-            "sums": (sums, "all"),
             "rf": (rf, "row"),
             "r": (r, "row"),
             "u": (u, "row"),
@@ -662,11 +807,7 @@
         | bcs
         | {"gx": (gx, "tok")}
         | x,
-        {
-            "gxo": ((T, W), BF16, "tok"),
-            "gdt": ((H, T), F32, "row"),
-            "params": ((SEQ * H, 256), F32, "all"),
-        },
+        {"gxo": ((T, W), BF16, "tok"), "gdt": ((H, T), F32, "row")},
         {
             "uu": ((H, T), F32),
             "dhi": ((STATE, W), BF16),
@@ -679,12 +820,21 @@
         begin=final_begin,
         end=final_x_end,
     )
-    params, back_bc = lax.optimization_barrier((params, back_bc))
-    grad_b = back_bc[:, :, :STATE].transpose(1, 0, 2).reshape(128, GRP * STATE)
-    grad_c = back_bc[:, :, STATE:].transpose(1, 0, 2).reshape(128, GRP * STATE)
-    summed = jnp.sum(exchange(params).reshape(SEQ, H, 256), axis=0)
-    grad_gain = summed[:8, :128].reshape(W)
-    grad_skip, grad_alog, grad_bias = summed[:, 128], summed[:, 129], summed[:, 130]
+    grad_b, grad_c = pl.pallas_call(
+        unpack_kernel,
+        out_shape=(pltpu.HBM((128, GRP * STATE), BF16), pltpu.HBM((128, GRP * STATE), BF16)),
+        in_specs=[pl.BlockSpec(memory_space=pltpu.VMEM)],
+        out_specs=(far, far),
+        scratch_shapes=[pltpu.SemaphoreType.DMA((2, GRP))],
+        compiler_params=pltpu.CompilerParams(vmem_limit_bytes=16 * 2**20),
+        name="unpack",
+    )(pltpu.with_memory_space_constraint(back_bc, pltpu.VMEM))
+    grad_gain = params[:, :128].reshape(W)
+
+    def by_head(at):
+        return params[:, 128 + at : 130 + at].T.reshape(H)
+
+    grad_skip, grad_alog, grad_bias = by_head(SKIPS), by_head(ALOGS), by_head(BIASES)
     return (grad_x, gz, grad_b, grad_c, grad_dt, grad_alog, grad_bias, grad_skip, grad_gain)
 
 

time: 140 us -> 133 us (0.950)
  Pallas kernels: 65 us -> 77.7 us
  starting transfers between devices: 39.9 us -> 29.2 us
  waiting for transfers between devices: 25.1 us -> 18.4 us
  local copies, waits for them, and re-layouts: 5.81 us -> 4.35 us
    all_to_all x5 -> x4, starting transfers between devices: 30.1 us -> 19.4 us  [exchange(): return lax.all_to_all(v, 'seq', split_axis=0, concat_axis=0, tiled=True)]
    pallas_call x7 -> x9, Pallas kernels: 59 us -> 68.2 us  [staged(): pl.pallas_call(kernel, out_shape=tuple((pltpu.HBM(s, d) for s, d, _ in ou...]
    all_to_all x1, waiting for transfers between devices: 4.72 us -> 0.82 us  [shard_body(): lax.all_to_all(mine, 'head', split_axis=0, concat_axis=0, tiled=True)]
    pallas_call x1 -> x3, Pallas kernels: 3.47 us -> 6.34 us  [the longest x1 3.5 us: shard_body(): pl.pallas_call(prep_kernel, out_shape=(sds((12 * H, T), BF16), sds((2 * H...]
    all_to_all x5 -> x4, waiting for transfers between devices: 19.7 us -> 17.5 us  [exchange(): return lax.all_to_all(v, 'seq', split_axis=0, concat_axis=0, tiled=True)]
  transfers between devices with their start and end apart: 7 -> 6, of which waited for: 5 -> 5; matrix products, arithmetic and copies ran while one was open for 2% -> 4% of each run, Pallas kernels for 30% -> 39%
where the time goes in v4:
time: 133 us; the launch traced here: 131 us
  Pallas kernels  77.7 us (58%)
  starting transfers between devices  29.2 us (22%)
  waiting for transfers between devices  18.4 us (14%)
  local copies, waits for them, and re-layouts  4.35 us (3%)
    pallas_call x9, Pallas kernels, staged(): pl.pallas_call(kernel, out_shape=tuple((pltpu.HBM(s, d) for s, d, _ in ou...  68.2 us
    all_to_all x4, starting transfers between devices, exchange(): return lax.all_to_all(v, 'seq', split_axis=0, concat_axis=0, tiled=True)  19.4 us
    all_to_all x4, waiting for transfers between devices, exchange(): return lax.all_to_all(v, 'seq', split_axis=0, concat_axis=0, tiled=True)  17.5 us
    all_to_all x1, starting transfers between devices, shard_body(): lax.all_to_all(mine, 'head', split_axis=0, concat_axis=0, tiled=True)  4.92 us
    all_to_all x1, starting transfers between devices, shard_body(): lax.all_to_all(gbc.reshape(GRP, 128, 2 * STATE), 'head', split_axis=0, co...  4.88 us
    pallas_call x1, Pallas kernels, shard_body(): pl.pallas_call(prep_kernel, out_shape=(sds((12 * H, T), BF16), sds((2 * H...  3.5 us
    pallas_call x2, Pallas kernels, scan(): pl.pallas_call(kernel, out_shape=outs, in_specs=[pl.BlockSpec(memory_spac...  3.17 us
  transfers between devices with their start and end apart: 6, of which 5 were waited for; matrix products, arithmetic and copies ran while one was open for 4% of the time, Pallas kernels for 39%

profile of v4, /device:TPU:8, one launch (start us, length us, event | category | flops | bytes accessed | tf_op | source)
XLA Modules:
  0.0 131.2 jit_solution(14459824197705799537)
XLA Ops:
  0.7 1.9 %pack.1 = bf16[8,128,256]{2,1,0:T(8,128)(2,1)} custom-call(bf16[128,1024]{1,0:T(8,128)(2,1)} %b_ref.1, bf16[128,1024]{1,0:T(8,128)(2,1)} %c_ref.1), custom_call_target="tpu_custom_call" | custom-call | tf_op jit(solution)/shard_map/pack/pallas_call | solution.py:594
  2.6 4.9 %all-to-all-start = ((bf16[8,128,256]{2,1,0:T(8,128)(2,1)}), bf16[8,128,256]{2,1,0:T(8,128)(2,1)S(1)}, u32[]{:S(2)}, u32[]{:S(2)}) async-start(bf16[8,128,256]{2,1,0:T(8,128)(2,1)} %pack.1), calls=%async_computation | async-start | bytes 1048576 | tf_op jit(solution)/shard_map/all_to_all | solution.py:600
  7.6 0.6 pad.8.par_ref.refs_5_.refs_6_
  8.2 3.5 %prep.1 = (bf16[192,1024]{1,0:T(8,128)(2,1)}, f32[32,1024]{1,0:T(8,128)}, bf16[1024,256]{1,0:T(8,128)(2,1)}, bf16[1024,128]{1,0:T(8,128)(2,1)}, bf16[1024,128]{1,0:T(8,128)(2,1)}, /*index=5*/f32[16,1024]{1,0:T(8,128)}) custom-call(f32[16,1024]{1,0:T(8,128)} %dt_ref.1, f32[16,128]{1,0:T(8,128)} %pad.8.par_ref.refs_5_.refs_6_, s32[1,1024]{1,0:T(1,128)} %bitcast.32, ...), custom_call_target="tpu_custom_call" | custom-call | tf_op jit(solution)/shard_map/prep/pallas_call | solution.py:603
  11.7 3.9 %scale.1 = (bf16[1024,1024]{1,0:T(8,128)(2,1)}, bf16[1024,1024]{1,0:T(8,128)(2,1)}) custom-call(bf16[48,1024]{1,0:T(8,128)(2,1)} %constant.5.clone.e3_ref.refs_0_, bf16[192,1024]{1,0:T(8,128)(2,1)} %get-tuple-element.58.refs_1_, bf16[1024,1024]{1,0:T(8,128)(2,1)} %refs_12_.1), custom_call_target="tpu_custom_call" | custom-call | flops 536870912 | bytes 8388608 | tf_op jit(solution)/shard_map/scale/pallas_call | solution.py:173
  15.6 0.8 all-to-all-done
  16.4 3.8 %states.1 = (f32[128,1152]{1,0:T(8,128)}, bf16[1024,256]{1,0:T(8,128)(2,1)}) custom-call(f32[16,1024]{1,0:T(8,128)} %get-tuple-element.59.refs_0_.refs_2_, bf16[1024,256]{1,0:T(8,128)(2,1)S(1)} %bitcast.25, bf16[1024,1024]{1,0:T(8,128)(2,1)} %get-tuple-element.63.refs_2_.refs_3_, bf16[1024,1024]{1,0:T(8,128)(2,1)} %get-tuple-element.64.refs_3_.refs_4_), custom_call_target="tpu_custom_call" | custom-call | flops 1073741824 | bytes 8388608 | tf_op jit(solution)/shard_map/states/pallas_call | solution.py:173
  20.2 7.9 %all-to-all-start.1 = ((f32[16,8,1152]{2,1,0:T(8,128)}), f32[16,8,1152]{2,1,0:T(8,128)S(1)}, u32[]{:S(2)}, u32[]{:S(2)}) async-start(f32[16,8,1152]{2,1,0:T(8,128)} %bitcast.28), calls=%async_computation.1 | async-start | bytes 1179648 | tf_op jit(solution)/shard_map/all_to_all | solution.py:657
  28.2 8.0 %within.1 = (f32[1024,1024]{1,0:T(8,128)}, f32[4,128,1024]{2,1,0:T(8,128)}) custom-call(bf16[48,1024]{1,0:T(8,128)(2,1)} %constant.5.clone.e3_ref.refs_0_, bf16[192,1024]{1,0:T(8,128)(2,1)} %get-tuple-element.58.refs_1_, f32[16,1024]{1,0:T(8,128)} %get-tuple-element.59.refs_0_.refs_2_, ...), custom_call_target="tpu_custom_call" | custom-call | flops 3758096384 | bytes 8388608 | tf_op jit(solution)/shard_map/within/pallas_call | solution.py:173
  36.2 3.7 %all-to-all-done.1 = f32[16,8,1152]{2,1,0:T(8,128)S(1)} async-done(((f32[16,8,1152]{2,1,0:T(8,128)}), f32[16,8,1152]{2,1,0:T(8,128)S(1)}, u32[]{:S(2)}, u32[]{:S(2)}) %all-to-all-start.1) | async-done | bytes 589856 | tf_op jit(solution)/shard_map/all_to_all | solution.py:657
  39.8 0.9 scan_forward.1
  40.7 3.8 %all-to-all-start.2 = ((f32[16,8,1024]{2,1,0:T(8,128)}), f32[16,8,1024]{2,1,0:T(8,128)S(1)}, u32[]{:S(2)}, u32[]{:S(2)}) async-start(f32[16,8,1024]{2,1,0:T(8,128)} %bitcast.31), calls=%async_computation.2 | async-start | bytes 1048576 | tf_op jit(solution)/shard_map/all_to_all | solution.py:657
  44.7 0.6 select_maximum_fusion.refs_3_
  45.3 5.8 %moments.1.refs_10_ = f32[128,2048]{1,0:T(8,128)} custom-call(bf16[48,1024]{1,0:T(8,128)(2,1)} %constant.5.clone.e3_ref.refs_0_, bf16[192,1024]{1,0:T(8,128)(2,1)} %get-tuple-element.58.refs_1_, bf16[1024,256]{1,0:T(8,128)(2,1)} %get-tuple-element.65.refs_3_.refs_2_.refs_5_.refs_9_.refs_10_, bf16[1024,1024]{1,0:T(8,128)(2,1)} %refs_12_.1), custom_call_target="tpu_custom_call" | custom-call | flops 2147483648 | bytes 8388608 | tf_op jit(solution)/shard_map/moments/pallas_call | solution.py:173
  51.1 3.9 %all-to-all-done.2 = f32[16,8,1024]{2,1,0:T(8,128)S(1)} async-done(((f32[16,8,1024]{2,1,0:T(8,128)}), f32[16,8,1024]{2,1,0:T(8,128)S(1)}, u32[]{:S(2)}, u32[]{:S(2)}) %all-to-all-start.2) | async-done | bytes 524320 | tf_op jit(solution)/shard_map/all_to_all | solution.py:657
  55.0 12.0 %norm.1 = (f32[1024,1024]{1,0:T(8,128)}, bf16[1024,1024]{1,0:T(8,128)(2,1)}, f32[16,1024]{1,0:T(8,128)}, f32[128,3072]{1,0:T(8,128)}, f32[8,1024]{1,0:T(8,128)}, /*index=5*/f32[128,1024]{1,0:T(8,128)}) custom-call(bf16[48,1024]{1,0:T(8,128)(2,1)} %constant.5.clone.e3_ref.refs_0_, bf16[192,1024]{1,0:T(8,128)(2,1)} %get-tuple-element.58.refs_1_, ...), custom_call_target="tpu_custom_call" | custom-call | flops 3221225472 | bytes 8388608 | tf_op jit(solution)/shard_map/norm/pallas_call | solution.py:173
  67.0 3.7 %all-to-all-start.3 = ((f32[16,8,3072]{2,1,0:T(8,128)}), f32[16,8,3072]{2,1,0:T(8,128)S(1)}, u32[]{:S(2)}, u32[]{:S(2)}) async-start(f32[16,8,3072]{2,1,0:T(8,128)} %bitcast.29), calls=%async_computation.3 | async-start | bytes 3145728 | tf_op jit(solution)/shard_map/all_to_all | solution.py:657
  70.8 12.3 %local_x.1 = (f32[1024,1024]{1,0:T(8,128)}, f32[16,1024]{1,0:T(8,128)}, f32[4,128,1024]{2,1,0:T(8,128)}, f32[1024,128]{1,0:T(8,128)}, f32[16,128]{1,0:T(8,128)}) custom-call(bf16[48,1024]{1,0:T(8,128)(2,1)} %constant.5.clone.e3_ref.refs_0_, bf16[192,1024]{1,0:T(8,128)(2,1)} %get-tuple-element.58.refs_1_, f32[16,1024]{1,0:T(8,128)} %get-tuple-element.59.refs_0_.refs_2_, ...), custom_call_target="tpu_custom_call" | custom-call | flops 3758096384 | bytes 8388608 | tf_op jit(solution)/shard_map/local_x/pallas_call | solution.py:173
  83.0 9.1 %all-to-all-done.3 = f32[16,8,3072]{2,1,0:T(8,128)S(1)} async-done(((f32[16,8,3072]{2,1,0:T(8,128)}), f32[16,8,3072]{2,1,0:T(8,128)S(1)}, u32[]{:S(2)}, u32[]{:S(2)}) %all-to-all-start.3) | async-done | bytes 1572896 | tf_op jit(solution)/shard_map/all_to_all | solution.py:657
  92.1 2.3 %scan_backward.1 = f32[128,1280]{1,0:T(8,128)} custom-call(f32[128,3072]{1,0:T(8,128)S(1)} %bitcast.22, f32[16,1024]{1,0:T(8,128)} %get-tuple-element.90.through_ref, f32[16,128]{1,0:T(8,128)} %get-tuple-element.91.loc_ref, f32[8,1024]{1,0:T(8,128)} %get-tuple-element.80.refs_6_.sums_ref, bf16[48,1024]{1,0:T(8,128)(2,1)} %constant.5.clone.e3_ref.refs_0_), custom_call_target="tpu_custom_call" | custom-call | tf_op jit(solution)/shard_map/scan_backward/pallas_call | solution.py:645
  94.4 4.0 %all-to-all-start.4 = ((f32[16,8,1280]{2,1,0:T(8,128)}), f32[16,8,1280]{2,1,0:T(8,128)S(1)}, u32[]{:S(2)}, u32[]{:S(2)}) async-start(f32[16,8,1280]{2,1,0:T(8,128)} %bitcast.27), calls=%async_computation.4 | async-start | bytes 1310720 | tf_op jit(solution)/shard_map/all_to_all | solution.py:657
  98.5 9.9 %local_bc.1 = (f32[1024,128]{1,0:T(8,128)}, bf16[1024,128]{1,0:T(8,128)(2,1)}) custom-call(bf16[48,1024]{1,0:T(8,128)(2,1)} %constant.5.clone.e3_ref.refs_0_, bf16[192,1024]{1,0:T(8,128)(2,1)} %get-tuple-element.58.refs_1_, f32[16,1024]{1,0:T(8,128)} %get-tuple-element.59.refs_0_.refs_2_, ...), custom_call_target="tpu_custom_call" | custom-call | flops 2684354560 | bytes 8388608 | tf_op jit(solution)/shard_map/local_bc/pallas_call | solution.py:173
  108.4 0.9 all-to-all-done.4
  109.3 4.4 %final_bc.1 = (bf16[1024,256]{1,0:T(8,128)(2,1)}, f32[128,1280]{1,0:T(8,128)}, f32[8,256]{1,0:T(8,128)}) custom-call(f32[128,1280]{1,0:T(8,128)S(1)} %bitcast.23, f32[1024,128]{1,0:T(8,128)} %get-tuple-element.93.refs_1_, bf16[1024,128]{1,0:T(8,128)(2,1)} %get-tuple-element.94.refs_2_, bf16[1024,1024]{1,0:T(8,128)(2,1)} %get-tuple-element.63.refs_2_.refs_3_, ...), custom_call_target="tpu_custom_call" | custom-call | flops 1073741824 | bytes 8388608 | tf_op jit(solution)/shard_map/final_bc/pallas_call | solution.py:173
  113.6 4.9 %all-to-all-start.5 = ((bf16[8,128,256]{2,1,0:T(8,128)(2,1)}), bf16[8,128,256]{2,1,0:T(8,128)(2,1)S(1)}, u32[]{:S(2)}, u32[]{:S(2)}) async-start(bf16[8,128,256]{2,1,0:T(8,128)(2,1)} %bitcast.30), calls=%async_computation.5 | async-start | bytes 1048576 | tf_op jit(solution)/shard_map/all_to_all | solution.py:792
  118.5 0.9 slice_bitcast_fusion.1
  119.5 0.6 reshape.52
  120.1 0.6 reshape.51
  120.8 0.6 reshape.50
  121.4 8.1 %final_x.1 = (bf16[1024,1024]{1,0:T(8,128)(2,1)}, f32[16,1024]{1,0:T(8,128)}) custom-call(bf16[48,1024]{1,0:T(8,128)(2,1)} %constant.5.clone.e3_ref.refs_0_, bf16[192,1024]{1,0:T(8,128)(2,1)} %get-tuple-element.58.refs_1_, f32[16,1024]{1,0:T(8,128)} %get-tuple-element.59.refs_0_.refs_2_, f32[128,1280]{1,0:T(8,128)} %get-tuple-element.95.refs_3_, ...), custom_call_target="tpu_custom_call" | custom-call | flops 1610612736 | bytes 8388608 | tf_op jit(solution)/shard_map/final_x/pallas_call | solution.py:173
  129.5 0.6 slice_bitcast_fusion
  130.1 0.9 unpack.1
  (18 shorter events, 0.5 us)
Async XLA Ops:
  0.6 6.9 %copy-start.3 = (f32[16]{0:T(128)S(1)}, f32[16]{0:T(128)}, u32[]{:S(2)}) copy-start(f32[16]{0:T(128)} %param.18) | copy-start | bytes 196
  0.7 6.9 %copy-start.4 = (f32[16]{0:T(128)S(1)}, f32[16]{0:T(128)}, u32[]{:S(2)}) copy-start(f32[16]{0:T(128)} %param.17) | copy-start | bytes 196
  2.6 13.8 %all-to-all-start = ((bf16[8,128,256]{2,1,0:T(8,128)(2,1)}), bf16[8,128,256]{2,1,0:T(8,128)(2,1)S(1)}, u32[]{:S(2)}, u32[]{:S(2)}) async-start(bf16[8,128,256]{2,1,0:T(8,128)(2,1)} %pack.1), calls=%async_computation | async-start | bytes 1048576 | tf_op jit(solution)/shard_map/all_to_all | solution.py:600
  20.2 19.6 %all-to-all-start.1 = ((f32[16,8,1152]{2,1,0:T(8,128)}), f32[16,8,1152]{2,1,0:T(8,128)S(1)}, u32[]{:S(2)}, u32[]{:S(2)}) async-start(f32[16,8,1152]{2,1,0:T(8,128)} %bitcast.28), calls=%async_computation.1 | async-start | bytes 1179648 | tf_op jit(solution)/shard_map/all_to_all | solution.py:657
  28.1 16.4 %copy-start.2 = (f32[16]{0:T(128)S(1)}, f32[16]{0:T(128)}, u32[]{:S(2)}) copy-start(f32[16]{0:T(128)} %param.19) | copy-start | bytes 196
  28.1 16.5 %copy-start.1 = (f32[1024]{0:T(1024)S(1)}, f32[1024]{0:T(1024)}, u32[]{:S(2)}) copy-start(f32[1024]{0:T(1024)} %param.20) | copy-start | bytes 12292
  40.7 14.3 %all-to-all-start.2 = ((f32[16,8,1024]{2,1,0:T(8,128)}), f32[16,8,1024]{2,1,0:T(8,128)S(1)}, u32[]{:S(2)}, u32[]{:S(2)}) async-start(f32[16,8,1024]{2,1,0:T(8,128)} %bitcast.31), calls=%async_computation.2 | async-start | bytes 1048576 | tf_op jit(solution)/shard_map/all_to_all | solution.py:657
  67.0 25.1 %all-to-all-start.3 = ((f32[16,8,3072]{2,1,0:T(8,128)}), f32[16,8,3072]{2,1,0:T(8,128)S(1)}, u32[]{:S(2)}, u32[]{:S(2)}) async-start(f32[16,8,3072]{2,1,0:T(8,128)} %bitcast.29), calls=%async_computation.3 | async-start | bytes 3145728 | tf_op jit(solution)/shard_map/all_to_all | solution.py:657
  94.4 14.8 %all-to-all-start.4 = ((f32[16,8,1280]{2,1,0:T(8,128)}), f32[16,8,1280]{2,1,0:T(8,128)S(1)}, u32[]{:S(2)}, u32[]{:S(2)}) async-start(f32[16,8,1280]{2,1,0:T(8,128)} %bitcast.27), calls=%async_computation.4 | async-start | bytes 1310720 | tf_op jit(solution)/shard_map/all_to_all | solution.py:657
  113.6 16.5 %all-to-all-start.5 = ((bf16[8,128,256]{2,1,0:T(8,128)(2,1)}), bf16[8,128,256]{2,1,0:T(8,128)(2,1)S(1)}, u32[]{:S(2)}, u32[]{:S(2)}) async-start(bf16[8,128,256]{2,1,0:T(8,128)(2,1)} %bitcast.30), calls=%async_computation.5 | async-start | bytes 1048576 | tf_op jit(solution)/shard_map/all_to_all | solution.py:792
  121.4 8.1 %copy-start = (f32[8,256]{1,0:T(8,128)S(1)}, f32[8,256]{1,0:T(8,128)}, u32[]{:S(2)}) copy-start(f32[8,256]{1,0:T(8,128)} %get-tuple-element.106) | copy-start | bytes 24580

commit v5 on v4

--- a/solution.py
+++ b/solution.py
@@ -26,7 +26,7 @@
 VMEM_LIMIT = 60 * 2**20
 VMEM_NEAR = 48 * 2**20
 
-THR, KAP, PRE, TOTAL, BY_ALOG, BY_BIAS, TABLE = 0, 4, 8, 12, 13, 14, 16
+THR, KAP, PRE, TOTAL, BY_ALOG, BY_BIAS, BASE, TABLE = 0, 4, 8, 12, 13, 14, 15, 16
 ALPHA, DTBETA, TO_END, FROM_START, END_ALOG, END_BIAS = 0, 1, 2, 3, 4, 5
 SKIPS, ALOGS, BIASES = 0, 2, 4
 
@@ -249,6 +249,7 @@
         put(FROM_START, slice(c * L, (c + 1) * L), enter[c] * passed)
         passed = passed * thr[c]
     columns = [*thr, *kap, *before, passed, passed * sum(rate_sum), passed * nega * sum(sig_sum)]
+    columns.append(jax.nn.sigmoid(bias) / jax.nn.softplus(bias))
     passed = jnp.ones((H, 1), F32)
     rate_after = jnp.zeros((H, 1), F32)
     sig_after = jnp.zeros((H, 1), F32)
@@ -312,12 +313,16 @@
     r.moments[...] = jnp.zeros((STATE, 2 * W), F32)
 
 
+def log_base(through):
+    return jnp.where(through > 1e-30, 0.5 * jnp.log(jnp.maximum(through, 1e-30)), 0.0)
+
+
 def through_row(got_ref, j):
     block = got_ref[ROWS * j : ROWS * (j + 1), W:]
     return jnp.concatenate([block[k : k + 1, :] for k in range(ROWS)], 1)
 
 
-def scan_forward_kernel(got_ref, out_ref, through_ref):
+def scan_forward_kernel(got_ref, out_ref, after_ref, through_ref):
     acc = jnp.zeros((ROWS, W), F32)
     for j in range(SEQ):
         at = slice(ROWS * j, ROWS * (j + 1))
@@ -325,18 +330,29 @@
         through = through_row(got_ref, j)
         through_ref[j : j + 1, :] = through
         acc = through * acc + got_ref[at, :W]
-
-
-def scan_backward_kernel(got_ref, through_ref, loc_ref, sums_ref, e3_ref, out_ref):
+        after_ref[at, :] = acc
+
+
+def scan_backward_kernel(got_ref, through_ref, after_ref, loc_ref, sums_ref, e3_ref, thx_ref, out_ref):
     acc = jnp.zeros((ROWS, W), F32)
     by_alog = jnp.zeros((ROWS, W), F32)
     by_bias = jnp.zeros((ROWS, W), F32)
     for j in reversed(range(SEQ)):
         at = slice(ROWS * j, ROWS * (j + 1))
         out_ref[at, :W] = acc
-        by_alog += acc * got_ref[at, W : 2 * W]
-        by_bias += acc * got_ref[at, 2 * W :]
-        acc = through_ref[j : j + 1, :] * acc + got_ref[at, :W]
+        block = got_ref[2 * ROWS * j : 2 * ROWS * (j + 1), :].astype(F32)
+        through = through_ref[j : j + 1, :]
+        state = after_ref[at, :]
+        rests = block[:ROWS, W:] + 256.0
+        back_rest = jnp.floor(rests * (1.0 / 16))
+        rests = rests - 16.0 * back_rest
+        alog_rest = jnp.floor(rests * 0.25)
+        bias_rest = rests - 4.0 * alog_rest
+        base = log_base(through)
+        bias_base = thx_ref[BASE : BASE + 1, :] * (1.0 + base)
+        by_alog += acc * (with_rest(block[ROWS:, :W], alog_rest, 4) + base * state)
+        by_bias += acc * (with_rest(block[ROWS:, W:], bias_rest, 4) + bias_base * state)
+        acc = through * acc + with_rest(block[:ROWS, :W], back_rest, 32)
     row = lax.broadcasted_iota(jnp.int32, (H, W), 0)
     vector = jnp.where(
         row == 0,
@@ -381,8 +397,7 @@
 def norm_begin(r):
     r.shi[...], r.slo[...] = split2(r.sin[...])
     r.gain_acc[...] = jnp.zeros((8, W), F32)
-    r.skip_acc[...] = jnp.zeros((8, W), F32)
-    r.back[:, :W] = jnp.zeros((STATE, W), F32)
+    r.acc[...] = jnp.zeros((STATE, W), F32)
 
 
 def norm_body(c, r):
@@ -413,24 +428,51 @@
         r.gz[at, :] = gz.astype(BF16)
         r.gy[at, :] = gy
         gpart = out * normed
-        spart = gy * x
         r.gain_acc[...] += gpart[0:8] + gpart[8:16]
-        r.skip_acc[...] += spart[0:8] + spart[8:16]
         r.hi[at, :], r.lo[at, :] = split2(gy * weight)
         r.rhi[at, :], r.rlo[at, :] = split2(gy * ys)
 
     each_rows(body)
     r.r[...] = dot2(r.e3[0:H, :], (r.rhi[...], r.rlo[...]), NT)
     new = dot2(cc, (r.hi[...], r.lo[...]), TN)
-    r.back[:, :W] += new
+    r.acc[...] += new
+
+
+def rest_level(value, levels):
+    high = value.astype(BF16).astype(F32)
+    place = (value - high) / jnp.maximum(jnp.abs(high) * 2.0**-8, 1e-30) + 1.0
+    return high, jnp.clip(jnp.floor(place * (levels / 2)), 0.0, levels - 1.0)
+
+
+def with_rest(high, level, levels):
+    return high + jnp.abs(high) * (2.0**-8 * ((level + 0.5) * (2.0 / levels) - 1.0))
 
 
 def norm_end(r):
-    r.back[:, W : 2 * W] = r.moments[:, :W] + r.thx[BY_ALOG : BY_ALOG + 1, :] * r.sin[...]
-    r.back[:, 2 * W :] = r.moments[:, W:] + r.thx[BY_BIAS : BY_BIAS + 1, :] * r.sin[...]
+    total = r.thx[TOTAL : TOTAL + 1, :]
+    base = log_base(total)
+    by_alog = r.thx[BY_ALOG : BY_ALOG + 1, :] - base * total
+    bias_base = r.thx[BASE : BASE + 1, :] * (1.0 + base)
+    by_bias = r.thx[BY_BIAS : BY_BIAS + 1, :] - bias_base * total
+    for d in range(SEQ):
+        at = slice(ROWS * d, ROWS * (d + 1))
+        back, back_rest = rest_level(r.acc[at, :], 32)
+        own = r.pay[at, :W]
+        sin = r.sin[at, :]
+        alog, alog_rest = rest_level(r.moments[at, :W] - base * own + by_alog * sin, 4)
+        bias, bias_rest = rest_level(r.moments[at, W:] - bias_base * own + by_bias * sin, 4)
+        rests = 16.0 * back_rest + 4.0 * alog_rest + bias_rest - 256.0
+        block = jnp.concatenate(
+            [jnp.concatenate([back, rests], 1), jnp.concatenate([alog, bias], 1)], 0
+        )
+        r.back[2 * ROWS * d : 2 * ROWS * (d + 1), :] = block.astype(BF16)
     r.sums[0:1, :] = jnp.sum(r.gain_acc[...], axis=0, keepdims=True)
-    r.sums[1:2, :] = jnp.sum(r.skip_acc[...], axis=0, keepdims=True)
-    r.sums[2:8, :] = jnp.zeros((6, W), F32)
+    r.sums[1:8, :] = jnp.zeros((7, W), F32)
+
+
+def local_x_begin(r):
+    r.acc[...] = jnp.zeros((STATE, W), F32)
+    r.skip_acc[...] = jnp.zeros((8, W), F32)
 
 
 def local_x_body(c, r):
@@ -438,6 +480,7 @@
     al = expand(r.pk, ALPHA, r.e3)
 
     def scale(at):
+        r.xhi[at, :], r.xlo[at, :] = split2(r.x[at, :].astype(F32) * ex[at, :])
         r.ghi[at, :], r.glo[at, :] = split2(r.gy[at, :] * al[at, :])
 
     each_rows(scale)
@@ -446,14 +489,19 @@
     gys = (r.ghi[...], r.glo[...])
     g = split2(dot(cc, b, NT) * r.mask[...].astype(F32))
     kappa = r.thx[pl.ds(KAP + c, 1), :]
-    r.dloc[...] = r.acc[...]
-    res = dot3(g, gys, TN) + dot2(b * r.me[...], split2(kappa * r.acc[...]), NN)
+    dstate = split2(kappa * r.acc[...])
+    res = dot3(g, gys, TN) + dot2(b * r.me[...], dstate, NN)
+    r.gbs[...] = r.me[...].astype(F32) * dot3_wide((r.xhi[...], r.xlo[...]), dstate)
     skip = r.vec[1:2, :]
 
     def finish(at):
+        x = r.x[at, :].astype(F32)
+        gy = r.gy[at, :]
         scaled = ex[at, :] * res[at, :]
-        r.gx[at, :] = scaled + skip * r.gy[at, :]
-        r.rhi[at, :], r.rlo[at, :] = split2(scaled * r.x[at, :].astype(F32))
+        r.gx[at, :] = scaled + skip * gy
+        r.rhi[at, :], r.rlo[at, :] = split2(scaled * x)
+        spart = gy * x
+        r.skip_acc[...] += spart[0:8] + spart[8:16]
 
     each_rows(finish)
     r.u[...] = dot2(r.e3[0:H, :], (r.rhi[...], r.rlo[...]), NT)
@@ -476,10 +524,7 @@
     gys = (r.ghi[...], r.glo[...])
     xs = (r.xhi[...], r.xlo[...])
     q = split2(dot3(gys, xs, NT) * r.mask[...].astype(F32))
-    kappa = r.thx[pl.ds(KAP + c, 1), :]
-    dstate = split2(kappa * r.dloc[...])
-    gb = joined(q, [cc, cc], TN) + r.me[...].astype(F32) * dot3_wide(xs, dstate)
-    r.gb[...] = gb
+    r.gb[...] = r.gbs[...] + joined(q, [cc, cc], TN)
     r.gc[...] = (r.gcs[...] + joined(q, [b, b], NN)).astype(BF16)
 
 
@@ -537,7 +582,7 @@
         sums[1] += jnp.sum(grad_dt, axis=1, keepdims=True)
 
     time_sums(r, r.u, jnp.zeros((H, 1), F32), write)
-    skips = jnp.broadcast_to(r.sums[1:2, :], (H, W))
+    skips = jnp.broadcast_to(jnp.sum(r.skip_acc[...], axis=0, keepdims=True), (H, W))
     skip_part = sum(dot(r.e3[0:H, :], part, NT) for part in split3(skips))[:, 0:1]
     lane = lax.broadcasted_iota(jnp.int32, (H, 128), 1)
     r.loc[...] = jnp.where(
@@ -546,6 +591,14 @@
 
 
 def final_x_end(r):
+    for k in range(8):
+        r.gain[:, 128 * k : 128 * (k + 1)] = r.params[k : k + 1, :128]
+    row = lax.broadcasted_iota(jnp.int32, (ROWS, ROWS), 0)
+    col = lax.broadcasted_iota(jnp.int32, (ROWS, ROWS), 1)
+    same = (row == col).astype(F32).astype(BF16)
+    turned = sum(dot(part, same, TN) for part in split3(r.params[:, 128:]))
+    for ref, at in ((r.gskip, SKIPS), (r.galog, ALOGS), (r.gbias, BIASES)):
+        ref[...] = jnp.concatenate([turned[at : at + 1, :], turned[at + 1 : at + 2, :]], 1)
     state = r.pay[:, :W] + r.thx[TOTAL : TOTAL + 1, :] * r.sin[...]
     ends = jnp.broadcast_to(jnp.sum(state * r.din[:, :W], axis=0, keepdims=True), (H, W))
     carry = sum(dot(r.e3[0:H, :], part, NT) for part in split3(ends))[:, 0:1]
@@ -671,8 +724,11 @@
         begin=clear,
     )
     ys, sloc, got = lax.optimization_barrier((ys, sloc, got))
-    before, through = scan(
-        scan_forward_kernel, "scan_forward", (sds((STATE, W), F32), sds((SEQ, W), F32)), got
+    before, after, through = scan(
+        scan_forward_kernel,
+        "scan_forward",
+        (sds((STATE, W), F32), sds((STATE, W), F32), sds((SEQ, W), F32)),
+        got,
     )
     sin = exchange(before)
     tied, _ = lax.optimization_barrier((x_in, got))
@@ -694,18 +750,18 @@
         | bcs
         | {"ys": (ys, "tok"), "z": (z_gate, "tok"), "go": (grad_out, "tok")}
         | x
-        | {"moments": (moments, "late")},
+        | {"moments": (moments, "late"), "pay": (pay, "late")},
         {
             "gy": ((T, W), F32, "tok"),
             "gz": ((T, W), BF16, "tok"),
             "r": ((H, T), F32, "row"),
-            "back": ((STATE, 3 * W), F32, "all"),
+            "back": ((2 * STATE, 2 * W), BF16, "all"),
             "sums": ((8, W), F32, "all"),
             "sin_copy": ((STATE, W), F32, "copy"),
         },
         {
             "gain_acc": ((8, W), F32),
-            "skip_acc": ((8, W), F32),
+            "acc": state,
             "shi": ((STATE, W), BF16),
             "slo": ((STATE, W), BF16),
             "hi": half,
@@ -720,14 +776,13 @@
     )
 
     got_back = exchange(back)
-    gx, u, dloc, gcs, loc = staged(
+    gx, u, gbs, gcs, loc = staged(
         local_x_body,
         common
         | {
             "vec": (vec, "all"),
             "sin": (sin, "all"),
             "par": (par, "all"),
-            "sums": (sums, "all"),
             "rf": (rf, "row"),
             "r": (r, "row"),
         }
@@ -738,28 +793,36 @@
         {
             "gx": ((T, W), F32, "tok"),
             "u": ((H, T), F32, "row"),
-            "dloc": ((C, STATE, W), F32, "state"),
+            "gbs": ((T, STATE), F32, "tok"),
             "gcs": ((T, STATE), F32, "tok"),
             "loc": ((H, 128), F32, "all"),
         },
-        {"acc": state, "ghi": half, "glo": half, "rhi": half, "rlo": half},
+        {
+            "acc": state,
+            "skip_acc": ((8, W), F32),
+            "ghi": half,
+            "glo": half,
+            "xhi": half,
+            "xlo": half,
+            "rhi": half,
+            "rlo": half,
+        },
         "local_x",
         7 * unit,
         backward=True,
-        begin=clear,
+        begin=local_x_begin,
         end=local_x_end,
     )
-    dloc, got_back = lax.optimization_barrier((dloc, got_back))
+    gbs, got_back = lax.optimization_barrier((gbs, got_back))
     behind = scan(
-        scan_backward_kernel, "scan_backward", sds((STATE, W + 256), F32), got_back, through, loc, sums, e3
+        scan_backward_kernel, "scan_backward", sds((STATE, W + 256), F32), got_back, through, after, loc, sums, e3, thx
     )
     din = exchange(behind)
     gb, gc = staged(
         local_bc_body,
-        common
+        {"e3": (e3, "all"), "pk": (pk, "row")}
         | bcs
-        | masks
-        | {"gy": (gy, "tok"), "dloc": (dloc, "state"), "gcs": (gcs, "tok")}
+        | {"mask": (mask, "tok"), "gy": (gy, "tok"), "gbs": (gbs, "tok"), "gcs": (gcs, "tok")}
         | x,
         {"gb": ((T, STATE), F32, "tok"), "gc": ((T, STATE), BF16, "tok")},
         {"ghi": half, "glo": half, "xhi": half, "xlo": half},
@@ -792,7 +855,7 @@
     back_bc = lax.all_to_all(
         gbc.reshape(GRP, 128, 2 * STATE), "head", split_axis=0, concat_axis=0, tiled=True
     )
-    grad_x, grad_dt = staged(
+    grad_x, grad_dt, grad_gain, grad_skip, grad_alog, grad_bias = staged(
         final_x_body,
         common
         | {
@@ -803,11 +866,19 @@
             "rf": (rf, "row"),
             "r": (r, "row"),
             "u": (u, "row"),
+            "params": (params, "all"),
         }
         | bcs
         | {"gx": (gx, "tok")}
         | x,
-        {"gxo": ((T, W), BF16, "tok"), "gdt": ((H, T), F32, "row")},
+        {
+            "gxo": ((T, W), BF16, "tok"),
+            "gdt": ((H, T), F32, "row"),
+            "gain": ((1, W), F32, "all"),
+            "gskip": ((1, H), F32, "all"),
+            "galog": ((1, H), F32, "all"),
+            "gbias": ((1, H), F32, "all"),
+        },
         {
             "uu": ((H, T), F32),
             "dhi": ((STATE, W), BF16),
@@ -829,12 +900,8 @@
         compiler_params=pltpu.CompilerParams(vmem_limit_bytes=16 * 2**20),
         name="unpack",
     )(pltpu.with_memory_space_constraint(back_bc, pltpu.VMEM))
-    grad_gain = params[:, :128].reshape(W)
-
-    def by_head(at):
-        return params[:, 128 + at : 130 + at].T.reshape(H)
-
-    grad_skip, grad_alog, grad_bias = by_head(SKIPS), by_head(ALOGS), by_head(BIASES)
+    grad_gain = grad_gain.reshape(W)
+    grad_skip, grad_alog, grad_bias = grad_skip.reshape(H), grad_alog.reshape(H), grad_bias.reshape(H)
     return (grad_x, gz, grad_b, grad_c, grad_dt, grad_alog, grad_bias, grad_skip, grad_gain)
 
 

time: 133 us -> 127 us (0.955)
  waiting for transfers between devices: 18.4 us -> 11.7 us
  local copies, waits for them, and re-layouts: 4.35 us -> 0.86 us
  Pallas kernels: 77.7 us -> 80.3 us
    all_to_all x4, waiting for transfers between devices: 17.5 us -> 10.3 us  [exchange(): return lax.all_to_all(v, 'seq', split_axis=0, concat_axis=0, tiled=True)]
    reshape x4 -> x0, local copies, waits for them, and re-layouts: 2.38 us -> none  [the longest x3 1.78 us: by_head(): return params[:, 128 + at:130 + at].T.reshape(H)]
    pallas_call x9, Pallas kernels: 68.2 us -> 69.7 us  [staged(): pl.pallas_call(kernel, out_shape=tuple((pltpu.HBM(s, d) for s, d, _ in ou...]
  transfers between devices with their start and end apart: 6 -> 6, of which waited for: 5 -> 6; matrix products, arithmetic and copies ran while one was open for 4% -> 1% of each run, Pallas kernels for 39% -> 42%
where the time goes in v5:
time: 127 us; the launch traced here: 125 us
  Pallas kernels  80.3 us (63%)
  starting transfers between devices  30.4 us (24%)
  waiting for transfers between devices  11.7 us (9%)
    pallas_call x9, Pallas kernels, staged(): pl.pallas_call(kernel, out_shape=tuple((pltpu.HBM(s, d) for s, d, _ in ou...  69.7 us
    all_to_all x4, starting transfers between devices, exchange(): return lax.all_to_all(v, 'seq', split_axis=0, concat_axis=0, tiled=True)  20.6 us
    all_to_all x4, waiting for transfers between devices, exchange(): return lax.all_to_all(v, 'seq', split_axis=0, concat_axis=0, tiled=True)  10.3 us
    all_to_all x1, starting transfers between devices, shard_body(): lax.all_to_all(mine, 'head', split_axis=0, concat_axis=0, tiled=True)  4.92 us
    all_to_all x1, starting transfers between devices, shard_body(): lax.all_to_all(gbc.reshape(GRP, 128, 2 * STATE), 'head', split_axis=0, co...  4.88 us
    pallas_call x2, Pallas kernels, scan(): pl.pallas_call(kernel, out_shape=outs, in_specs=[pl.BlockSpec(memory_spac...  4.21 us
    pallas_call x1, Pallas kernels, shard_body(): pl.pallas_call(prep_kernel, out_shape=(sds((12 * H, T), BF16), sds((2 * H...  3.55 us
  transfers between devices with their start and end apart: 6, of which 6 were waited for; matrix products, arithmetic and copies ran while one was open for 1% of the time, Pallas kernels for 42%

profile of v5, /device:TPU:8, one launch (start us, length us, event | category | flops | bytes accessed | tf_op | source)
XLA Modules:
  0.0 124.8 jit_solution(13712098327174378232)
XLA Ops:
  0.7 1.9 %pack.1 = bf16[8,128,256]{2,1,0:T(8,128)(2,1)} custom-call(bf16[128,1024]{1,0:T(8,128)(2,1)} %b_ref.1, bf16[128,1024]{1,0:T(8,128)(2,1)} %c_ref.1), custom_call_target="tpu_custom_call" | custom-call | tf_op jit(solution)/shard_map/pack/pallas_call | solution.py:647
  2.6 4.9 %all-to-all-start = ((bf16[8,128,256]{2,1,0:T(8,128)(2,1)}), bf16[8,128,256]{2,1,0:T(8,128)(2,1)S(1)}, u32[]{:S(2)}, u32[]{:S(2)}) async-start(bf16[8,128,256]{2,1,0:T(8,128)(2,1)} %pack.1), calls=%async_computation | async-start | bytes 1048576 | tf_op jit(solution)/shard_map/all_to_all | solution.py:653
  7.5 0.1 copy.23
  7.6 0.6 pad.8.par_ref.refs_5_.refs_6_
  8.2 3.6 %prep.1 = (bf16[192,1024]{1,0:T(8,128)(2,1)}, f32[32,1024]{1,0:T(8,128)}, bf16[1024,256]{1,0:T(8,128)(2,1)}, bf16[1024,128]{1,0:T(8,128)(2,1)}, bf16[1024,128]{1,0:T(8,128)(2,1)}, /*index=5*/f32[16,1024]{1,0:T(8,128)}) custom-call(f32[16,1024]{1,0:T(8,128)} %dt_ref.1, f32[16,128]{1,0:T(8,128)} %pad.8.par_ref.refs_5_.refs_6_, s32[1,1024]{1,0:T(1,128)} %bitcast.28, ...), custom_call_target="tpu_custom_call" | custom-call | tf_op jit(solution)/shard_map/prep/pallas_call | solution.py:656
  11.8 3.9 %scale.1 = (bf16[1024,1024]{1,0:T(8,128)(2,1)}, bf16[1024,1024]{1,0:T(8,128)(2,1)}) custom-call(bf16[48,1024]{1,0:T(8,128)(2,1)} %constant.5.clone.e3_ref.refs_0_, bf16[192,1024]{1,0:T(8,128)(2,1)} %get-tuple-element.63.refs_1_, bf16[1024,1024]{1,0:T(8,128)(2,1)} %refs_13_.1), custom_call_target="tpu_custom_call" | custom-call | flops 536870912 | bytes 8388608 | tf_op jit(solution)/shard_map/scale/pallas_call | solution.py:173
  15.7 0.7 all-to-all-done
  16.4 3.8 %states.1 = (f32[128,1152]{1,0:T(8,128)}, bf16[1024,256]{1,0:T(8,128)(2,1)}) custom-call(f32[16,1024]{1,0:T(8,128)} %get-tuple-element.64.refs_0_.refs_2_.thx_ref, bf16[1024,256]{1,0:T(8,128)(2,1)S(1)} %bitcast.21, bf16[1024,1024]{1,0:T(8,128)(2,1)} %get-tuple-element.68.refs_2_.refs_3_, bf16[1024,1024]{1,0:T(8,128)(2,1)} %get-tuple-element.69.refs_3_.refs_4_), custom_call_target="tpu_custom_call" | custom-call | flops 1073741824 | bytes 8388608 | tf_op jit(solution)/shard_map/states/pallas_call | solution.py:173
  20.2 7.9 %all-to-all-start.1 = ((f32[16,8,1152]{2,1,0:T(8,128)}), f32[16,8,1152]{2,1,0:T(8,128)S(1)}, u32[]{:S(2)}, u32[]{:S(2)}) async-start(f32[16,8,1152]{2,1,0:T(8,128)} %bitcast.23), calls=%async_computation.1 | async-start | bytes 1179648 | tf_op jit(solution)/shard_map/all_to_all | solution.py:710
  28.2 0.0 copy-start
  28.2 8.0 %within.1 = (f32[1024,1024]{1,0:T(8,128)}, f32[4,128,1024]{2,1,0:T(8,128)}) custom-call(bf16[48,1024]{1,0:T(8,128)(2,1)} %constant.5.clone.e3_ref.refs_0_, bf16[192,1024]{1,0:T(8,128)(2,1)} %get-tuple-element.63.refs_1_, f32[16,1024]{1,0:T(8,128)} %get-tuple-element.64.refs_0_.refs_2_.thx_ref, ...), custom_call_target="tpu_custom_call" | custom-call | flops 3758096384 | bytes 8388608 | tf_op jit(solution)/shard_map/within/pallas_call | solution.py:173
  36.2 3.7 %all-to-all-done.1 = f32[16,8,1152]{2,1,0:T(8,128)S(1)} async-done(((f32[16,8,1152]{2,1,0:T(8,128)}), f32[16,8,1152]{2,1,0:T(8,128)S(1)}, u32[]{:S(2)}, u32[]{:S(2)}) %all-to-all-start.1) | async-done | bytes 589856 | tf_op jit(solution)/shard_map/all_to_all | solution.py:710
  39.9 1.1 scan_forward.1
  40.9 3.8 %all-to-all-start.2 = ((f32[16,8,1024]{2,1,0:T(8,128)}), f32[16,8,1024]{2,1,0:T(8,128)S(1)}, u32[]{:S(2)}, u32[]{:S(2)}) async-start(f32[16,8,1024]{2,1,0:T(8,128)} %bitcast.27), calls=%async_computation.2 | async-start | bytes 1048576 | tf_op jit(solution)/shard_map/all_to_all | solution.py:710
  44.7 0.1 broadcast_in_dim.3
  44.8 0.1 stack_reshape.3
  44.9 0.6 select_maximum_fusion.refs_3_
  45.5 5.8 %moments.1.refs_10_ = f32[128,2048]{1,0:T(8,128)} custom-call(bf16[48,1024]{1,0:T(8,128)(2,1)} %constant.5.clone.e3_ref.refs_0_, bf16[192,1024]{1,0:T(8,128)(2,1)} %get-tuple-element.63.refs_1_, bf16[1024,256]{1,0:T(8,128)(2,1)} %get-tuple-element.70.refs_3_.refs_2_.refs_5_.refs_8_.refs_11_, bf16[1024,1024]{1,0:T(8,128)(2,1)} %refs_13_.1), custom_call_target="tpu_custom_call" | custom-call | flops 2147483648 | bytes 8388608 | tf_op jit(solution)/shard_map/moments/pallas_call | solution.py:173
  51.3 3.9 %all-to-all-done.2 = f32[16,8,1024]{2,1,0:T(8,128)S(1)} async-done(((f32[16,8,1024]{2,1,0:T(8,128)}), f32[16,8,1024]{2,1,0:T(8,128)S(1)}, u32[]{:S(2)}, u32[]{:S(2)}) %all-to-all-start.2) | async-done | bytes 524320 | tf_op jit(solution)/shard_map/all_to_all | solution.py:710
  55.2 12.2 %norm.1 = (f32[1024,1024]{1,0:T(8,128)}, bf16[1024,1024]{1,0:T(8,128)(2,1)}, f32[16,1024]{1,0:T(8,128)}, bf16[256,2048]{1,0:T(8,128)(2,1)}, f32[8,1024]{1,0:T(8,128)}, /*index=5*/f32[128,1024]{1,0:T(8,128)}) custom-call(bf16[48,1024]{1,0:T(8,128)(2,1)} %constant.5.clone.e3_ref.refs_0_, bf16[192,1024]{1,0:T(8,128)(2,1)} %get-tuple-element.63.refs_1_, ...), custom_call_target="tpu_custom_call" | custom-call | flops 3221225472 | bytes 8388608 | tf_op jit(solution)/shard_map/norm/pallas_call | solution.py:173
  67.4 3.7 %all-to-all-start.3 = ((bf16[16,16,2048]{2,1,0:T(8,128)(2,1)}), bf16[16,16,2048]{2,1,0:T(8,128)(2,1)S(1)}, u32[]{:S(2)}, u32[]{:S(2)}) async-start(bf16[16,16,2048]{2,1,0:T(8,128)(2,1)} %bitcast.25), calls=%async_computation.3 | async-start | bytes 2097152 | tf_op jit(solution)/shard_map/all_to_all | solution.py:710
  71.1 13.3 %local_x.1 = (f32[1024,1024]{1,0:T(8,128)}, f32[16,1024]{1,0:T(8,128)}, f32[1024,128]{1,0:T(8,128)}, f32[1024,128]{1,0:T(8,128)}, f32[16,128]{1,0:T(8,128)}) custom-call(bf16[48,1024]{1,0:T(8,128)(2,1)} %constant.5.clone.e3_ref.refs_0_, bf16[192,1024]{1,0:T(8,128)(2,1)} %get-tuple-element.63.refs_1_, f32[16,1024]{1,0:T(8,128)} %get-tuple-element.64.refs_0_.refs_2_.thx_ref, ...), custom_call_target="tpu_custom_call" | custom-call | flops 3758096384 | bytes 8388608 | tf_op jit(solution)/shard_map/local_x/pallas_call | solution.py:173
  84.4 1.9 %all-to-all-done.3 = bf16[16,16,2048]{2,1,0:T(8,128)(2,1)S(1)} async-done(((bf16[16,16,2048]{2,1,0:T(8,128)(2,1)}), bf16[16,16,2048]{2,1,0:T(8,128)(2,1)S(1)}, u32[]{:S(2)}, u32[]{:S(2)}) %all-to-all-start.3) | async-done | bytes 1048608 | tf_op jit(solution)/shard_map/all_to_all | solution.py:710
  86.3 3.1 %scan_backward.1 = f32[128,1280]{1,0:T(8,128)} custom-call(bf16[256,2048]{1,0:T(8,128)(2,1)S(1)} %bitcast.18, f32[16,1024]{1,0:T(8,128)} %get-tuple-element.94.through_ref, f32[128,1024]{1,0:T(8,128)} %get-tuple-element.95.after_ref, f32[16,128]{1,0:T(8,128)} %get-tuple-element.96.loc_ref, f32[8,1024]{1,0:T(8,128)} %get-tuple-element.97.sums_ref, ...), custom_call_target="tpu_custom_call" | custom-call | tf_op jit(solution)/shard_map/scan_backward/pallas_call | solution.py:698
  89.5 5.3 %all-to-all-start.4 = ((f32[16,8,1280]{2,1,0:T(8,128)}), f32[16,8,1280]{2,1,0:T(8,128)S(1)}, u32[]{:S(2)}, u32[]{:S(2)}) async-start(f32[16,8,1280]{2,1,0:T(8,128)} %bitcast.24), calls=%async_computation.4 | async-start | bytes 1310720 | tf_op jit(solution)/shard_map/all_to_all | solution.py:710
  94.8 10.0 %local_bc.1 = (f32[1024,128]{1,0:T(8,128)}, bf16[1024,128]{1,0:T(8,128)(2,1)}) custom-call(bf16[48,1024]{1,0:T(8,128)(2,1)} %constant.5.clone.e3_ref.refs_0_, bf16[192,1024]{1,0:T(8,128)(2,1)} %get-tuple-element.63.refs_1_, bf16[1024,256]{1,0:T(8,128)(2,1)} %get-tuple-element.70.refs_3_.refs_2_.refs_5_.refs_8_.refs_11_, ...), custom_call_target="tpu_custom_call" | custom-call | flops 2684354560 | bytes 8388608 | tf_op jit(solution)/shard_map/local_bc/pallas_call | solution.py:173
  104.8 0.8 all-to-all-done.4
  105.5 4.4 %final_bc.1 = (bf16[1024,256]{1,0:T(8,128)(2,1)}, f32[128,1280]{1,0:T(8,128)}, f32[8,256]{1,0:T(8,128)}) custom-call(f32[128,1280]{1,0:T(8,128)S(1)} %bitcast.19, f32[1024,128]{1,0:T(8,128)} %get-tuple-element.99.refs_1_, bf16[1024,128]{1,0:T(8,128)(2,1)} %get-tuple-element.100.refs_2_, bf16[1024,1024]{1,0:T(8,128)(2,1)} %get-tuple-element.68.refs_2_.refs_3_, ...), custom_call_target="tpu_custom_call" | custom-call | flops 1073741824 | bytes 8388608 | tf_op jit(solution)/shard_map/final_bc/pallas_call | solution.py:173
  109.9 4.9 %all-to-all-start.5 = ((bf16[8,128,256]{2,1,0:T(8,128)(2,1)}), bf16[8,128,256]{2,1,0:T(8,128)(2,1)S(1)}, u32[]{:S(2)}, u32[]{:S(2)}) async-start(bf16[8,128,256]{2,1,0:T(8,128)(2,1)} %bitcast.26), calls=%async_computation.5 | async-start | bytes 1048576 | tf_op jit(solution)/shard_map/all_to_all | solution.py:855
  114.8 8.2 %final_x.1 = (bf16[1024,1024]{1,0:T(8,128)(2,1)}, f32[16,1024]{1,0:T(8,128)}, f32[1,1024]{1,0:T(1,128)}, f32[1,16]{1,0:T(1,128)}, f32[1,16]{1,0:T(1,128)}, /*index=5*/f32[1,16]{1,0:T(1,128)}) custom-call(bf16[48,1024]{1,0:T(8,128)(2,1)} %constant.5.clone.e3_ref.refs_0_, bf16[192,1024]{1,0:T(8,128)(2,1)} %get-tuple-element.63.refs_1_, ...), custom_call_target="tpu_custom_call" | custom-call | flops 1610612736 | bytes 8388608 | tf_op jit(solution)/shard_map/final_x/pallas_call | solution.py:173
  123.1 0.7 all-to-all-done.5.in_ref
  123.7 0.9 unpack.1
  (8 shorter events, 0.0 us)
Async XLA Ops:
  0.6 6.9 %copy-start.2 = (f32[16]{0:T(128)S(1)}, f32[16]{0:T(128)}, u32[]{:S(2)}) copy-start(f32[16]{0:T(128)} %param.18) | copy-start | bytes 196
  0.7 6.9 %copy-start.3 = (f32[16]{0:T(128)S(1)}, f32[16]{0:T(128)}, u32[]{:S(2)}) copy-start(f32[16]{0:T(128)} %param.17) | copy-start | bytes 196
  2.6 13.8 %all-to-all-start = ((bf16[8,128,256]{2,1,0:T(8,128)(2,1)}), bf16[8,128,256]{2,1,0:T(8,128)(2,1)S(1)}, u32[]{:S(2)}, u32[]{:S(2)}) async-start(bf16[8,128,256]{2,1,0:T(8,128)(2,1)} %pack.1), calls=%async_computation | async-start | bytes 1048576 | tf_op jit(solution)/shard_map/all_to_all | solution.py:653
  20.2 19.6 %all-to-all-start.1 = ((f32[16,8,1152]{2,1,0:T(8,128)}), f32[16,8,1152]{2,1,0:T(8,128)S(1)}, u32[]{:S(2)}, u32[]{:S(2)}) async-start(f32[16,8,1152]{2,1,0:T(8,128)} %bitcast.23), calls=%async_computation.1 | async-start | bytes 1179648 | tf_op jit(solution)/shard_map/all_to_all | solution.py:710
  28.1 16.6 %copy-start.1 = (f32[16]{0:T(128)S(1)}, f32[16]{0:T(128)}, u32[]{:S(2)}) copy-start(f32[16]{0:T(128)} %param.19) | copy-start | bytes 196
  28.2 16.7 %copy-start = (f32[1024]{0:T(1024)S(1)}, f32[1024]{0:T(1024)}, u32[]{:S(2)}) copy-start(f32[1024]{0:T(1024)} %param.20) | copy-start | bytes 12292
  40.9 14.3 %all-to-all-start.2 = ((f32[16,8,1024]{2,1,0:T(8,128)}), f32[16,8,1024]{2,1,0:T(8,128)S(1)}, u32[]{:S(2)}, u32[]{:S(2)}) async-start(f32[16,8,1024]{2,1,0:T(8,128)} %bitcast.27), calls=%async_computation.2 | async-start | bytes 1048576 | tf_op jit(solution)/shard_map/all_to_all | solution.py:710
  67.4 18.9 %all-to-all-start.3 = ((bf16[16,16,2048]{2,1,0:T(8,128)(2,1)}), bf16[16,16,2048]{2,1,0:T(8,128)(2,1)S(1)}, u32[]{:S(2)}, u32[]{:S(2)}) async-start(bf16[16,16,2048]{2,1,0:T(8,128)(2,1)} %bitcast.25), calls=%async_computation.3 | async-start | bytes 2097152 | tf_op jit(solution)/shard_map/all_to_all | solution.py:710
  89.5 16.1 %all-to-all-start.4 = ((f32[16,8,1280]{2,1,0:T(8,128)}), f32[16,8,1280]{2,1,0:T(8,128)S(1)}, u32[]{:S(2)}, u32[]{:S(2)}) async-start(f32[16,8,1280]{2,1,0:T(8,128)} %bitcast.24), calls=%async_computation.4 | async-start | bytes 1310720 | tf_op jit(solution)/shard_map/all_to_all | solution.py:710
  109.9 13.8 %all-to-all-start.5 = ((bf16[8,128,256]{2,1,0:T(8,128)(2,1)}), bf16[8,128,256]{2,1,0:T(8,128)(2,1)S(1)}, u32[]{:S(2)}, u32[]{:S(2)}) async-start(bf16[8,128,256]{2,1,0:T(8,128)(2,1)} %bitcast.26), calls=%async_computation.5 | async-start | bytes 1048576 | tf_op jit(solution)/shard_map/all_to_all | solution.py:855

commit v6 on v5

--- a/solution.py
+++ b/solution.py
@@ -22,6 +22,7 @@
 ROWS = STATE // SEQ
 F32 = jnp.float32
 BF16 = jnp.bfloat16
+FLUSHES = 4
 STEP = 16
 VMEM_LIMIT = 60 * 2**20
 VMEM_NEAR = 48 * 2**20
@@ -94,6 +95,11 @@
     moving = ("tok", "state")
     here = [k for k in ins if kinds[k] in ("near", "near_tok")]
     copied = [k for k in outs if kinds[k] == "copy"]
+    steps = C
+    slot, count = {}, 0
+    for k in [*ins, *outs]:
+        slot[k] = count
+        count += {"tok": steps, "state": steps, "blocks": FLUSHES, "near": 0, "near_tok": 0}.get(kinds[k], 1)
     buffered_in = [k for k in ins if k not in here]
     buffered_out = [k for k in outs if k not in copied]
 
@@ -108,22 +114,21 @@
         near = dict(zip([*buffered_in, *buffered_out, *scratch], refs[n + m : -1]))
         near.update({k: far_in[k] for k in here})
         sems = refs[-1]
-        slot = {k: i for i, k in enumerate([*ins, *outs])}
 
         def copy_in(k, c):
-            return pltpu.make_async_copy(part(far_in[k], kinds[k], c), part(near[k], kinds[k], c), sems.at[slot[k], c])
+            return pltpu.make_async_copy(part(far_in[k], kinds[k], c), part(near[k], kinds[k], c), sems.at[slot[k] + c])
 
         def copy_out(k, c):
-            return pltpu.make_async_copy(part(near[k], kinds[k], c), part(far_out[k], kinds[k], c), sems.at[slot[k], c])
+            return pltpu.make_async_copy(part(near[k], kinds[k], c), part(far_out[k], kinds[k], c), sems.at[slot[k] + c])
 
         once = [
-            pltpu.make_async_copy(far_in[k], near[k], sems.at[slot[k], 0])
+            pltpu.make_async_copy(far_in[k], near[k], sems.at[slot[k]])
             for k in buffered_in
             if kinds[k] in ("row", "all")
         ]
-        late = [pltpu.make_async_copy(far_in[k], near[k], sems.at[slot[k], 0]) for k in ins if kinds[k] == "late"]
+        late = [pltpu.make_async_copy(far_in[k], near[k], sems.at[slot[k]]) for k in ins if kinds[k] == "late"]
         passed = [
-            pltpu.make_async_copy(near[k.removesuffix("_copy")], far_out[k], sems.at[slot[k], 0]) for k in copied
+            pltpu.make_async_copy(near[k.removesuffix("_copy")], far_out[k], sems.at[slot[k]]) for k in copied
         ]
         for copy in once:
             copy.start()
@@ -136,6 +141,14 @@
         for copy in once:
             copy.wait()
         whole = Views(near, {k: "all" for k in near}, 0)
+        flushed = []
+
+        def flush(k, i, at):
+            copy = pltpu.make_async_copy(near[k].at[at, :], far_out[k].at[at, :], sems.at[slot[k] + i])
+            copy.start()
+            flushed.append(copy)
+
+        whole.flush = flush
         if begin is not None:
             begin(whole)
 
@@ -156,9 +169,9 @@
         if end is not None:
             end(whole)
         once = [
-            pltpu.make_async_copy(near[k], far_out[k], sems.at[slot[k], 0])
+            pltpu.make_async_copy(near[k], far_out[k], sems.at[slot[k]])
             for k in buffered_out
-            if kinds[k] not in moving
+            if kinds[k] in ("row", "all")
         ]
         for copy in once:
             copy.start()
@@ -166,7 +179,7 @@
             for k in outs:
                 if kinds[k] in moving:
                     copy_out(k, c).wait()
-        for copy in once + passed:
+        for copy in once + passed + flushed:
             copy.wait()
 
     far = pl.BlockSpec(memory_space=pl.ANY)
@@ -179,7 +192,7 @@
             *[pltpu.VMEM(ins[k][0].shape, ins[k][0].dtype) for k in buffered_in],
             *[pltpu.VMEM(*outs[k][:2]) for k in buffered_out],
             *[pltpu.VMEM(s, d) for s, d in scratch.values()],
-            pltpu.SemaphoreType.DMA((n + m, C)),
+            pltpu.SemaphoreType.DMA((count,)),
         ],
         compiler_params=pltpu.CompilerParams(vmem_limit_bytes=VMEM_NEAR if here else VMEM_LIMIT),
         cost_estimate=pl.CostEstimate(flops=flops, bytes_accessed=8 * 2**20, transcendentals=0),
@@ -191,7 +204,24 @@
     return dot(pk[2 * H * which : 2 * H * (which + 1), :], e3[0 : 2 * H, :], TN)
 
 
-def prep_kernel(dt_ref, par_ref, st_ref, e3_ref, pk_ref, rf_ref, mask_ref, me_ref, mw_ref, thx_ref):
+def fold(v):
+    lane = lax.broadcasted_iota(jnp.int32, (STEP, 128), 1)
+    tiles = []
+    for k in range(0, W, 256):
+        a, b = v[:, k : k + 128], v[:, k + 128 : k + 256]
+        a = a + pltpu.roll(a, 96, 1)
+        b = b + pltpu.roll(b, 32, 1)
+        tiles.append(jnp.where((lane & 32) == 0, a, b))
+    return jnp.concatenate(tiles, 1)
+
+
+def folded_heads():
+    lane = np.arange(W // 2)
+    head = 4 * (lane // 128) + (lane % 128 >= 64) + 2 * ((lane & 32) != 0)
+    return jnp.asarray(head[None, :] == np.arange(H)[:, None], BF16)
+
+
+def prep_kernel(dt_ref, par_ref, st_ref, e3_ref, pk_ref, rf_ref, marks_ref, thx_ref):
     bias = par_ref[:, 0:1]
     nega = -jnp.exp(par_ref[:, 1:2])
     row = lax.broadcasted_iota(jnp.int32, (L, L), 0)
@@ -235,11 +265,11 @@
         seg_first = jnp.where(first, seg, 0.0).astype(BF16)
         seg_col = dot(seg_first, ones, TN)
         mask = causal & (seg_col == seg[0:1, :])
-        mask_ref[at, :] = mask.astype(F32).astype(BF16)
+        marks_ref[at, :L] = mask.astype(F32).astype(BF16)
         to_end = jnp.where(first & (seg == seg_end), 1.0, 0.0).astype(BF16)
         from_start = jnp.where(first & (seg == 0.0), 1.0, 0.0).astype(BF16)
-        me_ref[at, :] = dot(to_end, ones[:, :128], TN).astype(BF16)
-        mw_ref[at, :] = dot(from_start, ones[:, :128], TN).astype(BF16)
+        marks_ref[at, L : L + 128] = dot(to_end, ones[:, :128], TN).astype(BF16)
+        marks_ref[at, L + 128 :] = dot(from_start, ones[:, :128], TN).astype(BF16)
         thr.append(jnp.where(seg_end == 0.0, jnp.exp(cum_end), 0.0))
         kap.append(jnp.exp(half))
     passed = jnp.ones((H, 1), F32)
@@ -294,6 +324,10 @@
         r.pay[ROWS * d : ROWS * (d + 1), W:] = block
 
 
+def log_base(through):
+    return jnp.where(through > 1e-30, 0.5 * jnp.log(jnp.maximum(through, 1e-30)), 0.0)
+
+
 def moments_body(c, r):
     by_alog = expand(r.pk, END_ALOG, r.e3)
     by_bias = expand(r.pk, END_BIAS, r.e3)
@@ -313,8 +347,11 @@
     r.moments[...] = jnp.zeros((STATE, 2 * W), F32)
 
 
-def log_base(through):
-    return jnp.where(through > 1e-30, 0.5 * jnp.log(jnp.maximum(through, 1e-30)), 0.0)
+def moments_end(r):
+    base = log_base(r.thx[TOTAL : TOTAL + 1, :])
+    own = r.pay[:, :W]
+    r.moments[:, :W] -= base * own
+    r.moments[:, W:] -= (r.thx[BASE : BASE + 1, :] * (1.0 + base)) * own
 
 
 def through_row(got_ref, j):
@@ -333,23 +370,35 @@
         after_ref[at, :] = acc
 
 
-def scan_backward_kernel(got_ref, through_ref, after_ref, loc_ref, sums_ref, e3_ref, thx_ref, out_ref):
+def scan_backward_kernel(got_ref, through_ref, after_ref, loc_ref, sums_ref, e3_ref, thx_ref, far_ref, out_ref, sems):
     acc = jnp.zeros((ROWS, W), F32)
     by_alog = jnp.zeros((ROWS, W), F32)
     by_bias = jnp.zeros((ROWS, W), F32)
+    through_all = through_ref[...]
+    base_all = log_base(through_all)
+    bias_base_all = thx_ref[BASE : BASE + 1, :] * (1.0 + base_all)
+    copies = []
+
+    def send(j, lanes, k):
+        at = slice(ROWS * j, ROWS * (j + 1))
+        copy = pltpu.make_async_copy(out_ref.at[at, lanes], far_ref.at[at, lanes], sems.at[k, j])
+        copy.start()
+        copies.append(copy)
+
     for j in reversed(range(SEQ)):
         at = slice(ROWS * j, ROWS * (j + 1))
         out_ref[at, :W] = acc
+        send(j, slice(0, W), 0)
         block = got_ref[2 * ROWS * j : 2 * ROWS * (j + 1), :].astype(F32)
-        through = through_ref[j : j + 1, :]
+        through = through_all[j : j + 1, :]
         state = after_ref[at, :]
         rests = block[:ROWS, W:] + 256.0
         back_rest = jnp.floor(rests * (1.0 / 16))
         rests = rests - 16.0 * back_rest
         alog_rest = jnp.floor(rests * 0.25)
         bias_rest = rests - 4.0 * alog_rest
-        base = log_base(through)
-        bias_base = thx_ref[BASE : BASE + 1, :] * (1.0 + base)
+        base = base_all[j : j + 1, :]
+        bias_base = bias_base_all[j : j + 1, :]
         by_alog += acc * (with_rest(block[ROWS:, :W], alog_rest, 4) + base * state)
         by_bias += acc * (with_rest(block[ROWS:, W:], bias_rest, 4) + bias_base * state)
         acc = through * acc + with_rest(block[:ROWS, :W], back_rest, 32)
@@ -373,6 +422,9 @@
     for d in range(SEQ):
         out_ref[ROWS * d : ROWS * (d + 1), W : W + 128] = left
         out_ref[ROWS * d : ROWS * (d + 1), W + 128 :] = right
+        send(d, slice(W, W + 256), 1)
+    for copy in copies:
+        copy.wait()
 
 
 def within_body(c, r):
@@ -385,13 +437,14 @@
     each_rows(scale)
     b = r.bc[:, :STATE]
     cc = r.bc[:, STATE:]
-    g = split2(dot(cc, b, NT) * r.mask[...].astype(F32))
+    g = split2(dot(cc, b, NT) * r.marks[:, :L].astype(F32))
+    r.g[:, :L], r.g[:, L:] = g
     xs = (r.hi[...], r.lo[...])
     kappa = r.thx[pl.ds(KAP + c, 1), :]
     r.sloc[...] = r.acc[...]
-    res = dot3(g, xs, NN) + dot2(cc * r.mw[...], split2(kappa * r.acc[...]), NN)
-    r.ys[...] = al * res
-    r.acc[...] = r.thx[pl.ds(THR + c, 1), :] * r.acc[...] + kappa * dot2(b * r.me[...], xs, TN)
+    res = dot3(g, xs, NN) + dot2(cc * r.marks[:, L + 128 :], split2(kappa * r.acc[...]), NN)
+    r.y[...] = al * res + r.vec[1:2, :] * r.x[...].astype(F32)
+    r.acc[...] = r.thx[pl.ds(THR + c, 1), :] * r.acc[...] + kappa * dot2(b * r.marks[:, L : L + 128], xs, TN)
 
 
 def norm_begin(r):
@@ -405,15 +458,12 @@
     win = expand(r.pk, FROM_START, r.e3)
     res = dot2(cc, (r.shi[...], r.slo[...]), NN)
     gain = r.vec[0:1, :]
-    skip = r.vec[1:2, :]
 
     def body(at):
         weight = win[at, :]
-        x = r.x[at, :].astype(F32)
         z = r.z[at, :].astype(F32)
         out = r.go[at, :].astype(F32)
-        ys = r.ys[at, :] + weight * res[at, :]
-        y = ys + skip * x
+        y = r.y[at, :] + weight * res[at, :]
         logistic = jax.nn.sigmoid(z)
         silu = z * logistic
         gated = y * silu
@@ -430,7 +480,7 @@
         gpart = out * normed
         r.gain_acc[...] += gpart[0:8] + gpart[8:16]
         r.hi[at, :], r.lo[at, :] = split2(gy * weight)
-        r.rhi[at, :], r.rlo[at, :] = split2(gy * ys)
+        r.rhi[at, :], r.rlo[at, :] = split2(gy * y)
 
     each_rows(body)
     r.r[...] = dot2(r.e3[0:H, :], (r.rhi[...], r.rlo[...]), NT)
@@ -440,7 +490,7 @@
 
 def rest_level(value, levels):
     high = value.astype(BF16).astype(F32)
-    place = (value - high) / jnp.maximum(jnp.abs(high) * 2.0**-8, 1e-30) + 1.0
+    place = (value - high) * pl.reciprocal(jnp.maximum(jnp.abs(high) * 2.0**-8, 1e-30), approx=True) + 1.0
     return high, jnp.clip(jnp.floor(place * (levels / 2)), 0.0, levels - 1.0)
 
 
@@ -457,22 +507,25 @@
     for d in range(SEQ):
         at = slice(ROWS * d, ROWS * (d + 1))
         back, back_rest = rest_level(r.acc[at, :], 32)
-        own = r.pay[at, :W]
         sin = r.sin[at, :]
-        alog, alog_rest = rest_level(r.moments[at, :W] - base * own + by_alog * sin, 4)
-        bias, bias_rest = rest_level(r.moments[at, W:] - bias_base * own + by_bias * sin, 4)
+        alog, alog_rest = rest_level(r.moments[at, :W] + by_alog * sin, 4)
+        bias, bias_rest = rest_level(r.moments[at, W:] + by_bias * sin, 4)
         rests = 16.0 * back_rest + 4.0 * alog_rest + bias_rest - 256.0
         block = jnp.concatenate(
             [jnp.concatenate([back, rests], 1), jnp.concatenate([alog, bias], 1)], 0
         )
-        r.back[2 * ROWS * d : 2 * ROWS * (d + 1), :] = block.astype(BF16)
+        to = slice(2 * ROWS * d, 2 * ROWS * (d + 1))
+        r.back[to, :] = block.astype(BF16)
+        if (d + 1) % (SEQ // FLUSHES) == 0:
+            rows = 2 * STATE // FLUSHES
+            piece = d * FLUSHES // SEQ
+            r.flush("back", piece, slice(rows * piece, rows * (piece + 1)))
     r.sums[0:1, :] = jnp.sum(r.gain_acc[...], axis=0, keepdims=True)
     r.sums[1:8, :] = jnp.zeros((7, W), F32)
 
 
 def local_x_begin(r):
     r.acc[...] = jnp.zeros((STATE, W), F32)
-    r.skip_acc[...] = jnp.zeros((8, W), F32)
 
 
 def local_x_body(c, r):
@@ -487,11 +540,11 @@
     b = r.bc[:, :STATE]
     cc = r.bc[:, STATE:]
     gys = (r.ghi[...], r.glo[...])
-    g = split2(dot(cc, b, NT) * r.mask[...].astype(F32))
+    g = (r.g[:, :L], r.g[:, L:])
     kappa = r.thx[pl.ds(KAP + c, 1), :]
     dstate = split2(kappa * r.acc[...])
-    res = dot3(g, gys, TN) + dot2(b * r.me[...], dstate, NN)
-    r.gbs[...] = r.me[...].astype(F32) * dot3_wide((r.xhi[...], r.xlo[...]), dstate)
+    res = dot3(g, gys, TN) + dot2(b * r.marks[:, L : L + 128], dstate, NN)
+    r.gs[:, :STATE] = r.marks[:, L : L + 128].astype(F32) * dot3_wide((r.xhi[...], r.xlo[...]), dstate)
     skip = r.vec[1:2, :]
 
     def finish(at):
@@ -499,23 +552,22 @@
         gy = r.gy[at, :]
         scaled = ex[at, :] * res[at, :]
         r.gx[at, :] = scaled + skip * gy
-        r.rhi[at, :], r.rlo[at, :] = split2(scaled * x)
-        spart = gy * x
-        r.skip_acc[...] += spart[0:8] + spart[8:16]
+        r.rhi[at, :], r.rlo[at, :] = split2(fold(scaled * x))
+        r.shi[at, :], r.slo[at, :] = split2(fold(gy * x))
 
     each_rows(finish)
-    r.u[...] = dot2(r.e3[0:H, :], (r.rhi[...], r.rlo[...]), NT)
+    r.u[...] = dot2(r.eh[...], (r.rhi[...], r.rlo[...]), NT)
+    r.sx[...] = dot2(r.eh[...], (r.shi[...], r.slo[...]), NT)
+    r.rr[...] = r.r[...] - r.par[:, 2:3] * r.sx[...]
     state = split2(kappa * (r.sloc[...] + r.thx[pl.ds(PRE + c, 1), :] * r.sin[...]))
-    r.gcs[...] = r.mw[...].astype(F32) * dot3_wide(gys, state)
-    r.acc[...] = r.thx[pl.ds(THR + c, 1), :] * r.acc[...] + kappa * dot2(cc * r.mw[...], gys, TN)
+    r.gs[:, STATE:] = r.marks[:, L + 128 :].astype(F32) * dot3_wide(gys, state)
+    r.acc[...] = r.thx[pl.ds(THR + c, 1), :] * r.acc[...] + kappa * dot2(cc * r.marks[:, L + 128 :], gys, TN)
 
 
 def local_bc_body(c, r):
-    ex = expand(r.pk, DTBETA, r.e3)
     al = expand(r.pk, ALPHA, r.e3)
 
     def scale(at):
-        r.xhi[at, :], r.xlo[at, :] = split2(r.x[at, :].astype(F32) * ex[at, :])
         r.ghi[at, :], r.glo[at, :] = split2(r.gy[at, :] * al[at, :])
 
     each_rows(scale)
@@ -523,9 +575,9 @@
     cc = r.bc[:, STATE:]
     gys = (r.ghi[...], r.glo[...])
     xs = (r.xhi[...], r.xlo[...])
-    q = split2(dot3(gys, xs, NT) * r.mask[...].astype(F32))
-    r.gb[...] = r.gbs[...] + joined(q, [cc, cc], TN)
-    r.gc[...] = (r.gcs[...] + joined(q, [b, b], NN)).astype(BF16)
+    q = split2(dot3(gys, xs, NT) * r.marks[:, :L].astype(F32))
+    r.gb[...] = r.gs[:, :STATE] + joined(q, [cc, cc], TN)
+    r.gc[...] = (r.gs[:, STATE:] + joined(q, [b, b], NN)).astype(BF16)
 
 
 def final_begin(r):
@@ -552,23 +604,25 @@
     def body(at):
         scaled = fin[at, :] * v[at, :]
         r.gxo[at, :] = (r.gx[at, :] + scaled).astype(BF16)
-        r.rhi[at, :], r.rlo[at, :] = split2(scaled * r.x[at, :].astype(F32))
+        r.rhi[at, :], r.rlo[at, :] = split2(fold(scaled * r.x[at, :].astype(F32)))
 
     each_rows(body)
-    r.uu[...] = r.u[...] + dot2(r.e3[0:H, :], (r.rhi[...], r.rlo[...]), NT)
-
-
-def time_sums(r, u_ref, carry, write):
+    r.uu[...] = r.u[...] + dot2(r.eh[...], (r.rhi[...], r.rlo[...]), NT)
+
+
+def time_sums(r, r_ref, u_ref, carry, write):
     row = lax.broadcasted_iota(jnp.int32, (L, L), 0)
     col = lax.broadcasted_iota(jnp.int32, (L, L), 1)
     tri = (row >= col).astype(F32).astype(BF16)
     nega = -jnp.exp(r.par[:, 1:2])
+    chunks = [slice(c * L, (c + 1) * L) for c in range(C)]
+    parts = dot(jnp.concatenate([part for at in chunks for part in split3(r_ref[:, at] - u_ref[:, at])], 0), tri, NN)
     for c in reversed(range(C)):
-        at = slice(c * L, (c + 1) * L)
+        at = chunks[c]
         u = u_ref[:, at]
         dt = r.rf[0:H, at]
-        parts = dot(jnp.concatenate(split3(r.r[:, at] - u), 0), tri, NN)
-        later = parts[0:H] + parts[H : 2 * H] + parts[2 * H : 3 * H]
+        base = 3 * H * c
+        later = parts[base : base + H] + parts[base + H : base + 2 * H] + parts[base + 2 * H : base + 3 * H]
         grad_rate = later + carry
         carry = carry + later[:, 0:1]
         write(at, (u / dt + grad_rate * nega) * r.rf[H : 2 * H, at], grad_rate * dt * nega)
@@ -581,9 +635,8 @@
         sums[0] += jnp.sum(grad_alog, axis=1, keepdims=True)
         sums[1] += jnp.sum(grad_dt, axis=1, keepdims=True)
 
-    time_sums(r, r.u, jnp.zeros((H, 1), F32), write)
-    skips = jnp.broadcast_to(jnp.sum(r.skip_acc[...], axis=0, keepdims=True), (H, W))
-    skip_part = sum(dot(r.e3[0:H, :], part, NT) for part in split3(skips))[:, 0:1]
+    time_sums(r, r.rr, r.u, jnp.zeros((H, 1), F32), write)
+    skip_part = jnp.sum(r.sx[...], axis=1, keepdims=True)
     lane = lax.broadcasted_iota(jnp.int32, (H, 128), 1)
     r.loc[...] = jnp.where(
         lane == 0, skip_part, jnp.where(lane == 1, sums[0], jnp.where(lane == 2, sums[1], 0.0))
@@ -606,14 +659,19 @@
     def write(at, grad_dt, grad_alog):
         r.gdt[:, at] = grad_dt
 
-    time_sums(r, r.uu, carry, write)
-
-
-def pack_kernel(b_ref, c_ref, out_ref):
-    for g in range(GRP):
-        at = slice(STATE * g, STATE * (g + 1))
-        out_ref[g, :, :STATE] = b_ref[:, at]
-        out_ref[g, :, STATE:] = c_ref[:, at]
+    time_sums(r, r.r, r.uu, carry, write)
+
+
+def pack_kernel(b_ref, c_ref, out_ref, sems):
+    copies = []
+    for k, ref in enumerate((b_ref, c_ref)):
+        for g in range(GRP):
+            source = ref.at[:, STATE * g : STATE * (g + 1)]
+            copies.append(pltpu.make_async_copy(source, out_ref.at[g, :, STATE * k : STATE * (k + 1)], sems.at[k, g]))
+    for copy in copies:
+        copy.start()
+    for copy in copies:
+        copy.wait()
 
 
 def unpack_kernel(in_ref, b_ref, c_ref, sems):
@@ -638,7 +696,7 @@
     x_in, z_gate, b_proj, c_proj, dt_raw, dt_bias, a_log, skip, norm_weight, doc_starts, grad_out
 ):
     e3 = head_matrix()
-    par = jnp.pad(jnp.stack([dt_bias, a_log], 1), ((0, 0), (0, 126)))
+    par = jnp.pad(jnp.stack([dt_bias, a_log, skip], 1), ((0, 0), (0, 125)))
     vec = jnp.pad(
         jnp.stack([norm_weight, jnp.repeat(skip, HEAD_DIM)], 0), ((0, 6), (0, 0))
     )
@@ -647,32 +705,35 @@
     mine = pl.pallas_call(
         pack_kernel,
         out_shape=pltpu.HBM((GRP, 128, 2 * STATE), BF16),
+        out_specs=far,
+        scratch_shapes=[pltpu.SemaphoreType.DMA((2, GRP))],
         compiler_params=pltpu.CompilerParams(vmem_limit_bytes=VMEM_LIMIT),
         name="pack",
     )(*[pltpu.with_memory_space_constraint(a, pltpu.HBM) for a in (b_proj, c_proj)])
     bc = lax.all_to_all(mine, "head", split_axis=0, concat_axis=0, tiled=True).reshape(T, 2 * STATE)
 
     sds = pltpu.HBM
-    pk, rf, mask, me, mw, thx = pl.pallas_call(
+    pk, rf, marks, thx = pl.pallas_call(
         prep_kernel,
         out_shape=(
             sds((12 * H, T), BF16),
             sds((2 * H, T), F32),
-            sds((T, L), BF16),
-            sds((T, 128), BF16),
-            sds((T, 128), BF16),
+            sds((T, L + 256), BF16),
             sds((TABLE, W), F32),
         ),
         compiler_params=pltpu.CompilerParams(vmem_limit_bytes=VMEM_LIMIT),
         name="prep",
     )(*[pltpu.with_memory_space_constraint(a, pltpu.HBM) for a in (dt_raw, par, starts, e3)])
 
+    pk, vec = lax.optimization_barrier((pk, vec))
     state = ((STATE, W), F32)
     half = ((L, W), BF16)
+    folded = ((L, W // 2), BF16)
+    eh = {"eh": (folded_heads(), "all")}
     unit = 2 * T * L * W
     common = {"e3": (e3, "all"), "pk": (pk, "row"), "thx": (thx, "all")}
     x = {"x": (x_in, "tok")}
-    masks = {"mask": (mask, "tok"), "me": (me, "tok"), "mw": (mw, "tok")}
+    masks = {"marks": (marks, "tok")}
 
     xhi, xlo = staged(
         scale_body,
@@ -694,10 +755,11 @@
         end=states_end,
     )
 
-    def scan(kernel, name, outs, got, *others):
+    def scan(kernel, name, outs, got, *others, **more):
         return pl.pallas_call(
             kernel,
             out_shape=outs,
+            **more,
             in_specs=[pl.BlockSpec(memory_space=pltpu.VMEM)] * (1 + len(others)),
             compiler_params=pltpu.CompilerParams(vmem_limit_bytes=16 * 2**20),
             name=name,
@@ -711,19 +773,22 @@
 
     bcs = {"bc": (bc, "tok")}
     got = exchange(pay)
-    ys, sloc = staged(
+    y, sloc, wxhi, wxlo, g = staged(
         within_body,
-        common | bcs | masks | x,
+        common | {"vec": (vec, "all")} | bcs | masks | x,
         {
-            "ys": ((T, W), F32, "tok"),
+            "y": ((T, W), F32, "tok"),
             "sloc": ((C, STATE, W), F32, "state"),
+            "hi": ((T, W), BF16, "tok"),
+            "lo": ((T, W), BF16, "tok"),
+            "g": ((T, 2 * L), BF16, "tok"),
         },
-        {"acc": state, "hi": half, "lo": half},
+        {"acc": state},
         "within",
         7 * unit,
         begin=clear,
     )
-    ys, sloc, got = lax.optimization_barrier((ys, sloc, got))
+    y, sloc, got = lax.optimization_barrier((y, sloc, got))
     before, after, through = scan(
         scan_forward_kernel,
         "scan_forward",
@@ -734,12 +799,13 @@
     tied, _ = lax.optimization_barrier((x_in, got))
     (moments,) = staged(
         moments_body,
-        {"e3": (e3, "all"), "pk": (pk, "row")} | bcs | {"x": (tied, "tok")},
+        common | bcs | {"x": (tied, "tok"), "pay": (pay, "late")},
         {"moments": ((STATE, 2 * W), F32, "all")},
         {"hi": half, "lo": half, "hi2": half, "lo2": half},
         "moments",
         4 * unit,
         begin=moments_begin,
+        end=moments_end,
     )
     moments, sin = lax.optimization_barrier((moments, sin))
 
@@ -748,14 +814,13 @@
         common
         | {"vec": (vec, "all"), "sin": (sin, "near")}
         | bcs
-        | {"ys": (ys, "tok"), "z": (z_gate, "tok"), "go": (grad_out, "tok")}
-        | x
-        | {"moments": (moments, "late"), "pay": (pay, "late")},
+        | {"y": (y, "tok"), "z": (z_gate, "tok"), "go": (grad_out, "tok")}
+        | {"moments": (moments, "late")},
         {
             "gy": ((T, W), F32, "tok"),
             "gz": ((T, W), BF16, "tok"),
             "r": ((H, T), F32, "row"),
-            "back": ((2 * STATE, 2 * W), BF16, "all"),
+            "back": ((2 * STATE, 2 * W), BF16, "blocks"),
             "sums": ((8, W), F32, "all"),
             "sin_copy": ((STATE, W), F32, "copy"),
         },
@@ -776,9 +841,10 @@
     )
 
     got_back = exchange(back)
-    gx, u, gbs, gcs, loc = staged(
+    gx, u, r, gs, loc = staged(
         local_x_body,
         common
+        | eh
         | {
             "vec": (vec, "all"),
             "sin": (sin, "all"),
@@ -788,24 +854,26 @@
         }
         | bcs
         | masks
-        | {"gy": (gy, "tok"), "sloc": (sloc, "state")}
+        | {"g": (g, "tok"), "gy": (gy, "tok"), "sloc": (sloc, "state")}
         | x,
         {
             "gx": ((T, W), F32, "tok"),
             "u": ((H, T), F32, "row"),
-            "gbs": ((T, STATE), F32, "tok"),
-            "gcs": ((T, STATE), F32, "tok"),
+            "rr": ((H, T), F32, "row"),
+            "gs": ((T, 2 * STATE), F32, "tok"),
             "loc": ((H, 128), F32, "all"),
         },
         {
             "acc": state,
-            "skip_acc": ((8, W), F32),
+            "sx": ((H, T), F32),
+            "shi": folded,
+            "slo": folded,
             "ghi": half,
             "glo": half,
             "xhi": half,
             "xlo": half,
-            "rhi": half,
-            "rlo": half,
+            "rhi": folded,
+            "rlo": folded,
         },
         "local_x",
         7 * unit,
@@ -813,19 +881,25 @@
         begin=local_x_begin,
         end=local_x_end,
     )
-    gbs, got_back = lax.optimization_barrier((gbs, got_back))
+    gs, got_back = lax.optimization_barrier((gs, got_back))
     behind = scan(
-        scan_backward_kernel, "scan_backward", sds((STATE, W + 256), F32), got_back, through, after, loc, sums, e3, thx
+        scan_backward_kernel,
+        "scan_backward",
+        sds((STATE, W + 256), F32),
+        got_back,
+        *(through, after, loc, sums, e3, thx),
+        out_specs=far,
+        scratch_shapes=[pltpu.VMEM((STATE, W + 256), F32), pltpu.SemaphoreType.DMA((2, SEQ))],
     )
     din = exchange(behind)
     gb, gc = staged(
         local_bc_body,
         {"e3": (e3, "all"), "pk": (pk, "row")}
         | bcs
-        | {"mask": (mask, "tok"), "gy": (gy, "tok"), "gbs": (gbs, "tok"), "gcs": (gcs, "tok")}
-        | x,
+        | masks | {"gy": (gy, "tok"), "xhi": (wxhi, "tok"), "xlo": (wxlo, "tok")}
+        | {"gs": (gs, "tok")},
         {"gb": ((T, STATE), F32, "tok"), "gc": ((T, STATE), BF16, "tok")},
-        {"ghi": half, "glo": half, "xhi": half, "xlo": half},
+        {"ghi": half, "glo": half},
         "local_bc",
         5 * unit,
     )
@@ -858,6 +932,7 @@
     grad_x, grad_dt, grad_gain, grad_skip, grad_alog, grad_bias = staged(
         final_x_body,
         common
+        | eh
         | {
             "din": (din, "all"),
             "sin": (sin, "all"),
@@ -883,8 +958,8 @@
             "uu": ((H, T), F32),
             "dhi": ((STATE, W), BF16),
             "dlo": ((STATE, W), BF16),
-            "rhi": half,
-            "rlo": half,
+            "rhi": folded,
+            "rlo": folded,
         },
         "final_x",
         3 * unit,

time: 127 us -> 126 us (level)
  Pallas kernels: 80.3 us -> 76.4 us
  waiting for transfers between devices: 11.7 us -> 15.2 us
    pallas_call x9, Pallas kernels: 69.7 us -> 65.5 us  [staged(): pl.pallas_call(kernel, out_shape=tuple((pltpu.HBM(s, d) for s, d, _ in ou...]
    all_to_all x4, waiting for transfers between devices: 10.3 us -> 13.3 us  [exchange(): return lax.all_to_all(v, 'seq', split_axis=0, concat_axis=0, tiled=True)]
  transfers between devices with their start and end apart: 6 -> 6, of which waited for: 6 -> 5; matrix products, arithmetic and copies ran while one was open for 1% -> 1% of each run, Pallas kernels for 42% -> 41%
where the time goes in v6:
time: 126 us; the launch traced here: 124 us
  Pallas kernels  76.4 us (61%)
  starting transfers between devices  29.8 us (24%)
  waiting for transfers between devices  15.2 us (12%)
    pallas_call x9, Pallas kernels, staged(): pl.pallas_call(kernel, out_shape=tuple((pltpu.HBM(s, d) for s, d, _ in ou...  65.5 us
    all_to_all x4, starting transfers between devices, exchange(): return lax.all_to_all(v, 'seq', split_axis=0, concat_axis=0, tiled=True)  20.1 us
    all_to_all x4, waiting for transfers between devices, exchange(): return lax.all_to_all(v, 'seq', split_axis=0, concat_axis=0, tiled=True)  13.3 us
    all_to_all x1, starting transfers between devices, shard_body(): lax.all_to_all(mine, 'head', split_axis=0, concat_axis=0, tiled=True)  4.93 us
    all_to_all x1, starting transfers between devices, shard_body(): lax.all_to_all(gbc.reshape(GRP, 128, 2 * STATE), 'head', split_axis=0, co...  4.81 us
    pallas_call x2, Pallas kernels, scan(): pl.pallas_call(kernel, out_shape=outs, **more, in_specs=[pl.BlockSpec(mem...  4.26 us
    pallas_call x1, Pallas kernels, shard_body(): pl.pallas_call(prep_kernel, out_shape=(sds((12 * H, T), BF16), sds((2 * H...  3.67 us
  transfers between devices with their start and end apart: 6, of which 5 were waited for; matrix products, arithmetic and copies ran while one was open for 1% of the time, Pallas kernels for 41%

profile of v6, /device:TPU:8, one launch (start us, length us, event | category | flops | bytes accessed | tf_op | source)
XLA Modules:
  0.0 123.8 jit_solution(9843737610523420156)
XLA Ops:
  0.6 0.0 copy-start.1
  0.7 2.0 %pack.1 = bf16[8,128,256]{2,1,0:T(8,128)(2,1)} custom-call(bf16[128,1024]{1,0:T(8,128)(2,1)} %b_ref.1, bf16[128,1024]{1,0:T(8,128)(2,1)} %c_ref.1), custom_call_target="tpu_custom_call" | custom-call | tf_op jit(solution)/shard_map/pack/pallas_call | solution.py:705
  2.7 4.9 %all-to-all-start = ((bf16[8,128,256]{2,1,0:T(8,128)(2,1)}), bf16[8,128,256]{2,1,0:T(8,128)(2,1)S(1)}, u32[]{:S(2)}, u32[]{:S(2)}) async-start(bf16[8,128,256]{2,1,0:T(8,128)(2,1)} %pack.1), calls=%async_computation | async-start | bytes 1048576 | tf_op jit(solution)/shard_map/all_to_all | solution.py:713
  7.6 0.1 copy.25
  7.7 0.1 broadcast_in_dim.3
  7.8 0.1 stack_reshape.3
  7.9 0.6 pad.8.par_ref.refs_6_.refs_7_
  8.5 3.7 %prep.1 = (bf16[192,1024]{1,0:T(8,128)(2,1)}, f32[32,1024]{1,0:T(8,128)}, bf16[1024,512]{1,0:T(8,128)(2,1)}, f32[16,1024]{1,0:T(8,128)}) custom-call(f32[16,1024]{1,0:T(8,128)} %dt_ref.1, f32[16,128]{1,0:T(8,128)} %pad.8.par_ref.refs_6_.refs_7_, s32[1,1024]{1,0:T(1,128)} %bitcast.29, bf16[48,1024]{1,0:T(8,128)(2,1)} %constant.7.clone.e3_ref.refs_0_), custom_call_target="tpu_custom_call" | custom-call | tf_op jit(solution)/shard_map/prep/pallas_call | solution.py:716
  12.1 0.6 select_maximum_fusion.refs_3_.refs_4_
  12.8 3.8 %scale.1 = (bf16[1024,1024]{1,0:T(8,128)(2,1)}, bf16[1024,1024]{1,0:T(8,128)(2,1)}) custom-call(bf16[48,1024]{1,0:T(8,128)(2,1)} %constant.7.clone.e3_ref.refs_0_, bf16[192,1024]{1,0:T(8,128)(2,1)} %get-tuple-element.67.refs_1_, bf16[1024,1024]{1,0:T(8,128)(2,1)} %refs_14_.3), custom_call_target="tpu_custom_call" | custom-call | flops 536870912 | bytes 8388608 | tf_op jit(solution)/shard_map/scale/pallas_call | solution.py:186
  16.6 0.0 all-to-all-done
  16.6 3.7 %states.1 = (f32[128,1152]{1,0:T(8,128)}, bf16[1024,256]{1,0:T(8,128)(2,1)}) custom-call(f32[16,1024]{1,0:T(8,128)} %get-tuple-element.68.refs_0_.refs_2_.thx_ref, bf16[1024,256]{1,0:T(8,128)(2,1)S(1)} %bitcast.22, bf16[1024,1024]{1,0:T(8,128)(2,1)} %get-tuple-element.72.refs_2_.refs_3_, bf16[1024,1024]{1,0:T(8,128)(2,1)} %get-tuple-element.73.refs_3_.refs_4_), custom_call_target="tpu_custom_call" | custom-call | flops 1073741824 | bytes 8388608 | tf_op jit(solution)/shard_map/states/pallas_call | solution.py:186
  20.3 7.9 %all-to-all-start.1 = ((f32[16,8,1152]{2,1,0:T(8,128)}), f32[16,8,1152]{2,1,0:T(8,128)S(1)}, u32[]{:S(2)}, u32[]{:S(2)}) async-start(f32[16,8,1152]{2,1,0:T(8,128)} %bitcast.25), calls=%async_computation.1 | async-start | bytes 1179648 | tf_op jit(solution)/shard_map/all_to_all | solution.py:772
  28.2 8.2 %within.1 = (f32[1024,1024]{1,0:T(8,128)}, f32[4,128,1024]{2,1,0:T(8,128)}, bf16[1024,1024]{1,0:T(8,128)(2,1)}, bf16[1024,1024]{1,0:T(8,128)(2,1)}, bf16[1024,512]{1,0:T(8,128)(2,1)}) custom-call(bf16[48,1024]{1,0:T(8,128)(2,1)} %constant.7.clone.e3_ref.refs_0_, bf16[192,1024]{1,0:T(8,128)(2,1)} %get-tuple-element.67.refs_1_, ...), custom_call_target="tpu_custom_call" | custom-call | flops 3758096384 | bytes 8388608 | tf_op jit(solution)/shard_map/within/pallas_call | solution.py:186
  36.5 4.3 %all-to-all-done.1 = f32[16,8,1152]{2,1,0:T(8,128)S(1)} async-done(((f32[16,8,1152]{2,1,0:T(8,128)}), f32[16,8,1152]{2,1,0:T(8,128)S(1)}, u32[]{:S(2)}, u32[]{:S(2)}) %all-to-all-start.1) | async-done | bytes 589856 | tf_op jit(solution)/shard_map/all_to_all | solution.py:772
  40.8 1.1 scan_forward.1
  41.8 3.6 %all-to-all-start.2 = ((f32[16,8,1024]{2,1,0:T(8,128)}), f32[16,8,1024]{2,1,0:T(8,128)S(1)}, u32[]{:S(2)}, u32[]{:S(2)}) async-start(f32[16,8,1024]{2,1,0:T(8,128)} %bitcast.28), calls=%async_computation.2 | async-start | bytes 1048576 | tf_op jit(solution)/shard_map/all_to_all | solution.py:772
  45.4 5.8 %moments.1.refs_9_ = f32[128,2048]{1,0:T(8,128)} custom-call(bf16[48,1024]{1,0:T(8,128)(2,1)} %constant.7.clone.e3_ref.refs_0_, bf16[192,1024]{1,0:T(8,128)(2,1)} %get-tuple-element.67.refs_1_, f32[16,1024]{1,0:T(8,128)} %get-tuple-element.68.refs_0_.refs_2_.thx_ref, bf16[1024,256]{1,0:T(8,128)(2,1)} %get-tuple-element.74.refs_4_.refs_3_.refs_5_.refs_9_.refs_2_.refs_12_, ...), custom_call_target="tpu_custom_call" | custom-call | flops 2147483648 | bytes 8388608 | tf_op jit(solution)/shard_map/moments/pallas_call | solution.py:186
  51.3 4.8 %all-to-all-done.2 = f32[16,8,1024]{2,1,0:T(8,128)S(1)} async-done(((f32[16,8,1024]{2,1,0:T(8,128)}), f32[16,8,1024]{2,1,0:T(8,128)S(1)}, u32[]{:S(2)}, u32[]{:S(2)}) %all-to-all-start.2) | async-done | bytes 524320 | tf_op jit(solution)/shard_map/all_to_all | solution.py:772
  56.0 11.0 %norm.1 = (f32[1024,1024]{1,0:T(8,128)}, bf16[1024,1024]{1,0:T(8,128)(2,1)}, f32[16,1024]{1,0:T(8,128)}, bf16[256,2048]{1,0:T(8,128)(2,1)}, f32[8,1024]{1,0:T(8,128)}, /*index=5*/f32[128,1024]{1,0:T(8,128)}) custom-call(bf16[48,1024]{1,0:T(8,128)(2,1)} %constant.7.clone.e3_ref.refs_0_, bf16[192,1024]{1,0:T(8,128)(2,1)} %get-tuple-element.67.refs_1_, ...), custom_call_target="tpu_custom_call" | custom-call | flops 3221225472 | bytes 8388608 | tf_op jit(solution)/shard_map/norm/pallas_call | solution.py:186
  67.0 3.7 %all-to-all-start.3 = ((bf16[16,16,2048]{2,1,0:T(8,128)(2,1)}), bf16[16,16,2048]{2,1,0:T(8,128)(2,1)S(1)}, u32[]{:S(2)}, u32[]{:S(2)}) async-start(bf16[16,16,2048]{2,1,0:T(8,128)(2,1)} %bitcast.26), calls=%async_computation.3 | async-start | bytes 2097152 | tf_op jit(solution)/shard_map/all_to_all | solution.py:772
  70.7 12.8 %local_x.1 = (f32[1024,1024]{1,0:T(8,128)}, f32[16,1024]{1,0:T(8,128)}, f32[16,1024]{1,0:T(8,128)}, f32[1024,256]{1,0:T(8,128)}, f32[16,128]{1,0:T(8,128)}) custom-call(bf16[48,1024]{1,0:T(8,128)(2,1)} %constant.7.clone.e3_ref.refs_0_, bf16[192,1024]{1,0:T(8,128)(2,1)} %get-tuple-element.67.refs_1_, f32[16,1024]{1,0:T(8,128)} %get-tuple-element.68.refs_0_.refs_2_.thx_ref, ...), custom_call_target="tpu_custom_call" | custom-call | flops 3758096384 | bytes 8388608 | tf_op jit(solution)/shard_map/local_x/pallas_call | solution.py:186
  83.5 2.3 %all-to-all-done.3 = bf16[16,16,2048]{2,1,0:T(8,128)(2,1)S(1)} async-done(((bf16[16,16,2048]{2,1,0:T(8,128)(2,1)}), bf16[16,16,2048]{2,1,0:T(8,128)(2,1)S(1)}, u32[]{:S(2)}, u32[]{:S(2)}) %all-to-all-start.3) | async-done | bytes 1048608 | tf_op jit(solution)/shard_map/all_to_all | solution.py:772
  85.8 3.2 %scan_backward.1 = f32[128,1280]{1,0:T(8,128)} custom-call(bf16[256,2048]{1,0:T(8,128)(2,1)S(1)} %bitcast.19, f32[16,1024]{1,0:T(8,128)} %get-tuple-element.99.through_ref, f32[128,1024]{1,0:T(8,128)} %get-tuple-element.100.after_ref, f32[16,128]{1,0:T(8,128)} %get-tuple-element.101.loc_ref, f32[8,1024]{1,0:T(8,128)} %get-tuple-element.102.sums_ref, ...), custom_call_target="tpu_custom_call" | custom-call | tf_op jit(solution)/shard_map/scan_backward/pallas_call | solution.py:759
  89.0 4.9 %all-to-all-start.4 = ((f32[16,8,1280]{2,1,0:T(8,128)}), f32[16,8,1280]{2,1,0:T(8,128)S(1)}, u32[]{:S(2)}, u32[]{:S(2)}) async-start(f32[16,8,1280]{2,1,0:T(8,128)} %bitcast.24), calls=%async_computation.4 | async-start | bytes 1310720 | tf_op jit(solution)/shard_map/all_to_all | solution.py:772
  93.9 8.8 %local_bc.1 = (f32[1024,128]{1,0:T(8,128)}, bf16[1024,128]{1,0:T(8,128)(2,1)}) custom-call(bf16[48,1024]{1,0:T(8,128)(2,1)} %constant.7.clone.e3_ref.refs_0_, bf16[192,1024]{1,0:T(8,128)(2,1)} %get-tuple-element.67.refs_1_, bf16[1024,256]{1,0:T(8,128)(2,1)} %get-tuple-element.74.refs_4_.refs_3_.refs_5_.refs_9_.refs_2_.refs_12_, ...), custom_call_target="tpu_custom_call" | custom-call | flops 2684354560 | bytes 8388608 | tf_op jit(solution)/shard_map/local_bc/pallas_call | solution.py:186
  102.7 2.0 %all-to-all-done.4 = f32[16,8,1280]{2,1,0:T(8,128)S(1)} async-done(((f32[16,8,1280]{2,1,0:T(8,128)}), f32[16,8,1280]{2,1,0:T(8,128)S(1)}, u32[]{:S(2)}, u32[]{:S(2)}) %all-to-all-start.4) | async-done | bytes 655392 | tf_op jit(solution)/shard_map/all_to_all | solution.py:772
  104.7 4.3 %final_bc.1 = (bf16[1024,256]{1,0:T(8,128)(2,1)}, f32[128,1280]{1,0:T(8,128)}, f32[8,256]{1,0:T(8,128)}) custom-call(f32[128,1280]{1,0:T(8,128)S(1)} %bitcast.20, f32[1024,128]{1,0:T(8,128)} %get-tuple-element.104.refs_1_, bf16[1024,128]{1,0:T(8,128)(2,1)} %get-tuple-element.105.refs_2_, bf16[1024,1024]{1,0:T(8,128)(2,1)} %get-tuple-element.72.refs_2_.refs_3_, ...), custom_call_target="tpu_custom_call" | custom-call | flops 1073741824 | bytes 8388608 | tf_op jit(solution)/shard_map/final_bc/pallas_call | solution.py:186
  109.0 4.8 %all-to-all-start.5 = ((bf16[8,128,256]{2,1,0:T(8,128)(2,1)}), bf16[8,128,256]{2,1,0:T(8,128)(2,1)S(1)}, u32[]{:S(2)}, u32[]{:S(2)}) async-start(bf16[8,128,256]{2,1,0:T(8,128)(2,1)} %bitcast.27), calls=%async_computation.5 | async-start | bytes 1048576 | tf_op jit(solution)/shard_map/all_to_all | solution.py:929
  113.8 7.0 %final_x.1 = (bf16[1024,1024]{1,0:T(8,128)(2,1)}, f32[16,1024]{1,0:T(8,128)}, f32[1,1024]{1,0:T(1,128)}, f32[1,16]{1,0:T(1,128)}, f32[1,16]{1,0:T(1,128)}, /*index=5*/f32[1,16]{1,0:T(1,128)}) custom-call(bf16[48,1024]{1,0:T(8,128)(2,1)} %constant.7.clone.e3_ref.refs_0_, bf16[192,1024]{1,0:T(8,128)(2,1)} %get-tuple-element.67.refs_1_, ...), custom_call_target="tpu_custom_call" | custom-call | flops 1610612736 | bytes 8388608 | tf_op jit(solution)/shard_map/final_x/pallas_call | solution.py:186
  120.9 1.9 %all-to-all-done.5.in_ref = bf16[8,128,256]{2,1,0:T(8,128)(2,1)S(1)} async-done(((bf16[8,128,256]{2,1,0:T(8,128)(2,1)}), bf16[8,128,256]{2,1,0:T(8,128)(2,1)S(1)}, u32[]{:S(2)}, u32[]{:S(2)}) %all-to-all-start.5) | async-done | bytes 524320 | tf_op jit(solution)/shard_map/all_to_all | solution.py:929
  122.7 0.9 unpack.1
  (8 shorter events, 0.0 us)
Async XLA Ops:
  0.6 6.9 %copy-start.1 = (f32[16]{0:T(128)S(1)}, f32[16]{0:T(128)}, u32[]{:S(2)}) copy-start(f32[16]{0:T(128)} %param.20) | copy-start | bytes 196
  0.7 6.9 %copy-start.2 = (f32[16]{0:T(128)S(1)}, f32[16]{0:T(128)}, u32[]{:S(2)}) copy-start(f32[16]{0:T(128)} %param.19) | copy-start | bytes 196
  0.7 6.9 %copy-start.3 = (f32[16]{0:T(128)S(1)}, f32[16]{0:T(128)}, u32[]{:S(2)}) copy-start(f32[16]{0:T(128)} %param.18) | copy-start | bytes 196
  0.7 11.5 %copy-start = (f32[1024]{0:T(1024)S(1)}, f32[1024]{0:T(1024)}, u32[]{:S(2)}) copy-start(f32[1024]{0:T(1024)} %param.21) | copy-start | bytes 12292
  2.7 13.9 %all-to-all-start = ((bf16[8,128,256]{2,1,0:T(8,128)(2,1)}), bf16[8,128,256]{2,1,0:T(8,128)(2,1)S(1)}, u32[]{:S(2)}, u32[]{:S(2)}) async-start(bf16[8,128,256]{2,1,0:T(8,128)(2,1)} %pack.1), calls=%async_computation | async-start | bytes 1048576 | tf_op jit(solution)/shard_map/all_to_all | solution.py:713
  20.3 20.4 %all-to-all-start.1 = ((f32[16,8,1152]{2,1,0:T(8,128)}), f32[16,8,1152]{2,1,0:T(8,128)S(1)}, u32[]{:S(2)}, u32[]{:S(2)}) async-start(f32[16,8,1152]{2,1,0:T(8,128)} %bitcast.25), calls=%async_computation.1 | async-start | bytes 1179648 | tf_op jit(solution)/shard_map/all_to_all | solution.py:772
  41.8 14.2 %all-to-all-start.2 = ((f32[16,8,1024]{2,1,0:T(8,128)}), f32[16,8,1024]{2,1,0:T(8,128)S(1)}, u32[]{:S(2)}, u32[]{:S(2)}) async-start(f32[16,8,1024]{2,1,0:T(8,128)} %bitcast.28), calls=%async_computation.2 | async-start | bytes 1048576 | tf_op jit(solution)/shard_map/all_to_all | solution.py:772
  67.0 18.7 %all-to-all-start.3 = ((bf16[16,16,2048]{2,1,0:T(8,128)(2,1)}), bf16[16,16,2048]{2,1,0:T(8,128)(2,1)S(1)}, u32[]{:S(2)}, u32[]{:S(2)}) async-start(bf16[16,16,2048]{2,1,0:T(8,128)(2,1)} %bitcast.26), calls=%async_computation.3 | async-start | bytes 2097152 | tf_op jit(solution)/shard_map/all_to_all | solution.py:772
  89.0 15.7 %all-to-all-start.4 = ((f32[16,8,1280]{2,1,0:T(8,128)}), f32[16,8,1280]{2,1,0:T(8,128)S(1)}, u32[]{:S(2)}, u32[]{:S(2)}) async-start(f32[16,8,1280]{2,1,0:T(8,128)} %bitcast.24), calls=%async_computation.4 | async-start | bytes 1310720 | tf_op jit(solution)/shard_map/all_to_all | solution.py:772
  109.0 13.7 %all-to-all-start.5 = ((bf16[8,128,256]{2,1,0:T(8,128)(2,1)}), bf16[8,128,256]{2,1,0:T(8,128)(2,1)S(1)}, u32[]{:S(2)}, u32[]{:S(2)}) async-start(bf16[8,128,256]{2,1,0:T(8,128)(2,1)} %bitcast.27), calls=%async_computation.5 | async-start | bytes 1048576 | tf_op jit(solution)/shard_map/all_to_all | solution.py:929

commit v7 on v6

--- a/solution.py
+++ b/solution.py
@@ -23,6 +23,7 @@
 F32 = jnp.float32
 BF16 = jnp.bfloat16
 FLUSHES = 4
+BACK_LEVELS, ALOG_LEVELS, BIAS_LEVELS = 16, 2, 16
 STEP = 16
 VMEM_LIMIT = 60 * 2**20
 VMEM_NEAR = 48 * 2**20
@@ -393,15 +394,15 @@
         through = through_all[j : j + 1, :]
         state = after_ref[at, :]
         rests = block[:ROWS, W:] + 256.0
-        back_rest = jnp.floor(rests * (1.0 / 16))
-        rests = rests - 16.0 * back_rest
-        alog_rest = jnp.floor(rests * 0.25)
-        bias_rest = rests - 4.0 * alog_rest
+        upper = jnp.floor(rests * (1.0 / BIAS_LEVELS))
+        bias_rest = rests - BIAS_LEVELS * upper
+        back_rest = jnp.floor(upper * (1.0 / ALOG_LEVELS))
+        alog_rest = upper - ALOG_LEVELS * back_rest
         base = base_all[j : j + 1, :]
         bias_base = bias_base_all[j : j + 1, :]
-        by_alog += acc * (with_rest(block[ROWS:, :W], alog_rest, 4) + base * state)
-        by_bias += acc * (with_rest(block[ROWS:, W:], bias_rest, 4) + bias_base * state)
-        acc = through * acc + with_rest(block[:ROWS, :W], back_rest, 32)
+        by_alog += acc * (with_rest(block[ROWS:, :W], alog_rest, ALOG_LEVELS) + base * state)
+        by_bias += acc * (with_rest(block[ROWS:, W:], bias_rest, BIAS_LEVELS) + bias_base * state)
+        acc = through * acc + with_rest(block[:ROWS, :W], back_rest, BACK_LEVELS)
     row = lax.broadcasted_iota(jnp.int32, (H, W), 0)
     vector = jnp.where(
         row == 0,
@@ -506,11 +507,11 @@
     by_bias = r.thx[BY_BIAS : BY_BIAS + 1, :] - bias_base * total
     for d in range(SEQ):
         at = slice(ROWS * d, ROWS * (d + 1))
-        back, back_rest = rest_level(r.acc[at, :], 32)
+        back, back_rest = rest_level(r.acc[at, :], BACK_LEVELS)
         sin = r.sin[at, :]
-        alog, alog_rest = rest_level(r.moments[at, :W] + by_alog * sin, 4)
-        bias, bias_rest = rest_level(r.moments[at, W:] + by_bias * sin, 4)
-        rests = 16.0 * back_rest + 4.0 * alog_rest + bias_rest - 256.0
+        alog, alog_rest = rest_level(r.moments[at, :W] + by_alog * sin, ALOG_LEVELS)
+        bias, bias_rest = rest_level(r.moments[at, W:] + by_bias * sin, BIAS_LEVELS)
+        rests = (back_rest * ALOG_LEVELS + alog_rest) * BIAS_LEVELS + bias_rest - 256.0
         block = jnp.concatenate(
             [jnp.concatenate([back, rests], 1), jnp.concatenate([alog, bias], 1)], 0
         )

time: 126 us -> 126 us (level)
  no operation moved by 1% of the time
where the time goes in v7:
time: 126 us; the launch traced here: 124 us
  Pallas kernels  76.3 us (61%)
  starting transfers between devices  29.8 us (24%)
  waiting for transfers between devices  15.2 us (12%)
    pallas_call x9, Pallas kernels, staged(): pl.pallas_call(kernel, out_shape=tuple((pltpu.HBM(s, d) for s, d, _ in ou...  65.5 us
    all_to_all x4, starting transfers between devices, exchange(): return lax.all_to_all(v, 'seq', split_axis=0, concat_axis=0, tiled=True)  20.1 us
    all_to_all x4, waiting for transfers between devices, exchange(): return lax.all_to_all(v, 'seq', split_axis=0, concat_axis=0, tiled=True)  13.3 us
    all_to_all x1, starting transfers between devices, shard_body(): lax.all_to_all(mine, 'head', split_axis=0, concat_axis=0, tiled=True)  4.93 us
    all_to_all x1, starting transfers between devices, shard_body(): lax.all_to_all(gbc.reshape(GRP, 128, 2 * STATE), 'head', split_axis=0, co...  4.81 us
    pallas_call x2, Pallas kernels, scan(): pl.pallas_call(kernel, out_shape=outs, **more, in_specs=[pl.BlockSpec(mem...  4.24 us
    pallas_call x1, Pallas kernels, shard_body(): pl.pallas_call(prep_kernel, out_shape=(sds((12 * H, T), BF16), sds((2 * H...  3.67 us
  transfers between devices with their start and end apart: 6, of which 5 were waited for; matrix products, arithmetic and copies ran while one was open for 1% of the time, Pallas kernels for 41%

profile of v7, /device:TPU:8, one launch (start us, length us, event | category | flops | bytes accessed | tf_op | source)
XLA Modules:
  0.0 123.8 jit_solution(356282318710355693)
XLA Ops:
  0.6 0.0 copy-start.1
  0.7 2.0 %pack.1 = bf16[8,128,256]{2,1,0:T(8,128)(2,1)} custom-call(bf16[128,1024]{1,0:T(8,128)(2,1)} %b_ref.1, bf16[128,1024]{1,0:T(8,128)(2,1)} %c_ref.1), custom_call_target="tpu_custom_call" | custom-call | tf_op jit(solution)/shard_map/pack/pallas_call | solution.py:706
  2.7 4.9 %all-to-all-start = ((bf16[8,128,256]{2,1,0:T(8,128)(2,1)}), bf16[8,128,256]{2,1,0:T(8,128)(2,1)S(1)}, u32[]{:S(2)}, u32[]{:S(2)}) async-start(bf16[8,128,256]{2,1,0:T(8,128)(2,1)} %pack.1), calls=%async_computation | async-start | bytes 1048576 | tf_op jit(solution)/shard_map/all_to_all | solution.py:714
  7.6 0.1 copy.25
  7.7 0.1 broadcast_in_dim.3
  7.8 0.1 stack_reshape.3
  7.9 0.6 pad.8.par_ref.refs_6_.refs_7_
  8.5 3.7 %prep.1 = (bf16[192,1024]{1,0:T(8,128)(2,1)}, f32[32,1024]{1,0:T(8,128)}, bf16[1024,512]{1,0:T(8,128)(2,1)}, f32[16,1024]{1,0:T(8,128)}) custom-call(f32[16,1024]{1,0:T(8,128)} %dt_ref.1, f32[16,128]{1,0:T(8,128)} %pad.8.par_ref.refs_6_.refs_7_, s32[1,1024]{1,0:T(1,128)} %bitcast.29, bf16[48,1024]{1,0:T(8,128)(2,1)} %constant.7.clone.e3_ref.refs_0_), custom_call_target="tpu_custom_call" | custom-call | tf_op jit(solution)/shard_map/prep/pallas_call | solution.py:717
  12.1 0.6 select_maximum_fusion.refs_3_.refs_4_
  12.8 3.8 %scale.1 = (bf16[1024,1024]{1,0:T(8,128)(2,1)}, bf16[1024,1024]{1,0:T(8,128)(2,1)}) custom-call(bf16[48,1024]{1,0:T(8,128)(2,1)} %constant.7.clone.e3_ref.refs_0_, bf16[192,1024]{1,0:T(8,128)(2,1)} %get-tuple-element.67.refs_1_, bf16[1024,1024]{1,0:T(8,128)(2,1)} %refs_14_.3), custom_call_target="tpu_custom_call" | custom-call | flops 536870912 | bytes 8388608 | tf_op jit(solution)/shard_map/scale/pallas_call | solution.py:187
  16.6 0.0 all-to-all-done
  16.6 3.7 %states.1 = (f32[128,1152]{1,0:T(8,128)}, bf16[1024,256]{1,0:T(8,128)(2,1)}) custom-call(f32[16,1024]{1,0:T(8,128)} %get-tuple-element.68.refs_0_.refs_2_.thx_ref, bf16[1024,256]{1,0:T(8,128)(2,1)S(1)} %bitcast.22, bf16[1024,1024]{1,0:T(8,128)(2,1)} %get-tuple-element.72.refs_2_.refs_3_, bf16[1024,1024]{1,0:T(8,128)(2,1)} %get-tuple-element.73.refs_3_.refs_4_), custom_call_target="tpu_custom_call" | custom-call | flops 1073741824 | bytes 8388608 | tf_op jit(solution)/shard_map/states/pallas_call | solution.py:187
  20.3 7.9 %all-to-all-start.1 = ((f32[16,8,1152]{2,1,0:T(8,128)}), f32[16,8,1152]{2,1,0:T(8,128)S(1)}, u32[]{:S(2)}, u32[]{:S(2)}) async-start(f32[16,8,1152]{2,1,0:T(8,128)} %bitcast.25), calls=%async_computation.1 | async-start | bytes 1179648 | tf_op jit(solution)/shard_map/all_to_all | solution.py:773
  28.2 8.2 %within.1 = (f32[1024,1024]{1,0:T(8,128)}, f32[4,128,1024]{2,1,0:T(8,128)}, bf16[1024,1024]{1,0:T(8,128)(2,1)}, bf16[1024,1024]{1,0:T(8,128)(2,1)}, bf16[1024,512]{1,0:T(8,128)(2,1)}) custom-call(bf16[48,1024]{1,0:T(8,128)(2,1)} %constant.7.clone.e3_ref.refs_0_, bf16[192,1024]{1,0:T(8,128)(2,1)} %get-tuple-element.67.refs_1_, ...), custom_call_target="tpu_custom_call" | custom-call | flops 3758096384 | bytes 8388608 | tf_op jit(solution)/shard_map/within/pallas_call | solution.py:187
  36.5 4.3 %all-to-all-done.1 = f32[16,8,1152]{2,1,0:T(8,128)S(1)} async-done(((f32[16,8,1152]{2,1,0:T(8,128)}), f32[16,8,1152]{2,1,0:T(8,128)S(1)}, u32[]{:S(2)}, u32[]{:S(2)}) %all-to-all-start.1) | async-done | bytes 589856 | tf_op jit(solution)/shard_map/all_to_all | solution.py:773
  40.8 1.1 scan_forward.1
  41.8 3.6 %all-to-all-start.2 = ((f32[16,8,1024]{2,1,0:T(8,128)}), f32[16,8,1024]{2,1,0:T(8,128)S(1)}, u32[]{:S(2)}, u32[]{:S(2)}) async-start(f32[16,8,1024]{2,1,0:T(8,128)} %bitcast.28), calls=%async_computation.2 | async-start | bytes 1048576 | tf_op jit(solution)/shard_map/all_to_all | solution.py:773
  45.4 5.8 %moments.1.refs_9_ = f32[128,2048]{1,0:T(8,128)} custom-call(bf16[48,1024]{1,0:T(8,128)(2,1)} %constant.7.clone.e3_ref.refs_0_, bf16[192,1024]{1,0:T(8,128)(2,1)} %get-tuple-element.67.refs_1_, f32[16,1024]{1,0:T(8,128)} %get-tuple-element.68.refs_0_.refs_2_.thx_ref, bf16[1024,256]{1,0:T(8,128)(2,1)} %get-tuple-element.74.refs_4_.refs_3_.refs_5_.refs_9_.refs_2_.refs_12_, ...), custom_call_target="tpu_custom_call" | custom-call | flops 2147483648 | bytes 8388608 | tf_op jit(solution)/shard_map/moments/pallas_call | solution.py:187
  51.3 4.8 %all-to-all-done.2 = f32[16,8,1024]{2,1,0:T(8,128)S(1)} async-done(((f32[16,8,1024]{2,1,0:T(8,128)}), f32[16,8,1024]{2,1,0:T(8,128)S(1)}, u32[]{:S(2)}, u32[]{:S(2)}) %all-to-all-start.2) | async-done | bytes 524320 | tf_op jit(solution)/shard_map/all_to_all | solution.py:773
  56.0 11.0 %norm.1 = (f32[1024,1024]{1,0:T(8,128)}, bf16[1024,1024]{1,0:T(8,128)(2,1)}, f32[16,1024]{1,0:T(8,128)}, bf16[256,2048]{1,0:T(8,128)(2,1)}, f32[8,1024]{1,0:T(8,128)}, /*index=5*/f32[128,1024]{1,0:T(8,128)}) custom-call(bf16[48,1024]{1,0:T(8,128)(2,1)} %constant.7.clone.e3_ref.refs_0_, bf16[192,1024]{1,0:T(8,128)(2,1)} %get-tuple-element.67.refs_1_, ...), custom_call_target="tpu_custom_call" | custom-call | flops 3221225472 | bytes 8388608 | tf_op jit(solution)/shard_map/norm/pallas_call | solution.py:187
  67.0 3.7 %all-to-all-start.3 = ((bf16[16,16,2048]{2,1,0:T(8,128)(2,1)}), bf16[16,16,2048]{2,1,0:T(8,128)(2,1)S(1)}, u32[]{:S(2)}, u32[]{:S(2)}) async-start(bf16[16,16,2048]{2,1,0:T(8,128)(2,1)} %bitcast.26), calls=%async_computation.3 | async-start | bytes 2097152 | tf_op jit(solution)/shard_map/all_to_all | solution.py:773
  70.7 12.8 %local_x.1 = (f32[1024,1024]{1,0:T(8,128)}, f32[16,1024]{1,0:T(8,128)}, f32[16,1024]{1,0:T(8,128)}, f32[1024,256]{1,0:T(8,128)}, f32[16,128]{1,0:T(8,128)}) custom-call(bf16[48,1024]{1,0:T(8,128)(2,1)} %constant.7.clone.e3_ref.refs_0_, bf16[192,1024]{1,0:T(8,128)(2,1)} %get-tuple-element.67.refs_1_, f32[16,1024]{1,0:T(8,128)} %get-tuple-element.68.refs_0_.refs_2_.thx_ref, ...), custom_call_target="tpu_custom_call" | custom-call | flops 3758096384 | bytes 8388608 | tf_op jit(solution)/shard_map/local_x/pallas_call | solution.py:187
  83.5 2.3 %all-to-all-done.3 = bf16[16,16,2048]{2,1,0:T(8,128)(2,1)S(1)} async-done(((bf16[16,16,2048]{2,1,0:T(8,128)(2,1)}), bf16[16,16,2048]{2,1,0:T(8,128)(2,1)S(1)}, u32[]{:S(2)}, u32[]{:S(2)}) %all-to-all-start.3) | async-done | bytes 1048608 | tf_op jit(solution)/shard_map/all_to_all | solution.py:773
  85.8 3.2 %scan_backward.1 = f32[128,1280]{1,0:T(8,128)} custom-call(bf16[256,2048]{1,0:T(8,128)(2,1)S(1)} %bitcast.19, f32[16,1024]{1,0:T(8,128)} %get-tuple-element.99.through_ref, f32[128,1024]{1,0:T(8,128)} %get-tuple-element.100.after_ref, f32[16,128]{1,0:T(8,128)} %get-tuple-element.101.loc_ref, f32[8,1024]{1,0:T(8,128)} %get-tuple-element.102.sums_ref, ...), custom_call_target="tpu_custom_call" | custom-call | tf_op jit(solution)/shard_map/scan_backward/pallas_call | solution.py:760
  89.0 4.9 %all-to-all-start.4 = ((f32[16,8,1280]{2,1,0:T(8,128)}), f32[16,8,1280]{2,1,0:T(8,128)S(1)}, u32[]{:S(2)}, u32[]{:S(2)}) async-start(f32[16,8,1280]{2,1,0:T(8,128)} %bitcast.24), calls=%async_computation.4 | async-start | bytes 1310720 | tf_op jit(solution)/shard_map/all_to_all | solution.py:773
  93.9 8.8 %local_bc.1 = (f32[1024,128]{1,0:T(8,128)}, bf16[1024,128]{1,0:T(8,128)(2,1)}) custom-call(bf16[48,1024]{1,0:T(8,128)(2,1)} %constant.7.clone.e3_ref.refs_0_, bf16[192,1024]{1,0:T(8,128)(2,1)} %get-tuple-element.67.refs_1_, bf16[1024,256]{1,0:T(8,128)(2,1)} %get-tuple-element.74.refs_4_.refs_3_.refs_5_.refs_9_.refs_2_.refs_12_, ...), custom_call_target="tpu_custom_call" | custom-call | flops 2684354560 | bytes 8388608 | tf_op jit(solution)/shard_map/local_bc/pallas_call | solution.py:187
  102.7 2.0 %all-to-all-done.4 = f32[16,8,1280]{2,1,0:T(8,128)S(1)} async-done(((f32[16,8,1280]{2,1,0:T(8,128)}), f32[16,8,1280]{2,1,0:T(8,128)S(1)}, u32[]{:S(2)}, u32[]{:S(2)}) %all-to-all-start.4) | async-done | bytes 655392 | tf_op jit(solution)/shard_map/all_to_all | solution.py:773
  104.7 4.3 %final_bc.1 = (bf16[1024,256]{1,0:T(8,128)(2,1)}, f32[128,1280]{1,0:T(8,128)}, f32[8,256]{1,0:T(8,128)}) custom-call(f32[128,1280]{1,0:T(8,128)S(1)} %bitcast.20, f32[1024,128]{1,0:T(8,128)} %get-tuple-element.104.refs_1_, bf16[1024,128]{1,0:T(8,128)(2,1)} %get-tuple-element.105.refs_2_, bf16[1024,1024]{1,0:T(8,128)(2,1)} %get-tuple-element.72.refs_2_.refs_3_, ...), custom_call_target="tpu_custom_call" | custom-call | flops 1073741824 | bytes 8388608 | tf_op jit(solution)/shard_map/final_bc/pallas_call | solution.py:187
  109.0 4.8 %all-to-all-start.5 = ((bf16[8,128,256]{2,1,0:T(8,128)(2,1)}), bf16[8,128,256]{2,1,0:T(8,128)(2,1)S(1)}, u32[]{:S(2)}, u32[]{:S(2)}) async-start(bf16[8,128,256]{2,1,0:T(8,128)(2,1)} %bitcast.27), calls=%async_computation.5 | async-start | bytes 1048576 | tf_op jit(solution)/shard_map/all_to_all | solution.py:930
  113.8 7.0 %final_x.1 = (bf16[1024,1024]{1,0:T(8,128)(2,1)}, f32[16,1024]{1,0:T(8,128)}, f32[1,1024]{1,0:T(1,128)}, f32[1,16]{1,0:T(1,128)}, f32[1,16]{1,0:T(1,128)}, /*index=5*/f32[1,16]{1,0:T(1,128)}) custom-call(bf16[48,1024]{1,0:T(8,128)(2,1)} %constant.7.clone.e3_ref.refs_0_, bf16[192,1024]{1,0:T(8,128)(2,1)} %get-tuple-element.67.refs_1_, ...), custom_call_target="tpu_custom_call" | custom-call | flops 1610612736 | bytes 8388608 | tf_op jit(solution)/shard_map/final_x/pallas_call | solution.py:187
  120.8 1.9 %all-to-all-done.5.in_ref = bf16[8,128,256]{2,1,0:T(8,128)(2,1)S(1)} async-done(((bf16[8,128,256]{2,1,0:T(8,128)(2,1)}), bf16[8,128,256]{2,1,0:T(8,128)(2,1)S(1)}, u32[]{:S(2)}, u32[]{:S(2)}) %all-to-all-start.5) | async-done | bytes 524320 | tf_op jit(solution)/shard_map/all_to_all | solution.py:930
  122.7 0.9 unpack.1
  (8 shorter events, 0.0 us)
Async XLA Ops:
  0.6 6.9 %copy-start.1 = (f32[16]{0:T(128)S(1)}, f32[16]{0:T(128)}, u32[]{:S(2)}) copy-start(f32[16]{0:T(128)} %param.20) | copy-start | bytes 196
  0.7 6.9 %copy-start.2 = (f32[16]{0:T(128)S(1)}, f32[16]{0:T(128)}, u32[]{:S(2)}) copy-start(f32[16]{0:T(128)} %param.19) | copy-start | bytes 196
  0.7 6.9 %copy-start.3 = (f32[16]{0:T(128)S(1)}, f32[16]{0:T(128)}, u32[]{:S(2)}) copy-start(f32[16]{0:T(128)} %param.18) | copy-start | bytes 196
  0.7 11.5 %copy-start = (f32[1024]{0:T(1024)S(1)}, f32[1024]{0:T(1024)}, u32[]{:S(2)}) copy-start(f32[1024]{0:T(1024)} %param.21) | copy-start | bytes 12292
  2.7 13.9 %all-to-all-start = ((bf16[8,128,256]{2,1,0:T(8,128)(2,1)}), bf16[8,128,256]{2,1,0:T(8,128)(2,1)S(1)}, u32[]{:S(2)}, u32[]{:S(2)}) async-start(bf16[8,128,256]{2,1,0:T(8,128)(2,1)} %pack.1), calls=%async_computation | async-start | bytes 1048576 | tf_op jit(solution)/shard_map/all_to_all | solution.py:714
  20.3 20.4 %all-to-all-start.1 = ((f32[16,8,1152]{2,1,0:T(8,128)}), f32[16,8,1152]{2,1,0:T(8,128)S(1)}, u32[]{:S(2)}, u32[]{:S(2)}) async-start(f32[16,8,1152]{2,1,0:T(8,128)} %bitcast.25), calls=%async_computation.1 | async-start | bytes 1179648 | tf_op jit(solution)/shard_map/all_to_all | solution.py:773
  41.8 14.2 %all-to-all-start.2 = ((f32[16,8,1024]{2,1,0:T(8,128)}), f32[16,8,1024]{2,1,0:T(8,128)S(1)}, u32[]{:S(2)}, u32[]{:S(2)}) async-start(f32[16,8,1024]{2,1,0:T(8,128)} %bitcast.28), calls=%async_computation.2 | async-start | bytes 1048576 | tf_op jit(solution)/shard_map/all_to_all | solution.py:773
  67.0 18.7 %all-to-all-start.3 = ((bf16[16,16,2048]{2,1,0:T(8,128)(2,1)}), bf16[16,16,2048]{2,1,0:T(8,128)(2,1)S(1)}, u32[]{:S(2)}, u32[]{:S(2)}) async-start(bf16[16,16,2048]{2,1,0:T(8,128)(2,1)} %bitcast.26), calls=%async_computation.3 | async-start | bytes 2097152 | tf_op jit(solution)/shard_map/all_to_all | solution.py:773
  89.0 15.7 %all-to-all-start.4 = ((f32[16,8,1280]{2,1,0:T(8,128)}), f32[16,8,1280]{2,1,0:T(8,128)S(1)}, u32[]{:S(2)}, u32[]{:S(2)}) async-start(f32[16,8,1280]{2,1,0:T(8,128)} %bitcast.24), calls=%async_computation.4 | async-start | bytes 1310720 | tf_op jit(solution)/shard_map/all_to_all | solution.py:773
  109.0 13.7 %all-to-all-start.5 = ((bf16[8,128,256]{2,1,0:T(8,128)(2,1)}), bf16[8,128,256]{2,1,0:T(8,128)(2,1)S(1)}, u32[]{:S(2)}, u32[]{:S(2)}) async-start(bf16[8,128,256]{2,1,0:T(8,128)(2,1)} %bitcast.27), calls=%async_computation.5 | async-start | bytes 1048576 | tf_op jit(solution)/shard_map/all_to_all | solution.py:930
